TPU v7x, 256 devices: a whole 4x4x8 slice. The times are simulated.
256 devices in a mesh: fsdp: 64 (over z, y, core), tensor: 4 (over x).
Axes of the slice: x: 4, y: 4, z: 8, core: 2. Of those that a mesh axis runs over, the one named last changes fastest.
Arguments:
- gradient: bfloat16 [64, 1024, 1024], P(None, 'fsdp', 'tensor')
- left_stat: float32 [128, 1024, 1024], P('fsdp', 'tensor'), may hold values from -6 to 6
- right_stat: float32 [128, 1024, 1024], P('fsdp', 'tensor'), may hold values from -6 to 6
- left_root: bfloat16 [128, 1024, 1024], P('fsdp', 'tensor')
- right_root: bfloat16 [128, 1024, 1024], P('fsdp', 'tensor')
- block_owner: int32 [64], replicated, may hold values from 0 to 63, as said below
Outputs:
- new_left: float32 [128, 1024, 1024], P('fsdp', 'tensor')
- new_right: float32 [128, 1024, 1024], P('fsdp', 'tensor')
- update: bfloat16 [64, 1024, 1024], P(None, 'fsdp', 'tensor')
Inputs may be any that keep to these rules, and one draw needn't show every extreme that they name: `block_owner`: each owner holds at most 2 blocks, and some owner holds exactly 2.
All inputs are finite; a program needn't handle non-finite values.
Results may differ from a plain program's by a relative error of at most 0.0049.
Values may be sent and summed in bfloat16 or wider, within the bound.
No kernel may reach another device: no remote copies, remote signals or barrier semaphores. Data moves between devices by JAX's collectives and lax.ppermute only.
A program may use at most 128 MiB of HBM per device.

v0:
```python
import jax
import jax.numpy as jnp
from jax import lax
from jax.sharding import PartitionSpec as P

DECAY = 0.99
EPSILON = 1e-06


def on_device(gradient, left_stat, right_stat, left_root, right_root, block_owner):
    owners_count = lax.axis_size("fsdp")
    member = lax.axis_index("tensor")
    block_count, rows_blk, cols_dev = gradient.shape
    slot_count, slab_rows, block_width = left_stat.shape
    position = jnp.arange(block_count, dtype=jnp.int32)
    earlier = (block_owner[None, :] == block_owner[:, None]) & (
        position[None, :] < position[:, None]
    )
    target = block_owner * slot_count + jnp.sum(earlier.astype(jnp.int32), axis=1)
    wide_rows = lax.all_gather(gradient, "tensor", axis=2, tiled=True)
    outgoing = (
        jnp.zeros((owners_count * slot_count, rows_blk, block_width), gradient.dtype)
        .at[target]
        .set(wide_rows)
    )
    full_block = lax.all_to_all(outgoing, "fsdp", split_axis=0, concat_axis=1, tiled=True)
    own_rows = lax.dynamic_slice_in_dim(full_block, member * slab_rows, slab_rows, 1)
    own_cols = lax.dynamic_slice_in_dim(full_block, member * slab_rows, slab_rows, 2)
    left_term = jnp.einsum("sik,sjk->sij", own_rows, full_block, preferred_element_type=jnp.float32)
    right_term = jnp.einsum(
        "ski,skj->sij", own_cols, full_block, preferred_element_type=jnp.float32
    )
    new_left = DECAY * left_stat + (1.0 - DECAY) * left_term
    new_right = DECAY * right_stat + (1.0 - DECAY) * right_term
    left_part = jnp.einsum(
        "sik,skj->sij", left_root, full_block, preferred_element_type=jnp.float32
    ).astype(jnp.bfloat16)
    grad_wide = full_block.astype(jnp.float32)
    grad_square = jnp.sum(grad_wide * grad_wide, axis=(1, 2))
    raw_update = jnp.einsum(
        "sik,skj->sij",
        left_part,
        lax.all_gather(right_root, "tensor", axis=1, tiled=True),
        preferred_element_type=jnp.float32,
    )
    update_square = lax.psum(jnp.sum(raw_update * raw_update, axis=(1, 2)), "tensor")
    graft = jnp.sqrt((grad_square + EPSILON) / (update_square + EPSILON))
    grafted = (raw_update * graft[:, None, None]).astype(jnp.bfloat16)
    grafted = lax.all_to_all(grafted, "tensor", split_axis=2, concat_axis=1, tiled=True)
    returned = lax.all_to_all(grafted, "fsdp", split_axis=1, concat_axis=0, tiled=True)
    update = returned[target]
    return (new_left, new_right, update)


def solution(mesh):
    return jax.shard_map(
        on_device,
        mesh=mesh,
        in_specs=(
            P(None, "fsdp", "tensor"),
            P("fsdp", "tensor", None),
            P("fsdp", "tensor", None),
            P("fsdp", "tensor", None),
            P("fsdp", "tensor", None),
            P(),
        ),
        out_specs=(P("fsdp", "tensor", None), P("fsdp", "tensor", None), P(None, "fsdp", "tensor")),
        check_vma=False,
    )
```

profile of v0, /device:TPU:1, one launch (start us, length us, event | category | flops | bytes accessed | tf_op | source)
XLA Modules:
  0.0 257.7 jit_solution(8574028820406401284)
XLA Ops:
  7.2 0.0 copy-start
  7.2 0.0 all-gather.3.cloned.1.call-start
  7.2 0.7 all-gather.3.cloned.1.call-update
  7.9 0.9 convert_reduce_fusion
  8.8 0.7 compare_select_fusion
  9.5 40.3 %all-gather.3.cloned.1.call-done = bf16[64,16,1024]{2,1,0:T(8,128)(2,1)} async-done(((bf16[64,16,256]{2,1,0:T(8,128)(2,1)}), bf16[64,16,1024]{2,1,0:T(8,128)(2,1)}) %all-gather.3.cloned.1.call-update) | async-done | bytes 2097168 | tf_op jit(solution)/shard_map/all_gather | solution.py:20
  49.8 0.0 copy-start.2
  49.8 2.5 broadcast_in_dim.4
  52.3 0.0 copy-done.2
  52.3 8.6 %scatter_fusion = bf16[128,16,1024]{2,1,0:T(8,128)(2,1)} fusion(bf16[128,16,1024]{2,1,0:T(8,128)(2,1)} %broadcast_in_dim.4, s32[64]{0:T(128)S(1)} %compare_select_fusion, bf16[64,16,1024]{2,1,0:T(8,128)(2,1)S(1)} %copy-done.2), kind=kCustom, calls=%fused_computation.1 | custom fusion | bytes 6291712 | tf_op jit(solution)/shard_map/scatter | solution.py:24
  60.9 11.7 %all-to-all-start = ((bf16[128,16,1024]{2,1,0:T(8,128)(2,1)}), bf16[128,16,1024]{2,1,0:T(8,128)(2,1)}, u32[]{:S(2)}, u32[]{:S(2)}) async-start(bf16[128,16,1024]{2,1,0:T(8,128)(2,1)} %scatter_fusion), calls=%async_computation | async-start | bytes 8388608 | tf_op jit(solution)/shard_map/all_to_all | solution.py:26
  72.7 0.0 all-gather.5.cloned.1.call-start
  72.7 0.7 all-gather.5.cloned.1.call-update
  73.4 93.7 %all-to-all-done = bf16[128,16,1024]{2,1,0:T(8,128)(2,1)} async-done(((bf16[128,16,1024]{2,1,0:T(8,128)(2,1)}), bf16[128,16,1024]{2,1,0:T(8,128)(2,1)}, u32[]{:S(2)}, u32[]{:S(2)}) %all-to-all-start) | async-done | bytes 4194336 | tf_op jit(solution)/shard_map/all_to_all | solution.py:26
  167.1 5.0 %copy.30 = bf16[2,64,16,1024]{3,2,1,0:T(8,128)(2,1)} copy(bf16[2,64,16,1024]{3,2,0,1:T(8,128)(2,1)} %bitcast.1) | data formatting | bytes 8388608 | tf_op jit(solution)/shard_map/all_to_all | solution.py:26
  172.1 3.4 %multiply_reduce_fusion = f32[2]{0:T(128)S(1)} fusion(bf16[2,64,16,1024]{3,2,0,1:T(8,128)(2,1)} %bitcast.1), kind=kLoop, calls=%fused_computation.2 | loop fusion | flops 6291454 | bytes 4194312 | tf_op jit(solution)/shard_map/reduce_sum | solution.py:39
  175.5 0.0 all-gather.5.cloned.1.call-done
  175.5 0.0 copy-done
  175.5 7.3 %multiply_reduce_fusion.1 = (f32[2]{0:T(128)S(1)}, f32[2,256,1024]{2,1,0:T(8,128)}) fusion(bf16[2,1024,1024]{2,1,0:T(8,128)(2,1)} %all-gather.5.cloned.1.call-done, bf16[2,1024,1024]{2,1,0:T(8,128)(2,1)} %bitcast.17, bf16[2,256,1024]{2,1,0:T(8,128)(2,1)S(1)} %copy-done), kind=kOutput, calls=%fused_computation.4 | convolution fusion | flops 2149056512 | bytes 11534344 | tf_op jit(solution)/shard_map/sik,skj->sij/dot_general | solution.py:40
  182.8 7.7 %psum.7 = f32[2]{0:T(128)S(1)} all-reduce(f32[2]{0:T(128)S(1)} %get-tuple-element.3), channel_id=1, replica_groups=mesh['fsdp'=64,'tensor'=4] {'tensor'}, use_global_device_ids=true, to_apply=%region_4.0 | all-reduce | flops 2 | bytes 16 | tf_op jit(solution)/shard_map/psum | solution.py:46
  190.5 1.9 multiply_convert_fusion
  192.4 0.9 copy.34
  193.4 13.1 %all_to_all.54 = bf16[2,256,1024]{1,0,2:T(2,128)(2,1)S(1)} all-to-all(bf16[2,256,1024]{1,0,2:T(2,128)(2,1)S(1)} %copy.34), channel_id=1, replica_groups=mesh['fsdp'=64,'tensor'=4] {'tensor'}, dimensions={2} | all-to-all | bytes 2097152 | tf_op jit(solution)/shard_map/all_to_all | solution.py:49
  206.5 0.1 copy.35
  206.7 0.5 copy.36
  207.2 2.1 copy.37
  209.2 11.9 %all-to-all-start.2 = ((bf16[2,1024,256]{2,0,1:T(2,128)(2,1)}), bf16[2,1024,256]{2,0,1:T(2,128)(2,1)S(1)}, u32[]{:S(2)}, u32[]{:S(2)}) async-start(bf16[2,1024,256]{2,0,1:T(2,128)(2,1)} %copy.37), calls=%async_computation.2 | async-start | bytes 2097152 | tf_op jit(solution)/shard_map/all_to_all | solution.py:50
  221.2 0.0 copy-start.1
  221.2 0.0 copy-start.3
  221.2 6.1 %multiply_add_fusion = f32[2,256,1024]{2,1,0:T(8,128)} fusion(f32[2,256,1024]{2,1,0:T(8,128)} %param.8, bf16[2,1024,1024]{2,1,0:T(8,128)(2,1)} %bitcast.18, s32[]{:T(128)S(6)} %select_n.9), kind=kOutput, calls=%fused_computation.5 | convolution fusion | flops 1075314688 | bytes 9437188 | tf_op jit(solution)/shard_map/ski,skj->sij/dot_general | solution.py:30
  227.3 0.0 copy-done.1
  227.3 0.0 copy-done.3
  227.3 2.8 %multiply_add_fusion.1 = f32[2,256,1024]{2,1,0:T(8,128)} fusion(f32[2,256,1024]{2,1,0:T(8,128)S(1)} %copy-done.3, bf16[2,1024,1024]{2,1,0:T(8,128)(2,1)S(1)} %bitcast.19, s32[]{:T(128)S(6)} %select_n.9), kind=kOutput, calls=%fused_computation.6 | convolution fusion | flops 1075314688 | bytes 9437188 | tf_op jit(solution)/shard_map/sik,sjk->sij/dot_general | solution.py:29
  230.1 19.1 %all-to-all-done.2 = bf16[2,1024,256]{2,0,1:T(2,128)(2,1)S(1)} async-done(((bf16[2,1024,256]{2,0,1:T(2,128)(2,1)}), bf16[2,1024,256]{2,0,1:T(2,128)(2,1)S(1)}, u32[]{:S(2)}, u32[]{:S(2)}) %all-to-all-start.2) | async-done | bytes 1048608 | tf_op jit(solution)/shard_map/all_to_all | solution.py:50
  249.1 0.1 copy.38
  249.3 0.1 copy.39
  249.4 1.4 gather_fusion
  (2 shorter events, 0.0 us)
Async XLA Ops:
  7.2 168.3 %copy-start = (bf16[2,256,1024]{2,1,0:T(8,128)(2,1)S(1)}, bf16[2,256,1024]{2,1,0:T(8,128)(2,1)}, u32[]{:S(2)}) copy-start(bf16[2,256,1024]{2,1,0:T(8,128)(2,1)} %param.9) | copy-start | bytes 3145732
  7.2 42.6 %all-gather.3.cloned.1.call-start = ((), (), s32[]{:S(2)}) async-start(), calls=%async_computation.3 | async-start | bytes 2621440 | tf_op jit(solution)/shard_map/all_gather | solution.py:20
  49.8 2.5 copy-start.2
  60.9 106.2 %all-to-all-start = ((bf16[128,16,1024]{2,1,0:T(8,128)(2,1)}), bf16[128,16,1024]{2,1,0:T(8,128)(2,1)}, u32[]{:S(2)}, u32[]{:S(2)}) async-start(bf16[128,16,1024]{2,1,0:T(8,128)(2,1)} %scatter_fusion), calls=%async_computation | async-start | bytes 8388608 | tf_op jit(solution)/shard_map/all_to_all | solution.py:26
  72.7 102.8 %all-gather.5.cloned.1.call-start = ((), (), s32[]{:S(2)}) async-start(), calls=%async_computation.4 | async-start | bytes 5242880 | tf_op jit(solution)/shard_map/all_gather | solution.py:43
  209.2 39.9 %all-to-all-start.2 = ((bf16[2,1024,256]{2,0,1:T(2,128)(2,1)}), bf16[2,1024,256]{2,0,1:T(2,128)(2,1)S(1)}, u32[]{:S(2)}, u32[]{:S(2)}) async-start(bf16[2,1024,256]{2,0,1:T(2,128)(2,1)} %copy.37), calls=%async_computation.2 | async-start | bytes 2097152 | tf_op jit(solution)/shard_map/all_to_all | solution.py:50
  221.2 6.1 %copy-start.1 = (bf16[2,64,16,1024]{3,2,1,0:T(8,128)(2,1)S(1)}, bf16[2,64,16,1024]{3,2,1,0:T(8,128)(2,1)}, u32[]{:S(2)}) copy-start(bf16[2,64,16,1024]{3,2,1,0:T(8,128)(2,1)} %copy.30) | copy-start | bytes 12582916
  221.2 6.1 %copy-start.3 = (f32[2,256,1024]{2,1,0:T(8,128)S(1)}, f32[2,256,1024]{2,1,0:T(8,128)}, u32[]{:S(2)}) copy-start(f32[2,256,1024]{2,1,0:T(8,128)} %param.7) | copy-start | bytes 6291460
Sparse Core Ops, SparseCore 0:
  9.8 39.9 all-gather.2
  75.3 51.3 all-gather.4
where the time goes:
time: 258 us
  waiting for transfers between devices  154 us (60%)
  starting transfers between devices  23.7 us (9%)
  local copies, waits for them, and re-layouts  21.5 us (8%)
  blocking collectives  20.9 us (8%)
  matrix products  16.2 us (6%)
  between operations  14.1 us (5%)
  other arithmetic  6.87 us (3%)
    all_to_all x1, waiting for transfers between devices, on_device(): lax.all_to_all(outgoing, 'fsdp', split_axis=0, concat_axis=1, tiled=True)  93.7 us
    all_gather x1, waiting for transfers between devices, on_device(): wide_rows = lax.all_gather(gradient, 'tensor', axis=2, tiled=True)  40.3 us
    all_to_all x1, waiting for transfers between devices, on_device(): lax.all_to_all(grafted, 'fsdp', split_axis=1, concat_axis=0, tiled=True)  19.1 us
    all_to_all x1, blocking collectives, on_device(): lax.all_to_all(grafted, 'tensor', split_axis=2, concat_axis=1, tiled=True)  13.1 us
    all_to_all x1, starting transfers between devices, on_device(): lax.all_to_all(grafted, 'fsdp', split_axis=1, concat_axis=0, tiled=True)  11.9 us
    all_to_all x1, starting transfers between devices, on_device(): lax.all_to_all(outgoing, 'fsdp', split_axis=0, concat_axis=1, tiled=True)  11.7 us
    scatter x1, local copies, waits for them, and re-layouts, on_device(): outgoing = jnp.zeros((owners_count * slot_count, rows_blk, block_width),...  8.63 us
    psum x1, blocking collectives, on_device(): lax.psum(jnp.sum(raw_update * raw_update, axis=(1, 2)), 'tensor')  7.74 us
  transfers between devices with their start and end apart: 4, of which 3 were waited for; matrix products, arithmetic and copies ran while one was open for 7% of the time, Pallas kernels for 0%

commit v1 on v0

v1 whole, which is shorter than its diff:
```python
import jax
import jax.numpy as jnp
from jax import lax
from jax.experimental import pallas as pl
from jax.experimental.pallas import tpu as pltpu
from jax.sharding import PartitionSpec as P

DECAY = 0.99
EPSILON = 1e-06
BF16 = jnp.bfloat16
F32 = jnp.float32
VMEM_SPEC = pl.BlockSpec(memory_space=pltpu.VMEM)
SMEM_SPEC = pl.BlockSpec(memory_space=pltpu.SMEM)
PARAMS = pltpu.CompilerParams(vmem_limit_bytes=48 * 1024 * 1024)


def dot(a, b, ca=1, cb=0):
    return lax.dot_general(a, b, (((ca,), (cb,)), ((), ())), preferred_element_type=F32)


def cost(flops, nbytes):
    return pl.CostEstimate(flops=flops, bytes_accessed=nbytes, transcendentals=0)


def clear_counts(count_ref, owners):
    def clear(i, _):
        count_ref[i] = 0
        return 0

    lax.fori_loop(0, owners, clear, 0)


def route_kernel(owner_ref, grad_ref, first_ref, second_ref, count_ref):
    first_ref[...] = jnp.zeros_like(first_ref)
    second_ref[...] = jnp.zeros_like(second_ref)
    clear_counts(count_ref, first_ref.shape[0])

    def body(b, _):
        o = owner_ref[b]
        c = count_ref[o]
        count_ref[o] = c + 1

        @pl.when(c == 0)
        def _():
            first_ref[o] = grad_ref[b]

        @pl.when(c == 1)
        def _():
            second_ref[o] = grad_ref[b]

        return 0

    lax.fori_loop(0, grad_ref.shape[0], body, 0)


def route(block_owner, gradient, owners):
    _, rows, cols = gradient.shape
    shape = jax.ShapeDtypeStruct((owners, rows, cols), gradient.dtype)
    return pl.pallas_call(
        route_kernel,
        out_shape=(shape, shape),
        in_specs=[SMEM_SPEC, VMEM_SPEC],
        out_specs=(VMEM_SPEC, VMEM_SPEC),
        scratch_shapes=[pltpu.SMEM((owners,), jnp.int32)],
        compiler_params=PARAMS,
        cost_estimate=cost(0, 3 * gradient.size),
        name="route",
    )(block_owner, gradient)


def collect_kernel(owner_ref, first_ref, second_ref, out_ref, count_ref):
    clear_counts(count_ref, first_ref.shape[0])

    def body(b, _):
        o = owner_ref[b]
        c = count_ref[o]
        count_ref[o] = c + 1

        @pl.when(c == 0)
        def _():
            out_ref[b] = first_ref[o]

        @pl.when(c == 1)
        def _():
            out_ref[b] = second_ref[o]

        return 0

    lax.fori_loop(0, out_ref.shape[0], body, 0)


def collect(block_owner, first, second):
    blocks = block_owner.shape[0]
    return pl.pallas_call(
        collect_kernel,
        out_shape=jax.ShapeDtypeStruct((blocks,) + first.shape[1:], first.dtype),
        in_specs=[SMEM_SPEC, VMEM_SPEC, VMEM_SPEC],
        out_specs=VMEM_SPEC,
        scratch_shapes=[pltpu.SMEM((first.shape[0],), jnp.int32)],
        compiler_params=PARAMS,
        cost_estimate=cost(0, 3 * first.size),
        name="collect",
    )(block_owner, first, second)


def three_parts(value):
    high = value.astype(BF16)
    rest = value - high.astype(F32)
    middle = rest.astype(BF16)
    low = (rest - middle.astype(F32)).astype(BF16)
    return high, middle, low


def update_kernel(
    t_ref, l_ref, g0, g1, g3, g2a, g2b, r0, r1, r3, r2a, r2b, o0, o1, o2, o3, raw_ref
):
    width = g0.shape[1]
    left = l_ref[...]
    half = g2a.shape[0]

    def part(g):
        return dot(left, g[...]).astype(BF16)

    raw = dot(part(g0), r0[...])
    raw += dot(part(g1), r1[...])
    raw += dot(part(g3), r3[...])
    far = (dot(left[:, :half], g2a[...]) + dot(left[:, half:], g2b[...])).astype(BF16)
    raw += dot(far[:, : width // 2], r2a[...]) + dot(far[:, width // 2 :], r2b[...])
    raw_ref[...] = raw
    grad_own = g0[...].astype(F32)
    shape = (16, width)
    update_square = jnp.broadcast_to(jnp.sum(raw * raw, keepdims=True), shape)
    grad_square = jnp.broadcast_to(jnp.sum(grad_own * grad_own, keepdims=True), shape)
    row = lax.broadcasted_iota(jnp.int32, shape, 0)
    tile = jnp.zeros(shape, F32)
    for place, value in enumerate(three_parts(update_square) + three_parts(grad_square)):
        tile = jnp.where(row == place, value.astype(F32), tile)
    tile = tile.astype(BF16)
    rows = left.shape[0]
    for k, out in enumerate((o0, o1, o2, o3)):
        s = lax.rem(t_ref[0] + k, 4)
        out[0:rows, :] = raw_ref[:, pl.ds(pl.multiple_of(s * width, width), width)].astype(BF16)
        out[rows : rows + 16, :] = tile


def update_rows(slot, t, left_root, grads, roots):
    g0, g1, g3, g2a, g2b = grads
    r0, r1, r3, r2a, r2b = roots
    _, rows, full = left_root.shape
    width = g0.shape[1]
    slot_spec = pl.BlockSpec((None, rows, full), lambda i: (slot, 0, 0))
    out = jax.ShapeDtypeStruct((rows + 16, width), BF16)
    return pl.pallas_call(
        update_kernel,
        grid=(1,),
        out_shape=(out,) * 4,
        in_specs=[SMEM_SPEC, slot_spec] + [VMEM_SPEC] * 5 + [slot_spec] * 3 + [VMEM_SPEC] * 2,
        out_specs=(VMEM_SPEC,) * 4,
        scratch_shapes=[pltpu.VMEM((rows, full), F32)],
        compiler_params=PARAMS,
        cost_estimate=cost(4 * rows * full * full, 10 * rows * full * 2),
        name="update_rows",
    )(t, left_root, g0, g1, g3, g2a, g2b, r0, r1, r3, r2a, r2b)


def scale_kernel(t_ref, q0, q1, q2, q3, out_ref):
    rows = q0.shape[0] - 16

    def total(q, first):
        part = q[rows : rows + 16, 0:1].astype(F32)
        return part[first : first + 1] + part[first + 1 : first + 2] + part[first + 2 : first + 3]

    update_square = total(q0, 0) + total(q1, 0) + total(q2, 0) + total(q3, 0)
    grad_square = total(q0, 3) + total(q1, 3) + total(q2, 3) + total(q3, 3)
    graft = jnp.sqrt((grad_square + EPSILON) / (update_square + EPSILON))
    for k, q in enumerate((q0, q1, q2, q3)):
        s = lax.rem(t_ref[0] + 4 - k, 4)
        scaled = (q[0:rows, :].astype(F32) * graft).astype(BF16)
        out_ref[pl.ds(pl.multiple_of(s * rows, rows), rows), :] = scaled


def scale(t, pieces):
    rows, width = pieces[0].shape
    return pl.pallas_call(
        scale_kernel,
        out_shape=jax.ShapeDtypeStruct((4 * (rows - 16), width), BF16),
        in_specs=[SMEM_SPEC] + [VMEM_SPEC] * 4,
        out_specs=VMEM_SPEC,
        compiler_params=PARAMS,
        cost_estimate=cost(0, 16 * rows * width),
        name="scale",
    )(t, *pieces)


def stats_kernel(t_ref, *refs):
    slot_grads = (refs[0:5], refs[5:10])
    left_ref, right_ref, new_left_ref, new_right_ref = refs[10:]
    t = t_ref[0]
    rows = left_ref.shape[0]

    def work(g0, g1, g3, g2a, g2b):
        mine = pl.ds(pl.multiple_of(t * rows, rows), rows)
        half = g2a.shape[0]
        term = dot(g0[mine, :], g0[...], 1, 1)
        term += dot(g1[mine, :], g1[...], 1, 1)
        term += dot(g3[mine, :], g3[...], 1, 1)
        new_left_ref[...] = DECAY * left_ref[...] + (1.0 - DECAY) * term

        def far(g, other):
            inside = pl.ds(pl.multiple_of(lax.rem(t, 2) * rows, rows), rows)
            top = g[inside, :]
            new_left_ref[:, 0:half] += (1.0 - DECAY) * dot(top, g2a[...], 1, 1)
            new_left_ref[:, half:] += (1.0 - DECAY) * dot(top, g2b[...], 1, 1)

        pl.when(t < 2)(lambda: far(g2a, g2b))
        pl.when(t >= 2)(lambda: far(g2b, g2a))
        own = g0[...].T

        def place(k, term):
            s = lax.rem(t + 4 - k, 4)
            cols = pl.ds(pl.multiple_of(s * rows, rows), rows)
            new_right_ref[:, cols] = DECAY * right_ref[:, cols] + (1.0 - DECAY) * term

        place(0, dot(own, g0[...]))
        place(1, dot(own, g1[...]))
        place(3, dot(own, g3[...]))
        place(2, dot(own[:, :half], g2a[...]) + dot(own[:, half:], g2b[...]))

    for slot in range(2):
        pl.when(pl.program_id(0) == slot)(lambda: work(*slot_grads[slot]))


def statistics(t, grads_first, grads_second, left_stat, right_stat):
    slots, rows, full = left_stat.shape
    slot_spec = pl.BlockSpec((None, rows, full), lambda i: (i, 0, 0))
    shape = jax.ShapeDtypeStruct(left_stat.shape, F32)
    return pl.pallas_call(
        stats_kernel,
        grid=(slots,),
        out_shape=(shape, shape),
        in_specs=[SMEM_SPEC] + [VMEM_SPEC] * 10 + [slot_spec] * 2,
        out_specs=(slot_spec, slot_spec),
        compiler_params=PARAMS,
        cost_estimate=cost(8 * rows * full * full, 24 * rows * full),
        name="statistics",
    )(t, *grads_first, *grads_second, left_stat, right_stat)


def around(x, k):
    n = lax.axis_size("tensor")
    return lax.ppermute(x, "tensor", [(i, (i + k) % n) for i in range(n)])


def gather_ring(x):
    half = x.shape[0] // 2
    below, above = around(x, 1), around(x, -1)
    return x, below, above, around(below[:half], 1), around(above[half:], -1)


def on_device(gradient, left_stat, right_stat, left_root, right_root, block_owner):
    owners = lax.axis_size("fsdp")
    t = lax.axis_index("tensor").reshape(1)
    cols = gradient.shape[2]

    def exchange(x):
        return lax.all_to_all(x, "fsdp", split_axis=0, concat_axis=0, tiled=True)

    root_below, root_above = around(right_root, 1), around(right_root, -1)

    def root_far(slot):
        half = right_root.shape[1] // 2
        return around(root_below[slot, :half], 1), around(root_above[slot, half:], -1)

    routed = route(block_owner, gradient, owners)
    grads, returned = [], []
    for slot in range(2):
        grads.append(gather_ring(exchange(routed[slot]).reshape(-1, cols)))
        roots = (right_root, root_below, root_above) + root_far(slot)
        pieces = update_rows(slot, t, left_root, grads[slot], roots)
        arrived = [pieces[0]] + [around(pieces[k], k) for k in (1, 2, 3)]
        returned.append(exchange(scale(t, arrived).reshape(owners, -1, cols)))
    new_left, new_right = statistics(t, grads[0], grads[1], left_stat, right_stat)
    return (new_left, new_right, collect(block_owner, *returned))


def solution(mesh):
    return jax.shard_map(
        on_device,
        mesh=mesh,
        in_specs=(
            P(None, "fsdp", "tensor"),
            P("fsdp", "tensor", None),
            P("fsdp", "tensor", None),
            P("fsdp", "tensor", None),
            P("fsdp", "tensor", None),
            P(),
        ),
        out_specs=(P("fsdp", "tensor", None), P("fsdp", "tensor", None), P(None, "fsdp", "tensor")),
        check_vma=False,
    )
```

time: 258 us -> 170 us (0.66)
  waiting for transfers between devices: 154 us -> 61.4 us
  starting transfers between devices: 23.7 us -> 72.4 us
  Pallas kernels: 0 us -> 21.3 us
  blocking collectives: 20.9 us -> 0 us
  matrix products: 16.2 us -> 0 us
  between operations: 14.1 us -> 0.86 us
  local copies, waits for them, and re-layouts: 21.5 us -> 12.8 us
  other arithmetic: 6.87 us -> 0 us
    all_to_all x2 -> x4, waiting for transfers between devices: 113 us -> 24.1 us  [exchange(): return lax.all_to_all(x, 'fsdp', split_axis=0, concat_axis=0, tiled=True)]
    all_gather x2 -> x0, waiting for transfers between devices: 40.3 us -> none  [the longest x1 40.3 us: on_device(): wide_rows = lax.all_gather(gradient, 'tensor', axis=2, tiled=True)]
    ppermute x0 -> x20, waiting for transfers between devices: none -> 37.3 us  [around(): return lax.ppermute(x, 'tensor', [(i, (i + k) % n) for i in range(n)])]
    ppermute x0 -> x20, starting transfers between devices: none -> 27.6 us  [around(): return lax.ppermute(x, 'tensor', [(i, (i + k) % n) for i in range(n)])]
    pallas_call x0 -> x7, Pallas kernels: none -> 21.3 us  [the longest x2 7.52 us: update_rows(): pl.pallas_call(update_kernel, grid=(1,), out_shape=(out,) * 4, in_specs=[...]
    all_to_all x2 -> x4, starting transfers between devices: 23.7 us -> 44.8 us  [exchange(): return lax.all_to_all(x, 'fsdp', split_axis=0, concat_axis=0, tiled=True)]
    dot_general x3 -> x0, matrix products: 16.2 us -> none  [the longest x1 7.31 us: on_device(): jnp.einsum('sik,skj->sij', left_part, lax.all_gather(right_root, 'tensor'...]
    all_to_all x1 -> x0, blocking collectives: 13.1 us -> none  [on_device(): lax.all_to_all(grafted, 'tensor', split_axis=2, concat_axis=1, tiled=True)]
  transfers between devices with their start and end apart: 4 -> 24, of which waited for: 3 -> 14; matrix products, arithmetic and copies ran while one was open for 7% -> 3% of each run, Pallas kernels for 0% -> 9%
where the time goes in v1:
time: 170 us; the launch traced here: 169 us
  starting transfers between devices  72.4 us (43%)
  waiting for transfers between devices  61.4 us (36%)
  Pallas kernels  21.3 us (13%)
  local copies, waits for them, and re-layouts  12.8 us (8%)
    all_to_all x4, starting transfers between devices, exchange(): return lax.all_to_all(x, 'fsdp', split_axis=0, concat_axis=0, tiled=True)  44.8 us
    ppermute x20, waiting for transfers between devices, around(): return lax.ppermute(x, 'tensor', [(i, (i + k) % n) for i in range(n)])  37.3 us
    ppermute x20, starting transfers between devices, around(): return lax.ppermute(x, 'tensor', [(i, (i + k) % n) for i in range(n)])  27.6 us
    all_to_all x4, waiting for transfers between devices, exchange(): return lax.all_to_all(x, 'fsdp', split_axis=0, concat_axis=0, tiled=True)  24.1 us
    pallas_call x2, Pallas kernels, update_rows(): pl.pallas_call(update_kernel, grid=(1,), out_shape=(out,) * 4, in_specs=[...  7.52 us
    unnamed x44, local copies, waits for them, and re-layouts  7.51 us
    pallas_call x1, Pallas kernels, statistics(): pl.pallas_call(stats_kernel, grid=(slots,), out_shape=(shape, shape), in_...  6.55 us
    pallas_call x1, Pallas kernels, collect(): pl.pallas_call(collect_kernel, out_shape=jax.ShapeDtypeStruct((blocks,) +...  3.77 us
  transfers between devices with their start and end apart: 24, of which 14 were waited for; matrix products, arithmetic and copies ran while one was open for 3% of the time, Pallas kernels for 9%

profile of v1, /device:TPU:1, one launch (start us, length us, event | category | flops | bytes accessed | tf_op | source)
XLA Modules:
  0.0 168.9 jit_solution(15561256549422426)
XLA Ops:
  0.6 1.0 copy-done.18
  1.7 0.7 copy-done.20
  2.3 3.2 %route.1 = (bf16[64,16,256]{2,1,0:T(8,128)(2,1)S(1)}, bf16[64,16,256]{2,1,0:T(8,128)(2,1)}) custom-call(s32[64]{0:T(128)S(1)} %copy-done.20, bf16[64,16,256]{2,1,0:T(8,128)(2,1)S(1)} %copy-done.18), custom_call_target="tpu_custom_call" | custom-call | bytes 786432 | tf_op jit(solution)/shard_map/route/pallas_call | solution.py:59
  5.5 13.2 %all-to-all-start.1 = ((bf16[64,16,256]{2,1,0:T(8,128)(2,1)}), bf16[64,16,256]{2,1,0:T(8,128)(2,1)S(1)}, u32[]{:S(2)}, u32[]{:S(2)}) async-start(bf16[64,16,256]{2,1,0:T(8,128)(2,1)} %get-tuple-element.16), calls=%async_computation.1 | async-start | bytes 1048576 | tf_op jit(solution)/shard_map/all_to_all | solution.py:266
  18.7 1.3 collective-permute-start.8
  20.0 1.5 collective-permute-start.9
  21.4 15.0 %all-to-all-done.1 = bf16[64,16,256]{2,1,0:T(8,128)(2,1)S(1)} async-done(((bf16[64,16,256]{2,1,0:T(8,128)(2,1)}), bf16[64,16,256]{2,1,0:T(8,128)(2,1)S(1)}, u32[]{:S(2)}, u32[]{:S(2)}) %all-to-all-start.1) | async-done | bytes 524320 | tf_op jit(solution)/shard_map/all_to_all | solution.py:266
  36.4 5.9 %all-to-all-start = ((bf16[64,16,256]{2,1,0:T(8,128)(2,1)}), bf16[64,16,256]{2,1,0:T(8,128)(2,1)S(1)}, u32[]{:S(2)}, u32[]{:S(2)}) async-start(bf16[64,16,256]{2,1,0:T(8,128)(2,1)} %copy-done.19), calls=%async_computation | async-start | bytes 1048576 | tf_op jit(solution)/shard_map/all_to_all | solution.py:266
  42.2 1.3 collective-permute-start.4
  43.5 1.5 collective-permute-start.5
  45.0 1.9 %slice_bitcast_fusion.1 = (bf16[128,1024]{1,0:T(8,128)(2,1)}, bf16[128,1024]{1,0:T(8,128)(2,1)}) fusion(bf16[2,256,1024]{2,1,0:T(8,128)(2,1)} %collective-permute-done.8.r1), kind=kLoop, calls=%fused_computation.1 | loop fusion | bytes 1048576 | tf_op jit(solution)/shard_map/squeeze | solution.py:272
  46.9 1.9 %slice_bitcast_fusion = (bf16[128,1024]{1,0:T(8,128)(2,1)}, bf16[128,1024]{1,0:T(8,128)(2,1)}) fusion(bf16[2,256,1024]{2,1,0:T(8,128)(2,1)} %collective-permute-done.9.r3), kind=kLoop, calls=%fused_computation | loop fusion | bytes 1048576 | tf_op jit(solution)/shard_map/squeeze | solution.py:272
  48.8 2.7 %collective-permute-start.16 = (bf16[128,1024]{1,0:T(8,128)(2,1)}, bf16[128,1024]{1,0:T(8,128)(2,1)}, u32[]{:S(2)}, u32[]{:S(2)}) collective-permute-start(bf16[128,1024]{1,0:T(8,128)(2,1)} %get-tuple-element.27), channel_id=1, source_target_pairs={{0,3},{1,0},{2,1},{3,2},{4,7},{5,4},{6,5},{7,6},{8,11},{9,8},{10,9... | collective-permute-start | bytes 786440 | tf_op jit(solution)/shard_map/ppermute | solution.py:251
  51.5 5.1 %collective-permute-done.4.refs_6_.g1 = bf16[1024,256]{1,0:T(8,128)(2,1)S(1)} collective-permute-done((bf16[1024,256]{1,0:T(8,128)(2,1)S(1)}, bf16[1024,256]{1,0:T(8,128)(2,1)S(1)}, u32[]{:S(2)}, u32[]{:S(2)}) %collective-permute-start.4) | collective-permute-done | bytes 524320 | tf_op jit(solution)/shard_map/ppermute | solution.py:251
  56.6 0.8 slice.34
  57.5 0.8 slice.35
  58.4 2.6 %collective-permute-start.7 = (bf16[512,256]{1,0:T(8,128)(2,1)}, bf16[512,256]{1,0:T(8,128)(2,1)}, u32[]{:S(2)}, u32[]{:S(2)}) collective-permute-start(bf16[512,256]{1,0:T(8,128)(2,1)} %slice.35), channel_id=1, source_target_pairs={{0,3},{1,0},{2,1},{3,2},{4,7},{5,4},{6,5},{7,6},{8,11},{9,8},{10,9... | collective-permute-start | bytes 786440 | tf_op jit(solution)/shard_map/ppermute | solution.py:251
  60.9 1.4 collective-permute-done.15.r2a
  62.3 5.3 %collective-permute-done.6.refs_8_.g2a = bf16[512,256]{1,0:T(8,128)(2,1)S(1)} collective-permute-done((bf16[512,256]{1,0:T(8,128)(2,1)}, bf16[512,256]{1,0:T(8,128)(2,1)S(1)}, u32[]{:S(2)}, u32[]{:S(2)}) %collective-permute-start.6) | collective-permute-done | bytes 262176 | tf_op jit(solution)/shard_map/ppermute | solution.py:251
  67.6 1.0 copy-done.3
  68.7 1.0 copy-done.6
  69.7 3.8 %update_rows.3 = (bf16[272,256]{1,0:T(8,128)(2,1)S(1)}, bf16[272,256]{1,0:T(8,128)(2,1)S(1)}, bf16[272,256]{1,0:T(8,128)(2,1)S(1)}, bf16[272,256]{1,0:T(8,128)(2,1)S(1)}) custom-call(s32[1]{0:T(128)} %bitcast.t_ref, bf16[2,256,1024]{2,1,0:T(8,128)(2,1)S(1)} %copy-done, bf16[1024,256]{1,0:T(8,128)(2,1)S(1)} %bitcast.15, bf16[1024,256]{1,0:T(8,128)(2,1)S(1)} %copy-done.3, ...), custom_call_target="tpu_custom_call" | custom-call | flops 1073741824 | bytes 5242880 | tf_op jit(solution)/shard_map/update_rows/pallas_call | solution.py:153
  73.5 1.3 collective-permute-start.17
  74.8 1.6 collective-permute-start.18
  76.4 1.7 %collective-permute-start.19 = (bf16[272,256]{1,0:T(8,128)(2,1)S(1)}, bf16[272,256]{1,0:T(8,128)(2,1)S(1)}, u32[]{:S(2)}, u32[]{:S(2)}) collective-permute-start(bf16[272,256]{1,0:T(8,128)(2,1)S(1)} %get-tuple-element.26), channel_id=1, source_target_pairs={{0,3},{1,0},{2,1},{3,2},{4,7},{5,4},{6,5},{7,6},{8,11},{9,8},{10,9... | collective-permute-start | bytes 417800 | tf_op jit(solution)/shard_map/ppermute | solution.py:251
  78.1 0.6 collective-permute-done.17.q1
  78.7 1.7 %collective-permute-done.18.q2 = bf16[272,256]{1,0:T(8,128)(2,1)S(1)} collective-permute-done((bf16[272,256]{1,0:T(8,128)(2,1)S(1)}, bf16[272,256]{1,0:T(8,128)(2,1)S(1)}, u32[]{:S(2)}, u32[]{:S(2)}) %collective-permute-start.18) | collective-permute-done | bytes 139296 | tf_op jit(solution)/shard_map/ppermute | solution.py:251
  80.4 1.3 collective-permute-done.19.q3
  81.8 0.8 copy-done.12
  82.6 13.1 %all-to-all-start.3 = ((bf16[64,16,256]{2,1,0:T(8,128)(2,1)}), bf16[64,16,256]{2,1,0:T(8,128)(2,1)}, u32[]{:S(2)}, u32[]{:S(2)}) async-start(bf16[64,16,256]{2,1,0:T(8,128)(2,1)} %bitcast.21), calls=%async_computation.3 | async-start | bytes 1048576 | tf_op jit(solution)/shard_map/all_to_all | solution.py:266
  95.7 1.4 collective-permute-start
  97.2 1.3 collective-permute-start.1
  98.6 2.5 %collective-permute-start.11 = (bf16[128,1024]{1,0:T(8,128)(2,1)}, bf16[128,1024]{1,0:T(8,128)(2,1)S(1)}, u32[]{:S(2)}, u32[]{:S(2)}) collective-permute-start(bf16[128,1024]{1,0:T(8,128)(2,1)} %get-tuple-element.28), channel_id=1, source_target_pairs={{0,3},{1,0},{2,1},{3,2},{4,7},{5,4},{6,5},{7,6},{8,11},{9,8},{10,9... | collective-permute-start | bytes 786440 | tf_op jit(solution)/shard_map/ppermute | solution.py:251
  101.2 8.9 %collective-permute-done.refs_1_.g1 = bf16[1024,256]{1,0:T(8,128)(2,1)S(1)} collective-permute-done((bf16[1024,256]{1,0:T(8,128)(2,1)S(1)}, bf16[1024,256]{1,0:T(8,128)(2,1)S(1)}, u32[]{:S(2)}, u32[]{:S(2)}) %collective-permute-start) | collective-permute-done | bytes 524320 | tf_op jit(solution)/shard_map/ppermute | solution.py:251
  110.4 2.6 %collective-permute-start.3 = (bf16[512,256]{1,0:T(8,128)(2,1)S(1)}, bf16[512,256]{1,0:T(8,128)(2,1)S(1)}, u32[]{:S(2)}, u32[]{:S(2)}) collective-permute-start(bf16[512,256]{1,0:T(8,128)(2,1)S(1)} %slice.33), channel_id=1, source_target_pairs={{0,3},{1,0},{2,1},{3,2},{4,7},{5,4},{6,5},{7,6},{8,11},{9,8},{10,9... | collective-permute-start | bytes 786440 | tf_op jit(solution)/shard_map/ppermute | solution.py:251
  113.0 2.6 %collective-permute-done.10.r2a = bf16[128,1024]{1,0:T(8,128)(2,1)S(1)} collective-permute-done((bf16[128,1024]{1,0:T(8,128)(2,1)}, bf16[128,1024]{1,0:T(8,128)(2,1)S(1)}, u32[]{:S(2)}, u32[]{:S(2)}) %collective-permute-start.10) | collective-permute-done | bytes 262176 | tf_op jit(solution)/shard_map/ppermute | solution.py:251
  115.6 5.6 %collective-permute-done.2.refs_3_.g2a = bf16[512,256]{1,0:T(8,128)(2,1)S(1)} collective-permute-done((bf16[512,256]{1,0:T(8,128)(2,1)S(1)}, bf16[512,256]{1,0:T(8,128)(2,1)S(1)}, u32[]{:S(2)}, u32[]{:S(2)}) %collective-permute-start.2) | collective-permute-done | bytes 262176 | tf_op jit(solution)/shard_map/ppermute | solution.py:251
  121.2 3.7 %update_rows.2 = (bf16[272,256]{1,0:T(8,128)(2,1)S(1)}, bf16[272,256]{1,0:T(8,128)(2,1)S(1)}, bf16[272,256]{1,0:T(8,128)(2,1)S(1)}, bf16[272,256]{1,0:T(8,128)(2,1)S(1)}) custom-call(s32[1]{0:T(128)} %bitcast.t_ref, bf16[2,256,1024]{2,1,0:T(8,128)(2,1)S(1)} %copy-done, bf16[1024,256]{1,0:T(8,128)(2,1)S(1)} %bitcast.19, ...), custom_call_target="tpu_custom_call" | custom-call | flops 1073741824 | bytes 5242880 | tf_op jit(solution)/shard_map/update_rows/pallas_call | solution.py:153
  125.5 3.0 %collective-permute-start.13 = (bf16[272,256]{1,0:T(8,128)(2,1)S(1)}, bf16[272,256]{1,0:T(8,128)(2,1)S(1)}, u32[]{:S(2)}, u32[]{:S(2)}) collective-permute-start(bf16[272,256]{1,0:T(8,128)(2,1)S(1)} %get-tuple-element.21), channel_id=1, source_target_pairs={{0,2},{1,3},{2,0},{3,1},{4,6},{5,7},{6,4},{7,5},{8,10},{9,11},{10,... | collective-permute-start | bytes 417800 | tf_op jit(solution)/shard_map/ppermute | solution.py:251
  129.1 1.2 collective-permute-done.12.q1
  130.2 3.0 %collective-permute-done.13.q2 = bf16[272,256]{1,0:T(8,128)(2,1)S(1)} collective-permute-done((bf16[272,256]{1,0:T(8,128)(2,1)S(1)}, bf16[272,256]{1,0:T(8,128)(2,1)S(1)}, u32[]{:S(2)}, u32[]{:S(2)}) %collective-permute-start.13) | collective-permute-done | bytes 139296 | tf_op jit(solution)/shard_map/ppermute | solution.py:251
  134.0 0.8 copy-done.13
  134.8 12.7 %all-to-all-start.2 = ((bf16[64,16,256]{2,1,0:T(8,128)(2,1)}), bf16[64,16,256]{2,1,0:T(8,128)(2,1)}, u32[]{:S(2)}, u32[]{:S(2)}) async-start(bf16[64,16,256]{2,1,0:T(8,128)(2,1)} %bitcast.22), calls=%async_computation.2 | async-start | bytes 1048576 | tf_op jit(solution)/shard_map/all_to_all | solution.py:266
  147.5 0.9 copy-done.15
  148.5 0.9 copy-done.17
  149.4 6.6 %statistics.1 = (f32[2,256,1024]{2,1,0:T(8,128)}, f32[2,256,1024]{2,1,0:T(8,128)}) custom-call(s32[1]{0:T(128)} %bitcast.t_ref, bf16[1024,256]{1,0:T(8,128)(2,1)S(1)} %bitcast.20, bf16[1024,256]{1,0:T(8,128)(2,1)S(1)} %copy-done.9, bf16[1024,256]{1,0:T(8,128)(2,1)S(1)} %copy-done.11, bf16[512,256]{1,0:T(8,128)(2,1)S(1)} %copy-done.15, ...), custom_call_target="tpu_custom_call" | custom-call | flops 2147483648 | bytes 6291456 | tf_op jit(solution)/shard_map/statistics/pallas_call | solution.py:237
  156.0 9.1 %all-to-all-done.2.first_ref = bf16[64,16,256]{2,1,0:T(8,128)(2,1)} async-done(((bf16[64,16,256]{2,1,0:T(8,128)(2,1)}), bf16[64,16,256]{2,1,0:T(8,128)(2,1)}, u32[]{:S(2)}, u32[]{:S(2)}) %all-to-all-start.2) | async-done | bytes 524320 | tf_op jit(solution)/shard_map/all_to_all | solution.py:266
  165.1 3.8 %collect.1 = bf16[64,16,256]{2,1,0:T(8,128)(2,1)} custom-call(s32[64]{0:T(128)S(1)} %copy-done.21, bf16[64,16,256]{2,1,0:T(8,128)(2,1)} %all-to-all-done.2.first_ref, bf16[64,16,256]{2,1,0:T(8,128)(2,1)} %all-to-all-done.3.second_ref), custom_call_target="tpu_custom_call" | custom-call | bytes 786432 | tf_op jit(solution)/shard_map/collect/pallas_call | solution.py:94
  (57 shorter events, 2.6 us)
Async XLA Ops:
  0.6 1.0 copy-start.18
  1.7 0.7 copy-start.20
  5.5 30.9 %copy-start.19 = (bf16[64,16,256]{2,1,0:T(8,128)(2,1)}, bf16[64,16,256]{2,1,0:T(8,128)(2,1)S(1)}, u32[]{:S(2)}) copy-start(bf16[64,16,256]{2,1,0:T(8,128)(2,1)S(1)} %get-tuple-element.15) | copy-start | bytes 1572868
  5.5 30.9 %all-to-all-start.1 = ((bf16[64,16,256]{2,1,0:T(8,128)(2,1)}), bf16[64,16,256]{2,1,0:T(8,128)(2,1)S(1)}, u32[]{:S(2)}, u32[]{:S(2)}) async-start(bf16[64,16,256]{2,1,0:T(8,128)(2,1)} %get-tuple-element.16), calls=%async_computation.1 | async-start | bytes 1048576 | tf_op jit(solution)/shard_map/all_to_all | solution.py:266
  18.7 26.3 %collective-permute-start.8 = (bf16[2,256,1024]{2,1,0:T(8,128)(2,1)}, bf16[2,256,1024]{2,1,0:T(8,128)(2,1)}, u32[]{:S(2)}, u32[]{:S(2)}) collective-permute-start(bf16[2,256,1024]{2,1,0:T(8,128)(2,1)} %r0.3), channel_id=1, source_target_pairs={{0,1},{1,2},{2,3},{3,0},{4,5},{5,6},{6,7},{7,4},{8,9},{9,10},{10,1... | collective-permute-start | bytes 3145736 | tf_op jit(solution)/shard_map/ppermute | solution.py:251
  20.0 26.9 %collective-permute-start.9 = (bf16[2,256,1024]{2,1,0:T(8,128)(2,1)}, bf16[2,256,1024]{2,1,0:T(8,128)(2,1)}, u32[]{:S(2)}, u32[]{:S(2)}) collective-permute-start(bf16[2,256,1024]{2,1,0:T(8,128)(2,1)} %r0.3), channel_id=1, source_target_pairs={{0,3},{1,0},{2,1},{3,2},{4,7},{5,4},{6,5},{7,6},{8,11},{9,8},{10,9... | collective-permute-start | bytes 3145736 | tf_op jit(solution)/shard_map/ppermute | solution.py:251
  36.4 31.2 %copy-start = (bf16[2,256,1024]{2,1,0:T(8,128)(2,1)S(1)}, bf16[2,256,1024]{2,1,0:T(8,128)(2,1)}, u32[]{:S(2)}) copy-start(bf16[2,256,1024]{2,1,0:T(8,128)(2,1)} %l_ref.3) | copy-start | bytes 3145732
  36.4 31.2 %copy-start.1 = (bf16[2,256,1024]{2,1,0:T(8,128)(2,1)S(1)}, bf16[2,256,1024]{2,1,0:T(8,128)(2,1)}, u32[]{:S(2)}) copy-start(bf16[2,256,1024]{2,1,0:T(8,128)(2,1)} %r0.3) | copy-start | bytes 3145732
  36.4 46.2 %all-to-all-start = ((bf16[64,16,256]{2,1,0:T(8,128)(2,1)}), bf16[64,16,256]{2,1,0:T(8,128)(2,1)S(1)}, u32[]{:S(2)}, u32[]{:S(2)}) async-start(bf16[64,16,256]{2,1,0:T(8,128)(2,1)} %copy-done.19), calls=%async_computation | async-start | bytes 1048576 | tf_op jit(solution)/shard_map/all_to_all | solution.py:266
  42.2 14.3 %collective-permute-start.4 = (bf16[1024,256]{1,0:T(8,128)(2,1)S(1)}, bf16[1024,256]{1,0:T(8,128)(2,1)S(1)}, u32[]{:S(2)}, u32[]{:S(2)}) collective-permute-start(bf16[1024,256]{1,0:T(8,128)(2,1)S(1)} %bitcast.13), channel_id=1, source_target_pairs={{0,1},{1,2},{2,3},{3,0},{4,5},{5,6},{6,7},{7,4},{8,9},{9,10},{10,1... | collective-permute-start | bytes 1572872 | tf_op jit(solution)/shard_map/ppermute | solution.py:251
  43.5 13.8 %collective-permute-start.5 = (bf16[1024,256]{1,0:T(8,128)(2,1)S(1)}, bf16[1024,256]{1,0:T(8,128)(2,1)S(1)}, u32[]{:S(2)}, u32[]{:S(2)}) collective-permute-start(bf16[1024,256]{1,0:T(8,128)(2,1)S(1)} %bitcast.14), channel_id=1, source_target_pairs={{0,3},{1,0},{2,1},{3,2},{4,7},{5,4},{6,5},{7,6},{8,11},{9,8},{10,9... | collective-permute-start | bytes 1572872 | tf_op jit(solution)/shard_map/ppermute | solution.py:251
  46.9 15.4 %collective-permute-start.15 = (bf16[128,1024]{1,0:T(8,128)(2,1)}, bf16[128,1024]{1,0:T(8,128)(2,1)}, u32[]{:S(2)}, u32[]{:S(2)}) collective-permute-start(bf16[128,1024]{1,0:T(8,128)(2,1)} %get-tuple-element.29), channel_id=1, source_target_pairs={{0,1},{1,2},{2,3},{3,0},{4,5},{5,6},{6,7},{7,4},{8,9},{9,10},{10,1... | collective-permute-start | bytes 786440 | tf_op jit(solution)/shard_map/ppermute | solution.py:251
  48.8 13.5 %collective-permute-start.16 = (bf16[128,1024]{1,0:T(8,128)(2,1)}, bf16[128,1024]{1,0:T(8,128)(2,1)}, u32[]{:S(2)}, u32[]{:S(2)}) collective-permute-start(bf16[128,1024]{1,0:T(8,128)(2,1)} %get-tuple-element.27), channel_id=1, source_target_pairs={{0,3},{1,0},{2,1},{3,2},{4,7},{5,4},{6,5},{7,6},{8,11},{9,8},{10,9... | collective-permute-start | bytes 786440 | tf_op jit(solution)/shard_map/ppermute | solution.py:251
  56.6 0.9 copy-start.2
  57.4 10.3 %collective-permute-start.6 = (bf16[512,256]{1,0:T(8,128)(2,1)}, bf16[512,256]{1,0:T(8,128)(2,1)S(1)}, u32[]{:S(2)}, u32[]{:S(2)}) collective-permute-start(bf16[512,256]{1,0:T(8,128)(2,1)} %slice.34), channel_id=1, source_target_pairs={{0,1},{1,2},{2,3},{3,0},{4,5},{5,6},{6,7},{7,4},{8,9},{9,10},{10,1... | collective-permute-start | bytes 786440 | tf_op jit(solution)/shard_map/ppermute | solution.py:251
  57.5 0.9 copy-start.5
  58.4 9.3 %collective-permute-start.7 = (bf16[512,256]{1,0:T(8,128)(2,1)}, bf16[512,256]{1,0:T(8,128)(2,1)}, u32[]{:S(2)}, u32[]{:S(2)}) collective-permute-start(bf16[512,256]{1,0:T(8,128)(2,1)} %slice.35), channel_id=1, source_target_pairs={{0,3},{1,0},{2,1},{3,2},{4,7},{5,4},{6,5},{7,6},{8,11},{9,8},{10,9... | collective-permute-start | bytes 786440 | tf_op jit(solution)/shard_map/ppermute | solution.py:251
  67.6 1.0 copy-start.3
  68.7 1.0 copy-start.6
  73.5 5.2 %collective-permute-start.17 = (bf16[272,256]{1,0:T(8,128)(2,1)S(1)}, bf16[272,256]{1,0:T(8,128)(2,1)S(1)}, u32[]{:S(2)}, u32[]{:S(2)}) collective-permute-start(bf16[272,256]{1,0:T(8,128)(2,1)S(1)} %get-tuple-element.24), channel_id=1, source_target_pairs={{0,1},{1,2},{2,3},{3,0},{4,5},{5,6},{6,7},{7,4},{8,9},{9,10},{10,1... | collective-permute-start | bytes 417800 | tf_op jit(solution)/shard_map/ppermute | solution.py:251
  74.8 5.6 %collective-permute-start.18 = (bf16[272,256]{1,0:T(8,128)(2,1)S(1)}, bf16[272,256]{1,0:T(8,128)(2,1)S(1)}, u32[]{:S(2)}, u32[]{:S(2)}) collective-permute-start(bf16[272,256]{1,0:T(8,128)(2,1)S(1)} %get-tuple-element.25), channel_id=1, source_target_pairs={{0,2},{1,3},{2,0},{3,1},{4,6},{5,7},{6,4},{7,5},{8,10},{9,11},{10,... | collective-permute-start | bytes 417800 | tf_op jit(solution)/shard_map/ppermute | solution.py:251
  76.4 5.3 %collective-permute-start.19 = (bf16[272,256]{1,0:T(8,128)(2,1)S(1)}, bf16[272,256]{1,0:T(8,128)(2,1)S(1)}, u32[]{:S(2)}, u32[]{:S(2)}) collective-permute-start(bf16[272,256]{1,0:T(8,128)(2,1)S(1)} %get-tuple-element.26), channel_id=1, source_target_pairs={{0,3},{1,0},{2,1},{3,2},{4,7},{5,4},{6,5},{7,6},{8,11},{9,8},{10,9... | collective-permute-start | bytes 417800 | tf_op jit(solution)/shard_map/ppermute | solution.py:251
  81.8 0.8 copy-start.12
  82.6 52.2 %all-to-all-start.3 = ((bf16[64,16,256]{2,1,0:T(8,128)(2,1)}), bf16[64,16,256]{2,1,0:T(8,128)(2,1)}, u32[]{:S(2)}, u32[]{:S(2)}) async-start(bf16[64,16,256]{2,1,0:T(8,128)(2,1)} %bitcast.21), calls=%async_computation.3 | async-start | bytes 1048576 | tf_op jit(solution)/shard_map/all_to_all | solution.py:266
  95.7 14.3 %collective-permute-start = (bf16[1024,256]{1,0:T(8,128)(2,1)S(1)}, bf16[1024,256]{1,0:T(8,128)(2,1)S(1)}, u32[]{:S(2)}, u32[]{:S(2)}) collective-permute-start(bf16[1024,256]{1,0:T(8,128)(2,1)S(1)} %bitcast.17), channel_id=1, source_target_pairs={{0,1},{1,2},{2,3},{3,0},{4,5},{5,6},{6,7},{7,4},{8,9},{9,10},{10,1... | collective-permute-start | bytes 1572872 | tf_op jit(solution)/shard_map/ppermute | solution.py:251
  97.2 13.2 %collective-permute-start.1 = (bf16[1024,256]{1,0:T(8,128)(2,1)S(1)}, bf16[1024,256]{1,0:T(8,128)(2,1)S(1)}, u32[]{:S(2)}, u32[]{:S(2)}) collective-permute-start(bf16[1024,256]{1,0:T(8,128)(2,1)S(1)} %bitcast.18), channel_id=1, source_target_pairs={{0,3},{1,0},{2,1},{3,2},{4,7},{5,4},{6,5},{7,6},{8,11},{9,8},{10,9... | collective-permute-start | bytes 1572872 | tf_op jit(solution)/shard_map/ppermute | solution.py:251
  98.5 17.1 %collective-permute-start.10 = (bf16[128,1024]{1,0:T(8,128)(2,1)}, bf16[128,1024]{1,0:T(8,128)(2,1)S(1)}, u32[]{:S(2)}, u32[]{:S(2)}) collective-permute-start(bf16[128,1024]{1,0:T(8,128)(2,1)} %get-tuple-element.30), channel_id=1, source_target_pairs={{0,1},{1,2},{2,3},{3,0},{4,5},{5,6},{6,7},{7,4},{8,9},{9,10},{10,1... | collective-permute-start | bytes 786440 | tf_op jit(solution)/shard_map/ppermute | solution.py:251
  98.6 17.0 %collective-permute-start.11 = (bf16[128,1024]{1,0:T(8,128)(2,1)}, bf16[128,1024]{1,0:T(8,128)(2,1)S(1)}, u32[]{:S(2)}, u32[]{:S(2)}) collective-permute-start(bf16[128,1024]{1,0:T(8,128)(2,1)} %get-tuple-element.28), channel_id=1, source_target_pairs={{0,3},{1,0},{2,1},{3,2},{4,7},{5,4},{6,5},{7,6},{8,11},{9,8},{10,9... | collective-permute-start | bytes 786440 | tf_op jit(solution)/shard_map/ppermute | solution.py:251
  110.1 14.9 %copy-start.8 = (bf16[1024,256]{1,0:T(8,128)(2,1)}, bf16[1024,256]{1,0:T(8,128)(2,1)S(1)}, u32[]{:S(2)}) copy-start(bf16[1024,256]{1,0:T(8,128)(2,1)S(1)} %collective-permute-done.refs_1_.g1) | copy-start | bytes 1572868
  110.1 11.1 %collective-permute-start.2 = (bf16[512,256]{1,0:T(8,128)(2,1)S(1)}, bf16[512,256]{1,0:T(8,128)(2,1)S(1)}, u32[]{:S(2)}, u32[]{:S(2)}) collective-permute-start(bf16[512,256]{1,0:T(8,128)(2,1)S(1)} %slice.32), channel_id=1, source_target_pairs={{0,1},{1,2},{2,3},{3,0},{4,5},{5,6},{6,7},{7,4},{8,9},{9,10},{10,1... | collective-permute-start | bytes 786440 | tf_op jit(solution)/shard_map/ppermute | solution.py:251
  110.3 14.6 %copy-start.10 = (bf16[1024,256]{1,0:T(8,128)(2,1)}, bf16[1024,256]{1,0:T(8,128)(2,1)S(1)}, u32[]{:S(2)}) copy-start(bf16[1024,256]{1,0:T(8,128)(2,1)S(1)} %collective-permute-done.1.refs_2_.g3) | copy-start | bytes 1572868
  110.4 10.9 %collective-permute-start.3 = (bf16[512,256]{1,0:T(8,128)(2,1)S(1)}, bf16[512,256]{1,0:T(8,128)(2,1)S(1)}, u32[]{:S(2)}, u32[]{:S(2)}) collective-permute-start(bf16[512,256]{1,0:T(8,128)(2,1)S(1)} %slice.33), channel_id=1, source_target_pairs={{0,3},{1,0},{2,1},{3,2},{4,7},{5,4},{6,5},{7,6},{8,11},{9,8},{10,9... | collective-permute-start | bytes 786440 | tf_op jit(solution)/shard_map/ppermute | solution.py:251
  121.2 3.8 %copy-start.14 = (bf16[512,256]{1,0:T(8,128)(2,1)}, bf16[512,256]{1,0:T(8,128)(2,1)S(1)}, u32[]{:S(2)}) copy-start(bf16[512,256]{1,0:T(8,128)(2,1)S(1)} %collective-permute-done.2.refs_3_.g2a) | copy-start | bytes 786436
  121.2 3.8 %copy-start.16 = (bf16[512,256]{1,0:T(8,128)(2,1)}, bf16[512,256]{1,0:T(8,128)(2,1)S(1)}, u32[]{:S(2)}) copy-start(bf16[512,256]{1,0:T(8,128)(2,1)S(1)} %collective-permute-done.3.refs_4_.g2b) | copy-start | bytes 786436
  125.0 22.5 %copy-start.4 = (bf16[1024,256]{1,0:T(8,128)(2,1)S(1)}, bf16[1024,256]{1,0:T(8,128)(2,1)}, u32[]{:S(2)}) copy-start(bf16[1024,256]{1,0:T(8,128)(2,1)} %copy-done.2) | copy-start | bytes 1572868
  125.0 22.5 %copy-start.7 = (bf16[1024,256]{1,0:T(8,128)(2,1)S(1)}, bf16[1024,256]{1,0:T(8,128)(2,1)}, u32[]{:S(2)}) copy-start(bf16[1024,256]{1,0:T(8,128)(2,1)} %copy-done.5) | copy-start | bytes 1572868
  125.0 22.5 %copy-start.9 = (bf16[1024,256]{1,0:T(8,128)(2,1)S(1)}, bf16[1024,256]{1,0:T(8,128)(2,1)}, u32[]{:S(2)}) copy-start(bf16[1024,256]{1,0:T(8,128)(2,1)} %copy-done.8) | copy-start | bytes 1572868
  125.0 22.5 %copy-start.11 = (bf16[1024,256]{1,0:T(8,128)(2,1)S(1)}, bf16[1024,256]{1,0:T(8,128)(2,1)}, u32[]{:S(2)}) copy-start(bf16[1024,256]{1,0:T(8,128)(2,1)} %copy-done.10) | copy-start | bytes 1572868
  125.0 5.2 %collective-permute-start.12 = (bf16[272,256]{1,0:T(8,128)(2,1)S(1)}, bf16[272,256]{1,0:T(8,128)(2,1)S(1)}, u32[]{:S(2)}, u32[]{:S(2)}) collective-permute-start(bf16[272,256]{1,0:T(8,128)(2,1)S(1)} %get-tuple-element.20), channel_id=1, source_target_pairs={{0,1},{1,2},{2,3},{3,0},{4,5},{5,6},{6,7},{7,4},{8,9},{9,10},{10,1... | collective-permute-start | bytes 417800 | tf_op jit(solution)/shard_map/ppermute | solution.py:251
  125.5 7.7 %collective-permute-start.13 = (bf16[272,256]{1,0:T(8,128)(2,1)S(1)}, bf16[272,256]{1,0:T(8,128)(2,1)S(1)}, u32[]{:S(2)}, u32[]{:S(2)}) collective-permute-start(bf16[272,256]{1,0:T(8,128)(2,1)S(1)} %get-tuple-element.21), channel_id=1, source_target_pairs={{0,2},{1,3},{2,0},{3,1},{4,6},{5,7},{6,4},{7,5},{8,10},{9,11},{10,... | collective-permute-start | bytes 417800 | tf_op jit(solution)/shard_map/ppermute | solution.py:251
  128.6 5.2 %collective-permute-start.14 = (bf16[272,256]{1,0:T(8,128)(2,1)S(1)}, bf16[272,256]{1,0:T(8,128)(2,1)S(1)}, u32[]{:S(2)}, u32[]{:S(2)}) collective-permute-start(bf16[272,256]{1,0:T(8,128)(2,1)S(1)} %get-tuple-element.22), channel_id=1, source_target_pairs={{0,3},{1,0},{2,1},{3,2},{4,7},{5,4},{6,5},{7,6},{8,11},{9,8},{10,9... | collective-permute-start | bytes 417800 | tf_op jit(solution)/shard_map/ppermute | solution.py:251
  134.0 0.8 copy-start.13
  134.8 30.3 %all-to-all-start.2 = ((bf16[64,16,256]{2,1,0:T(8,128)(2,1)}), bf16[64,16,256]{2,1,0:T(8,128)(2,1)}, u32[]{:S(2)}, u32[]{:S(2)}) async-start(bf16[64,16,256]{2,1,0:T(8,128)(2,1)} %bitcast.22), calls=%async_computation.2 | async-start | bytes 1048576 | tf_op jit(solution)/shard_map/all_to_all | solution.py:266
  147.5 1.0 copy-start.15
  148.5 0.9 copy-start.17
  149.4 15.7 %copy-start.21 = (s32[64]{0:T(128)S(1)}, s32[64]{0:T(128)}, u32[]{:S(2)}) copy-start(s32[64]{0:T(128)} %owner_ref.3) | copy-start | bytes 772

commit v2 on v1

v2 whole, which is shorter than its diff:
```python
import functools

import jax
import jax.numpy as jnp
from jax import lax
from jax.experimental import pallas as pl
from jax.experimental.pallas import tpu as pltpu
from jax.sharding import PartitionSpec as P

DECAY = 0.99
EPSILON = 1e-06
BF16 = jnp.bfloat16
F32 = jnp.float32
VMEM_SPEC = pl.BlockSpec(memory_space=pltpu.VMEM)
SMEM_SPEC = pl.BlockSpec(memory_space=pltpu.SMEM)
ANY_SPEC = pl.BlockSpec(memory_space=pl.ANY)
PARAMS = pltpu.CompilerParams(vmem_limit_bytes=48 * 1024 * 1024)


def dot(a, b, ca=1, cb=0):
    return lax.dot_general(a, b, (((ca,), (cb,)), ((), ())), preferred_element_type=F32)


def cost(flops, nbytes):
    return pl.CostEstimate(flops=flops, bytes_accessed=nbytes, transcendentals=0)


def clear_counts(count_ref, owners):
    def clear(i, _):
        count_ref[i] = 0
        return 0

    lax.fori_loop(0, owners, clear, 0, unroll=8)


def route_kernel(owner_ref, grad_hbm, out_hbm, grad, out, count_ref, sems):
    bring = pltpu.make_async_copy(grad_hbm, grad, sems.at[0])
    bring.start()
    out[...] = jnp.zeros_like(out)
    clear_counts(count_ref, out.shape[0])
    bring.wait()

    def body(b, _):
        o = owner_ref[b]
        c = count_ref[o]
        count_ref[o] = c + 1
        out[o, c] = grad[b]
        return 0

    lax.fori_loop(0, grad.shape[0], body, 0, unroll=8)
    send = pltpu.make_async_copy(out, out_hbm, sems.at[1])
    send.start()
    send.wait()


def route(block_owner, gradient, owners):
    _, rows, cols = gradient.shape
    shape = (owners, 2, rows, cols)
    return pl.pallas_call(
        route_kernel,
        out_shape=jax.ShapeDtypeStruct(shape, gradient.dtype),
        in_specs=[SMEM_SPEC, ANY_SPEC],
        out_specs=ANY_SPEC,
        scratch_shapes=[
            pltpu.VMEM(gradient.shape, gradient.dtype),
            pltpu.VMEM(shape, gradient.dtype),
            pltpu.SMEM((owners,), jnp.int32),
            pltpu.SemaphoreType.DMA((2,)),
        ],
        compiler_params=PARAMS,
        cost_estimate=cost(0, 3 * gradient.size),
        name="route",
    )(block_owner, gradient)


def collect_kernel(owner_ref, slots_hbm, out_hbm, slots, out, count_ref, sems):
    bring = pltpu.make_async_copy(slots_hbm, slots, sems.at[0])
    bring.start()
    clear_counts(count_ref, slots.shape[0])
    bring.wait()

    def body(b, _):
        o = owner_ref[b]
        c = count_ref[o]
        count_ref[o] = c + 1
        out[b] = slots[o, c]
        return 0

    lax.fori_loop(0, out.shape[0], body, 0, unroll=8)
    send = pltpu.make_async_copy(out, out_hbm, sems.at[1])
    send.start()
    send.wait()


def collect(block_owner, slots):
    shape = (block_owner.shape[0],) + slots.shape[2:]
    return pl.pallas_call(
        collect_kernel,
        out_shape=jax.ShapeDtypeStruct(shape, slots.dtype),
        in_specs=[SMEM_SPEC, ANY_SPEC],
        out_specs=ANY_SPEC,
        scratch_shapes=[
            pltpu.VMEM(slots.shape, slots.dtype),
            pltpu.VMEM(shape, slots.dtype),
            pltpu.SMEM((slots.shape[0],), jnp.int32),
            pltpu.SemaphoreType.DMA((2,)),
        ],
        compiler_params=PARAMS,
        cost_estimate=cost(0, 3 * slots.size),
        name="collect",
    )(block_owner, slots)


def split_kernel(both_hbm, first_hbm, second_hbm, sems):
    copies = [
        pltpu.make_async_copy(both_hbm.at[:, slot], out, sems.at[slot])
        for slot, out in enumerate((first_hbm, second_hbm))
    ]
    for c in copies:
        c.start()
    for c in copies:
        c.wait()


def split(both):
    shape = jax.ShapeDtypeStruct((both.shape[0],) + both.shape[2:], both.dtype)
    return pl.pallas_call(
        split_kernel,
        out_shape=(shape, shape),
        in_specs=[ANY_SPEC],
        out_specs=(ANY_SPEC, ANY_SPEC),
        scratch_shapes=[pltpu.SemaphoreType.DMA((2,))],
        compiler_params=PARAMS,
        cost_estimate=cost(0, 4 * both.size),
        name="split",
    )(both)


def three_parts(value):
    high = value.astype(BF16)
    rest = value - high.astype(F32)
    middle = rest.astype(BF16)
    low = (rest - middle.astype(F32)).astype(BF16)
    return high, middle, low


def pick_kernel(first, second, below_hbm, above_hbm, first_hbm, second_hbm, sems):
    copies = [
        pltpu.make_async_copy(below_hbm.at[first], first_hbm, sems.at[0]),
        pltpu.make_async_copy(above_hbm.at[second], second_hbm, sems.at[1]),
    ]
    for c in copies:
        c.start()
    for c in copies:
        c.wait()


def pick(below, above, first, second, shape, flops):
    shape = jax.ShapeDtypeStruct(shape, below.dtype)
    return pl.pallas_call(
        functools.partial(pick_kernel, first, second),
        out_shape=(shape, shape),
        in_specs=[ANY_SPEC] * 2,
        out_specs=(ANY_SPEC, ANY_SPEC),
        scratch_shapes=[pltpu.SemaphoreType.DMA((2,))],
        compiler_params=PARAMS,
        cost_estimate=cost(flops, 4 * below.size),
        name="pick",
    )(below, above)


def opposite(below, above):
    rows, width = below.shape
    half = rows // 2
    upper, lower = pick(below, above, pl.ds(0, half), pl.ds(half, half), (half, width), 3 * 10**10)
    return around(upper, 1), around(lower, -1)


def update_kernel(
    slot, t_ref, l_hbm, g0, g1, g3, g2a, g2b, r0, r1, r3, r2, o0, o1, o2, o3, left, grads, roots, raw_ref, sems
):
    bring = [pltpu.make_async_copy(l_hbm.at[slot], left, sems.at[8])]
    for i, (g, r) in enumerate(((g0, r0), (g1, r1), (g3, r3), (g2a, r2))):
        r = r.at[slot] if i < 3 else r
        to = grads.at[i] if i < 3 else grads.at[3, pl.ds(0, g2a.shape[0])]
        bring.append(pltpu.make_async_copy(g, to, sems.at[2 * i]))
        bring.append(pltpu.make_async_copy(r, roots.at[i], sems.at[2 * i + 1]))
    lower = grads.at[3, pl.ds(g2a.shape[0], g2b.shape[0])]
    bring.append(pltpu.make_async_copy(g2b, lower, sems.at[9]))
    for c in bring:
        c.start()
    rows = left.shape[0]
    width = o0.shape[1]
    bring[0].wait()
    raw = None
    for i in range(4):
        bring[2 * i + 1].wait()
        if i == 3:
            bring[9].wait()
        part = dot(left[...], grads[i]).astype(BF16)
        bring[2 * i + 2].wait()
        term = dot(part, roots[i])
        raw = term if raw is None else raw + term
    raw_ref[...] = raw
    grad_own = grads[0].astype(F32)
    shape = (16, width)
    update_square = jnp.broadcast_to(jnp.sum(raw * raw, keepdims=True), shape)
    grad_square = jnp.broadcast_to(jnp.sum(grad_own * grad_own, keepdims=True), shape)
    row = lax.broadcasted_iota(jnp.int32, shape, 0)
    tile = jnp.zeros(shape, F32)
    for place, value in enumerate(three_parts(update_square) + three_parts(grad_square)):
        tile = jnp.where(row == place, value.astype(F32), tile)
    for k, out in enumerate((o0, o1, o2, o3)):
        s = lax.rem(t_ref[0] + k, 4)
        cols = pl.ds(pl.multiple_of(s * width, width), width)
        out[0:rows, :] = raw_ref[:, cols].astype(BF16)
        out[rows : rows + 16, :] = tile.astype(BF16)


def update_rows(slot, t, left_root, grads, roots):
    _, rows, full = left_root.shape
    width = grads[0].shape[1]
    out = jax.ShapeDtypeStruct((rows + 16, width), BF16)
    return pl.pallas_call(
        functools.partial(update_kernel, slot),
        out_shape=(out,) * 4,
        in_specs=[SMEM_SPEC] + [ANY_SPEC] * 10,
        out_specs=(VMEM_SPEC,) * 4,
        scratch_shapes=[
            pltpu.VMEM((rows, full), BF16),
            pltpu.VMEM((4, full, width), BF16),
            pltpu.VMEM((4, rows, full), BF16),
            pltpu.VMEM((rows, full), F32),
            pltpu.SemaphoreType.DMA((10,)),
        ],
        compiler_params=PARAMS,
        cost_estimate=cost(4 * rows * full * full, 10 * rows * full * 2),
        name="update_rows",
    )(t, left_root, *grads, *roots)


def scale_kernel(t_ref, *refs):
    slot_pieces = (refs[0:4], refs[4:8])
    out_hbm, ready, sems = refs[8:]
    _, here, _, height, width = ready.shape
    rows = here * height
    grafts = []
    for pieces in slot_pieces:
        tiles = [q[rows : rows + 16, 0:1].astype(F32) for q in pieces]

        def total(first):
            parts = [x[first : first + 1] + x[first + 1 : first + 2] + x[first + 2 : first + 3] for x in tiles]
            return parts[0] + parts[1] + parts[2] + parts[3]

        grafts.append(jnp.sqrt((total(3) + EPSILON) / (total(0) + EPSILON)))
    copies = []
    for k in range(4):
        for slot, pieces in enumerate(slot_pieces):
            scaled = pieces[k][0:rows, :].astype(F32) * grafts[slot]
            ready[k, :, slot] = scaled.astype(BF16).reshape(here, height, width)
        s = lax.rem(t_ref[0] + 4 - k, 4)
        to = out_hbm.at[pl.ds(s * here, here)]
        copies.append(pltpu.make_async_copy(ready.at[k], to, sems.at[k]))
        copies[k].start()
    for c in copies:
        c.wait()


def scale(t, first, second, shape):
    owners, slots, height, width = shape
    return pl.pallas_call(
        scale_kernel,
        out_shape=jax.ShapeDtypeStruct(shape, BF16),
        in_specs=[SMEM_SPEC] + [VMEM_SPEC] * 8,
        out_specs=ANY_SPEC,
        scratch_shapes=[
            pltpu.VMEM((4, owners // 4, slots, height, width), BF16),
            pltpu.SemaphoreType.DMA((4,)),
        ],
        compiler_params=PARAMS,
        cost_estimate=cost(0, 16 * owners * height * width),
        name="scale",
    )(t, *first, *second)


def stats_kernel(t_ref, *refs):
    slot_grads = (refs[0:3], refs[3:6])
    halves = refs[6:10]
    left_ref, right_ref, new_left_ref, new_right_ref, far, sems = refs[10:]
    t = t_ref[0]
    rows = left_ref.shape[0]
    mine = pl.ds(pl.multiple_of(t * rows, rows), rows)

    def work(slot):
        half = halves[0].shape[0]
        copies = []
        for i in range(2):
            to = far.at[slot, pl.ds(i * half, half)]
            copies.append(pltpu.make_async_copy(halves[2 * slot + i], to, sems.at[slot, i]))
        for c in copies:
            c.start()
        grads = slot_grads[slot]
        own = grads[0][...].T

        def place(k, g):
            s = lax.rem(t + 4 - k, 4)
            cols = pl.ds(pl.multiple_of(s * rows, rows), rows)
            new_right_ref[:, cols] = DECAY * right_ref[:, cols] + (1.0 - DECAY) * dot(own, g[...])

        term = None
        for k, g in zip((0, 1, 3), grads):
            part = dot(g[mine, :], g[...], 1, 1)
            term = part if term is None else term + part
            place(k, g)
        for c in copies:
            c.wait()
        term += dot(far[slot, mine, :], far[slot], 1, 1)
        place(2, far.at[slot])
        new_left_ref[...] = DECAY * left_ref[...] + (1.0 - DECAY) * term

    for slot in range(2):
        pl.when(pl.program_id(0) == slot)(lambda: work(slot))


def statistics(t, first, second, left_stat, right_stat):
    slots, rows, full = left_stat.shape
    slot_spec = pl.BlockSpec((None, rows, full), lambda i: (i, 0, 0))
    shape = jax.ShapeDtypeStruct(left_stat.shape, F32)
    return pl.pallas_call(
        stats_kernel,
        grid=(slots,),
        out_shape=(shape, shape),
        in_specs=[SMEM_SPEC] + [VMEM_SPEC] * 6 + [ANY_SPEC] * 4 + [slot_spec] * 2,
        out_specs=(slot_spec, slot_spec),
        scratch_shapes=[
            pltpu.VMEM((slots, full, first[0].shape[1]), BF16),
            pltpu.SemaphoreType.DMA((slots, 2)),
        ],
        compiler_params=PARAMS,
        cost_estimate=cost(8 * rows * full * full, 24 * rows * full),
        name="statistics",
    )(t, *first[:3], *second[:3], *first[3:], *second[3:], left_stat, right_stat)


def around(x, k):
    n = lax.axis_size("tensor")
    return lax.ppermute(x, "tensor", [(i, (i + k) % n) for i in range(n)])


def exchange(x):
    return lax.all_to_all(x, "fsdp", split_axis=0, concat_axis=0, tiled=True)


def on_device(gradient, left_stat, right_stat, left_root, right_root, block_owner):
    owners = lax.axis_size("fsdp")
    t = lax.axis_index("tensor").reshape(1)
    cols = gradient.shape[2]
    root_below, root_above = around(right_root, 1), around(right_root, -1)
    onward = pick(root_below, root_above, 0, 1, right_root.shape[1:], 2 * 10**11)
    root_far = [around(onward[0], 1), around(onward[1], -1)]
    routed = route(block_owner, gradient, owners)
    owned = exchange(routed)
    owned, root_far = lax.optimization_barrier((owned, root_far))
    own_0, own_1 = (x.reshape(-1, cols) for x in split(owned))
    grads = []
    for own in (own_0, own_1):
        below, above = around(own, 1), around(own, -1)
        grads.append((own, below, above) + opposite(below, above))
    arrived = []
    for slot in range(2):
        roots = (right_root, root_below, root_above, root_far[slot])
        pieces = update_rows(slot, t, left_root, grads[slot], roots)
        if slot == 1:
            pieces, arrived[0] = lax.optimization_barrier((pieces, arrived[0]))
        arrived.append([pieces[0]] + [around(pieces[k], k) for k in (1, 2, 3)])
    returned = exchange(scale(t, *arrived, routed.shape))
    new_left, new_right = statistics(t, *grads, left_stat, right_stat)
    return (new_left, new_right, collect(block_owner, returned))


def solution(mesh):
    return jax.shard_map(
        on_device,
        mesh=mesh,
        in_specs=(
            P(None, "fsdp", "tensor"),
            P("fsdp", "tensor", None),
            P("fsdp", "tensor", None),
            P("fsdp", "tensor", None),
            P("fsdp", "tensor", None),
            P(),
        ),
        out_specs=(P("fsdp", "tensor", None), P("fsdp", "tensor", None), P(None, "fsdp", "tensor")),
        check_vma=False,
    )
```

time: 170 us -> 151 us (0.89)
  starting transfers between devices: 72.4 us -> 53.6 us
  local copies, waits for them, and re-layouts: 12.8 us -> 9.9 us
  waiting for transfers between devices: 61.4 us -> 63.3 us
    all_to_all x4 -> x2, starting transfers between devices: 44.8 us -> 28.7 us  [exchange(): return lax.all_to_all(x, 'fsdp', split_axis=0, concat_axis=0, tiled=True)]
    squeeze x2 -> x0, local copies, waits for them, and re-layouts: 3.76 us -> none  [the longest x1 1.88 us: root_far(): root_below[slot, :half]]
    ppermute x20 -> x18, starting transfers between devices: 27.6 us -> 24.9 us  [around(): return lax.ppermute(x, 'tensor', [(i, (i + k) % n) for i in range(n)])]
    unnamed x44 -> x46, local copies, waits for them, and re-layouts: 7.51 us -> 9.9 us
    all_to_all x4 -> x2, waiting for transfers between devices: 24.1 us -> 26 us  [exchange(): return lax.all_to_all(x, 'fsdp', split_axis=0, concat_axis=0, tiled=True)]
    pallas_call x6 -> x9, Pallas kernels: 14.8 us -> 14.9 us  [the longest x2 6.94 us: update_rows(): pl.pallas_call(functools.partial(update_kernel, slot), out_shape=(out,) *...]
    ppermute x20 -> x18, waiting for transfers between devices: 37.3 us -> 37.2 us  [around(): return lax.ppermute(x, 'tensor', [(i, (i + k) % n) for i in range(n)])]
  transfers between devices with their start and end apart: 24 -> 20, of which waited for: 14 -> 12; matrix products, arithmetic and copies ran while one was open for 3% -> 0% of each run, Pallas kernels for 9% -> 12%
where the time goes in v2:
time: 151 us; the launch traced here: 150 us
  waiting for transfers between devices  63.3 us (42%)
  starting transfers between devices  53.6 us (35%)
  Pallas kernels  22.2 us (15%)
  local copies, waits for them, and re-layouts  9.9 us (7%)
    ppermute x18, waiting for transfers between devices, around(): return lax.ppermute(x, 'tensor', [(i, (i + k) % n) for i in range(n)])  37.2 us
    all_to_all x2, starting transfers between devices, exchange(): return lax.all_to_all(x, 'fsdp', split_axis=0, concat_axis=0, tiled=True)  28.7 us
    all_to_all x2, waiting for transfers between devices, exchange(): return lax.all_to_all(x, 'fsdp', split_axis=0, concat_axis=0, tiled=True)  26 us
    ppermute x18, starting transfers between devices, around(): return lax.ppermute(x, 'tensor', [(i, (i + k) % n) for i in range(n)])  24.9 us
    unnamed x46, local copies, waits for them, and re-layouts  9.9 us
    pallas_call x1, Pallas kernels, statistics(): pl.pallas_call(stats_kernel, grid=(slots,), out_shape=(shape, shape), in_...  7.31 us
    pallas_call x2, Pallas kernels, update_rows(): pl.pallas_call(functools.partial(update_kernel, slot), out_shape=(out,) *...  6.94 us
  transfers between devices with their start and end apart: 20, of which 12 were waited for; matrix products, arithmetic and copies ran while one was open for 0% of the time, Pallas kernels for 12%

profile of v2, /device:TPU:1, one launch (start us, length us, event | category | flops | bytes accessed | tf_op | source)
XLA Modules:
  0.0 150.1 jit_solution(2217398536444618920)
XLA Ops:
  0.6 2.1 %collective-permute-start = (bf16[2,256,1024]{2,1,0:T(8,128)(2,1)}, bf16[2,256,1024]{2,1,0:T(8,128)(2,1)S(1)}, u32[]{:S(2)}, u32[]{:S(2)}) collective-permute-start(bf16[2,256,1024]{2,1,0:T(8,128)(2,1)} %r0.3), channel_id=1, source_target_pairs={{0,1},{1,2},{2,3},{3,0},{4,5},{5,6},{6,7},{7,4},{8,9},{9,10},{10,1... | collective-permute-start | bytes 3145736 | tf_op jit(solution)/shard_map/ppermute | solution.py:347
  2.7 1.4 collective-permute-start.1
  4.1 1.0 copy-done.16
  5.2 0.7 copy-done.21
  5.8 2.0 %route.1 = bf16[64,2,16,256]{3,2,1,0:T(8,128)(2,1)} custom-call(s32[64]{0:T(128)S(1)} %copy-done.21, bf16[64,16,256]{2,1,0:T(8,128)(2,1)S(1)} %copy-done.16), custom_call_target="tpu_custom_call" | custom-call | bytes 786432 | tf_op jit(solution)/shard_map/route/pallas_call | solution.py:59
  7.8 13.2 %all-to-all-start = ((bf16[64,2,16,256]{3,2,1,0:T(8,128)(2,1)}), bf16[64,2,16,256]{3,2,1,0:T(8,128)(2,1)}, u32[]{:S(2)}, u32[]{:S(2)}) async-start(bf16[64,2,16,256]{3,2,1,0:T(8,128)(2,1)} %route.1), calls=%async_computation | async-start | bytes 2097152 | tf_op jit(solution)/shard_map/all_to_all | solution.py:351
  21.0 3.9 %collective-permute-done.below_hbm.r1 = bf16[2,256,1024]{2,1,0:T(8,128)(2,1)S(1)} collective-permute-done((bf16[2,256,1024]{2,1,0:T(8,128)(2,1)}, bf16[2,256,1024]{2,1,0:T(8,128)(2,1)S(1)}, u32[]{:S(2)}, u32[]{:S(2)}) %collective-permute-start) | collective-permute-done | bytes 1048608 | tf_op jit(solution)/shard_map/ppermute | solution.py:347
  24.9 1.5 collective-permute-done.1.above_hbm.r3
  26.5 0.9 copy-done.3
  27.4 1.6 %collective-permute-start.2 = (bf16[256,1024]{1,0:T(8,128)(2,1)S(1)}, bf16[256,1024]{1,0:T(8,128)(2,1)S(1)}, u32[]{:S(2)}, u32[]{:S(2)}) collective-permute-start(bf16[256,1024]{1,0:T(8,128)(2,1)S(1)} %get-tuple-element.32), channel_id=1, source_target_pairs={{0,1},{1,2},{2,3},{3,0},{4,5},{5,6},{6,7},{7,4},{8,9},{9,10},{10,1... | collective-permute-start | bytes 1572872 | tf_op jit(solution)/shard_map/ppermute | solution.py:347
  29.0 1.1 collective-permute-start.3
  30.1 9.8 %collective-permute-done.2.r2 = bf16[256,1024]{1,0:T(8,128)(2,1)S(1)} collective-permute-done((bf16[256,1024]{1,0:T(8,128)(2,1)S(1)}, bf16[256,1024]{1,0:T(8,128)(2,1)S(1)}, u32[]{:S(2)}, u32[]{:S(2)}) %collective-permute-start.2) | collective-permute-done | bytes 524320 | tf_op jit(solution)/shard_map/ppermute | solution.py:347
  39.9 0.8 copy-done.19
  40.7 0.8 copy-done.17
  41.5 7.5 %all-to-all-done.both_hbm = bf16[64,2,16,256]{3,2,1,0:T(8,128)(2,1)} async-done(((bf16[64,2,16,256]{3,2,1,0:T(8,128)(2,1)}), bf16[64,2,16,256]{3,2,1,0:T(8,128)(2,1)}, u32[]{:S(2)}, u32[]{:S(2)}) %all-to-all-start) | async-done | bytes 1048608 | tf_op jit(solution)/shard_map/all_to_all | solution.py:351
  48.9 1.2 split.1
  50.2 2.7 %collective-permute-start.5 = (bf16[1024,256]{1,0:T(8,128)(2,1)S(1)}, bf16[1024,256]{1,0:T(8,128)(2,1)S(1)}, u32[]{:S(2)}, u32[]{:S(2)}) collective-permute-start(bf16[1024,256]{1,0:T(8,128)(2,1)S(1)} %bitcast.4), channel_id=1, source_target_pairs={{0,3},{1,0},{2,1},{3,2},{4,7},{5,4},{6,5},{7,6},{8,11},{9,8},{10,9... | collective-permute-start | bytes 1572872 | tf_op jit(solution)/shard_map/ppermute | solution.py:347
  52.9 2.7 %collective-permute-start.7 = (bf16[1024,256]{1,0:T(8,128)(2,1)S(1)}, bf16[1024,256]{1,0:T(8,128)(2,1)S(1)}, u32[]{:S(2)}, u32[]{:S(2)}) collective-permute-start(bf16[1024,256]{1,0:T(8,128)(2,1)S(1)} %bitcast.8), channel_id=1, source_target_pairs={{0,3},{1,0},{2,1},{3,2},{4,7},{5,4},{6,5},{7,6},{8,11},{9,8},{10,9... | collective-permute-start | bytes 1572872 | tf_op jit(solution)/shard_map/ppermute | solution.py:347
  55.6 7.9 %collective-permute-done.4.below_hbm.refs_1_.g1 = bf16[1024,256]{1,0:T(8,128)(2,1)S(1)} collective-permute-done((bf16[1024,256]{1,0:T(8,128)(2,1)S(1)}, bf16[1024,256]{1,0:T(8,128)(2,1)S(1)}, u32[]{:S(2)}, u32[]{:S(2)}) %collective-permute-start.4) | collective-permute-done | bytes 524320 | tf_op jit(solution)/shard_map/ppermute | solution.py:347
  63.5 0.9 pick.4
  64.5 0.2 copy-done.7
  64.6 2.7 %collective-permute-start.9 = (bf16[512,256]{1,0:T(8,128)(2,1)}, bf16[512,256]{1,0:T(8,128)(2,1)}, u32[]{:S(2)}, u32[]{:S(2)}) collective-permute-start(bf16[512,256]{1,0:T(8,128)(2,1)} %get-tuple-element.38), channel_id=1, source_target_pairs={{0,3},{1,0},{2,1},{3,2},{4,7},{5,4},{6,5},{7,6},{8,11},{9,8},{10,9... | collective-permute-start | bytes 786440 | tf_op jit(solution)/shard_map/ppermute | solution.py:347
  67.3 7.4 %collective-permute-done.6.below_hbm.refs_4_.g1 = bf16[1024,256]{1,0:T(8,128)(2,1)S(1)} collective-permute-done((bf16[1024,256]{1,0:T(8,128)(2,1)S(1)}, bf16[1024,256]{1,0:T(8,128)(2,1)S(1)}, u32[]{:S(2)}, u32[]{:S(2)}) %collective-permute-start.6) | collective-permute-done | bytes 524320 | tf_op jit(solution)/shard_map/ppermute | solution.py:347
  74.7 0.9 pick.5
  75.6 0.1 copy-done.10
  75.7 0.1 copy-done.13
  75.9 2.7 %collective-permute-start.11 = (bf16[512,256]{1,0:T(8,128)(2,1)}, bf16[512,256]{1,0:T(8,128)(2,1)}, u32[]{:S(2)}, u32[]{:S(2)}) collective-permute-start(bf16[512,256]{1,0:T(8,128)(2,1)} %get-tuple-element.40), channel_id=1, source_target_pairs={{0,3},{1,0},{2,1},{3,2},{4,7},{5,4},{6,5},{7,6},{8,11},{9,8},{10,9... | collective-permute-start | bytes 786440 | tf_op jit(solution)/shard_map/ppermute | solution.py:347
  78.6 1.8 %collective-permute-done.8.refs_6_.g2a = bf16[512,256]{1,0:T(8,128)(2,1)S(1)} collective-permute-done((bf16[512,256]{1,0:T(8,128)(2,1)}, bf16[512,256]{1,0:T(8,128)(2,1)S(1)}, u32[]{:S(2)}, u32[]{:S(2)}) %collective-permute-start.8) | collective-permute-done | bytes 262176 | tf_op jit(solution)/shard_map/ppermute | solution.py:347
  80.4 1.0 copy-done.5
  81.4 1.0 copy-done.8
  82.4 1.0 copy-done.20
  83.5 3.5 %update_rows.3 = (bf16[272,256]{1,0:T(8,128)(2,1)S(1)}, bf16[272,256]{1,0:T(8,128)(2,1)S(1)}, bf16[272,256]{1,0:T(8,128)(2,1)S(1)}, bf16[272,256]{1,0:T(8,128)(2,1)S(1)}) custom-call(s32[1]{0:T(128)} %bitcast.t_ref, bf16[2,256,1024]{2,1,0:T(8,128)(2,1)S(1)} %copy-done, bf16[1024,256]{1,0:T(8,128)(2,1)S(1)} %bitcast.5, bf16[1024,256]{1,0:T(8,128)(2,1)S(1)} %copy-done.5, ...), custom_call_target="tpu_custom_call" | custom-call | flops 1073741824 | bytes 5242880 | tf_op jit(solution)/shard_map/update_rows/pallas_call | solution.py:224
  87.1 3.7 %collective-permute-start.13 = (bf16[272,256]{1,0:T(8,128)(2,1)S(1)}, bf16[272,256]{1,0:T(8,128)(2,1)S(1)}, u32[]{:S(2)}, u32[]{:S(2)}) collective-permute-start(bf16[272,256]{1,0:T(8,128)(2,1)S(1)} %get-tuple-element.51), channel_id=1, source_target_pairs={{0,2},{1,3},{2,0},{3,1},{4,6},{5,7},{6,4},{7,5},{8,10},{9,11},{10,... | collective-permute-start | bytes 417800 | tf_op jit(solution)/shard_map/ppermute | solution.py:347
  90.8 3.4 %update_rows.2 = (bf16[272,256]{1,0:T(8,128)(2,1)S(1)}, bf16[272,256]{1,0:T(8,128)(2,1)S(1)}, bf16[272,256]{1,0:T(8,128)(2,1)S(1)}, bf16[272,256]{1,0:T(8,128)(2,1)S(1)}) custom-call(s32[1]{0:T(128)} %bitcast.t_ref, bf16[2,256,1024]{2,1,0:T(8,128)(2,1)S(1)} %copy-done, bf16[1024,256]{1,0:T(8,128)(2,1)S(1)} %bitcast.9, bf16[1024,256]{1,0:T(8,128)(2,1)S(1)} %copy-done.11, ...), custom_call_target="tpu_custom_call" | custom-call | flops 1073741824 | bytes 5242880 | tf_op jit(solution)/shard_map/update_rows/pallas_call | solution.py:224
  94.3 0.4 collective-permute-done.13.refs_2_
  94.7 1.1 collective-permute-start.15
  95.8 2.0 %collective-permute-start.16 = (bf16[272,256]{1,0:T(8,128)(2,1)S(1)}, bf16[272,256]{1,0:T(8,128)(2,1)S(1)}, u32[]{:S(2)}, u32[]{:S(2)}) collective-permute-start(bf16[272,256]{1,0:T(8,128)(2,1)S(1)} %get-tuple-element.59), channel_id=1, source_target_pairs={{0,2},{1,3},{2,0},{3,1},{4,6},{5,7},{6,4},{7,5},{8,10},{9,11},{10,... | collective-permute-start | bytes 417800 | tf_op jit(solution)/shard_map/ppermute | solution.py:347
  97.9 1.1 collective-permute-start.17
  98.9 2.5 %collective-permute-done.15.refs_5_ = bf16[272,256]{1,0:T(8,128)(2,1)S(1)} collective-permute-done((bf16[272,256]{1,0:T(8,128)(2,1)S(1)}, bf16[272,256]{1,0:T(8,128)(2,1)S(1)}, u32[]{:S(2)}, u32[]{:S(2)}) %collective-permute-start.15) | collective-permute-done | bytes 139296 | tf_op jit(solution)/shard_map/ppermute | solution.py:347
  101.4 1.5 collective-permute-done.16.refs_6_
  102.9 0.5 collective-permute-done.17.refs_7_
  103.4 1.1 scale.1
  104.5 15.6 %all-to-all-start.1 = ((bf16[64,2,16,256]{3,2,1,0:T(8,128)(2,1)}), bf16[64,2,16,256]{3,2,1,0:T(8,128)(2,1)S(1)}, u32[]{:S(2)}, u32[]{:S(2)}) async-start(bf16[64,2,16,256]{3,2,1,0:T(8,128)(2,1)} %scale.1), calls=%async_computation.1 | async-start | bytes 2097152 | tf_op jit(solution)/shard_map/all_to_all | solution.py:351
  120.1 1.0 copy-done.12
  121.2 1.0 copy-done.15
  122.2 7.3 %statistics.1 = (f32[2,256,1024]{2,1,0:T(8,128)}, f32[2,256,1024]{2,1,0:T(8,128)}) custom-call(s32[1]{0:T(128)} %bitcast.t_ref, bf16[1024,256]{1,0:T(8,128)(2,1)S(1)} %bitcast.6, bf16[1024,256]{1,0:T(8,128)(2,1)S(1)} %copy-done.6, bf16[1024,256]{1,0:T(8,128)(2,1)S(1)} %copy-done.9, bf16[1024,256]{1,0:T(8,128)(2,1)S(1)} %bitcast.10, ...), custom_call_target="tpu_custom_call" | custom-call | flops 2147483648 | bytes 6291456 | tf_op jit(solution)/shard_map/statistics/pallas_call | solution.py:329
  129.5 18.6 %all-to-all-done.1.slots_hbm = bf16[64,2,16,256]{3,2,1,0:T(8,128)(2,1)S(1)} async-done(((bf16[64,2,16,256]{3,2,1,0:T(8,128)(2,1)}), bf16[64,2,16,256]{3,2,1,0:T(8,128)(2,1)S(1)}, u32[]{:S(2)}, u32[]{:S(2)}) %all-to-all-start.1) | async-done | bytes 1048608 | tf_op jit(solution)/shard_map/all_to_all | solution.py:351
  148.1 1.8 %collect.1 = bf16[64,16,256]{2,1,0:T(8,128)(2,1)} custom-call(s32[64]{0:T(128)S(1)} %copy-done.22, bf16[64,2,16,256]{3,2,1,0:T(8,128)(2,1)S(1)} %all-to-all-done.1.slots_hbm), custom_call_target="tpu_custom_call" | custom-call | bytes 1572864 | tf_op jit(solution)/shard_map/collect/pallas_call | solution.py:97
  (48 shorter events, 0.4 us)
Async XLA Ops:
  0.6 24.3 %collective-permute-start = (bf16[2,256,1024]{2,1,0:T(8,128)(2,1)}, bf16[2,256,1024]{2,1,0:T(8,128)(2,1)S(1)}, u32[]{:S(2)}, u32[]{:S(2)}) collective-permute-start(bf16[2,256,1024]{2,1,0:T(8,128)(2,1)} %r0.3), channel_id=1, source_target_pairs={{0,1},{1,2},{2,3},{3,0},{4,5},{5,6},{6,7},{7,4},{8,9},{9,10},{10,1... | collective-permute-start | bytes 3145736 | tf_op jit(solution)/shard_map/ppermute | solution.py:347
  2.7 23.7 %collective-permute-start.1 = (bf16[2,256,1024]{2,1,0:T(8,128)(2,1)}, bf16[2,256,1024]{2,1,0:T(8,128)(2,1)S(1)}, u32[]{:S(2)}, u32[]{:S(2)}) collective-permute-start(bf16[2,256,1024]{2,1,0:T(8,128)(2,1)} %r0.3), channel_id=1, source_target_pairs={{0,3},{1,0},{2,1},{3,2},{4,7},{5,4},{6,5},{7,6},{8,11},{9,8},{10,9... | collective-permute-start | bytes 3145736 | tf_op jit(solution)/shard_map/ppermute | solution.py:347
  4.1 1.0 copy-start.16
  5.2 0.7 copy-start.21
  7.8 41.1 %all-to-all-start = ((bf16[64,2,16,256]{3,2,1,0:T(8,128)(2,1)}), bf16[64,2,16,256]{3,2,1,0:T(8,128)(2,1)}, u32[]{:S(2)}, u32[]{:S(2)}) async-start(bf16[64,2,16,256]{3,2,1,0:T(8,128)(2,1)} %route.1), calls=%async_computation | async-start | bytes 2097152 | tf_op jit(solution)/shard_map/all_to_all | solution.py:351
  24.9 1.6 %copy-start.2 = (bf16[2,256,1024]{2,1,0:T(8,128)(2,1)}, bf16[2,256,1024]{2,1,0:T(8,128)(2,1)S(1)}, u32[]{:S(2)}) copy-start(bf16[2,256,1024]{2,1,0:T(8,128)(2,1)S(1)} %collective-permute-done.below_hbm.r1) | copy-start | bytes 3145732
  26.4 1.0 copy-start.3
  27.4 12.5 %collective-permute-start.2 = (bf16[256,1024]{1,0:T(8,128)(2,1)S(1)}, bf16[256,1024]{1,0:T(8,128)(2,1)S(1)}, u32[]{:S(2)}, u32[]{:S(2)}) collective-permute-start(bf16[256,1024]{1,0:T(8,128)(2,1)S(1)} %get-tuple-element.32), channel_id=1, source_target_pairs={{0,1},{1,2},{2,3},{3,0},{4,5},{5,6},{6,7},{7,4},{8,9},{9,10},{10,1... | collective-permute-start | bytes 1572872 | tf_op jit(solution)/shard_map/ppermute | solution.py:347
  29.0 11.7 %collective-permute-start.3 = (bf16[256,1024]{1,0:T(8,128)(2,1)S(1)}, bf16[256,1024]{1,0:T(8,128)(2,1)S(1)}, u32[]{:S(2)}, u32[]{:S(2)}) collective-permute-start(bf16[256,1024]{1,0:T(8,128)(2,1)S(1)} %get-tuple-element.33), channel_id=1, source_target_pairs={{0,3},{1,0},{2,1},{3,2},{4,7},{5,4},{6,5},{7,6},{8,11},{9,8},{10,9... | collective-permute-start | bytes 1572872 | tf_op jit(solution)/shard_map/ppermute | solution.py:347
  39.9 0.8 copy-start.19
  40.7 0.8 copy-start.17
  50.2 13.3 %collective-permute-start.4 = (bf16[1024,256]{1,0:T(8,128)(2,1)S(1)}, bf16[1024,256]{1,0:T(8,128)(2,1)S(1)}, u32[]{:S(2)}, u32[]{:S(2)}) collective-permute-start(bf16[1024,256]{1,0:T(8,128)(2,1)S(1)} %bitcast.3), channel_id=1, source_target_pairs={{0,1},{1,2},{2,3},{3,0},{4,5},{5,6},{6,7},{7,4},{8,9},{9,10},{10,1... | collective-permute-start | bytes 1572872 | tf_op jit(solution)/shard_map/ppermute | solution.py:347
  50.2 13.3 %collective-permute-start.5 = (bf16[1024,256]{1,0:T(8,128)(2,1)S(1)}, bf16[1024,256]{1,0:T(8,128)(2,1)S(1)}, u32[]{:S(2)}, u32[]{:S(2)}) collective-permute-start(bf16[1024,256]{1,0:T(8,128)(2,1)S(1)} %bitcast.4), channel_id=1, source_target_pairs={{0,3},{1,0},{2,1},{3,2},{4,7},{5,4},{6,5},{7,6},{8,11},{9,8},{10,9... | collective-permute-start | bytes 1572872 | tf_op jit(solution)/shard_map/ppermute | solution.py:347
  52.9 21.8 %collective-permute-start.6 = (bf16[1024,256]{1,0:T(8,128)(2,1)S(1)}, bf16[1024,256]{1,0:T(8,128)(2,1)S(1)}, u32[]{:S(2)}, u32[]{:S(2)}) collective-permute-start(bf16[1024,256]{1,0:T(8,128)(2,1)S(1)} %bitcast.7), channel_id=1, source_target_pairs={{0,1},{1,2},{2,3},{3,0},{4,5},{5,6},{6,7},{7,4},{8,9},{9,10},{10,1... | collective-permute-start | bytes 1572872 | tf_op jit(solution)/shard_map/ppermute | solution.py:347
  52.9 21.8 %collective-permute-start.7 = (bf16[1024,256]{1,0:T(8,128)(2,1)S(1)}, bf16[1024,256]{1,0:T(8,128)(2,1)S(1)}, u32[]{:S(2)}, u32[]{:S(2)}) collective-permute-start(bf16[1024,256]{1,0:T(8,128)(2,1)S(1)} %bitcast.8), channel_id=1, source_target_pairs={{0,3},{1,0},{2,1},{3,2},{4,7},{5,4},{6,5},{7,6},{8,11},{9,8},{10,9... | collective-permute-start | bytes 1572872 | tf_op jit(solution)/shard_map/ppermute | solution.py:347
  63.5 1.0 copy-start.4
  63.5 1.1 copy-start.7
  64.6 15.7 %collective-permute-start.8 = (bf16[512,256]{1,0:T(8,128)(2,1)}, bf16[512,256]{1,0:T(8,128)(2,1)S(1)}, u32[]{:S(2)}, u32[]{:S(2)}) collective-permute-start(bf16[512,256]{1,0:T(8,128)(2,1)} %get-tuple-element.37), channel_id=1, source_target_pairs={{0,1},{1,2},{2,3},{3,0},{4,5},{5,6},{6,7},{7,4},{8,9},{9,10},{10,1... | collective-permute-start | bytes 786440 | tf_op jit(solution)/shard_map/ppermute | solution.py:347
  64.6 15.7 %copy-start = (bf16[2,256,1024]{2,1,0:T(8,128)(2,1)S(1)}, bf16[2,256,1024]{2,1,0:T(8,128)(2,1)}, u32[]{:S(2)}) copy-start(bf16[2,256,1024]{2,1,0:T(8,128)(2,1)} %l_hbm.3) | copy-start | bytes 3145732
  64.6 15.7 %copy-start.1 = (bf16[2,256,1024]{2,1,0:T(8,128)(2,1)S(1)}, bf16[2,256,1024]{2,1,0:T(8,128)(2,1)}, u32[]{:S(2)}) copy-start(bf16[2,256,1024]{2,1,0:T(8,128)(2,1)} %r0.3) | copy-start | bytes 3145732
  64.6 15.7 %collective-permute-start.9 = (bf16[512,256]{1,0:T(8,128)(2,1)}, bf16[512,256]{1,0:T(8,128)(2,1)}, u32[]{:S(2)}, u32[]{:S(2)}) collective-permute-start(bf16[512,256]{1,0:T(8,128)(2,1)} %get-tuple-element.38), channel_id=1, source_target_pairs={{0,3},{1,0},{2,1},{3,2},{4,7},{5,4},{6,5},{7,6},{8,11},{9,8},{10,9... | collective-permute-start | bytes 786440 | tf_op jit(solution)/shard_map/ppermute | solution.py:347
  74.7 1.0 copy-start.10
  74.7 1.1 copy-start.13
  75.9 14.9 %collective-permute-start.10 = (bf16[512,256]{1,0:T(8,128)(2,1)}, bf16[512,256]{1,0:T(8,128)(2,1)}, u32[]{:S(2)}, u32[]{:S(2)}) collective-permute-start(bf16[512,256]{1,0:T(8,128)(2,1)} %get-tuple-element.39), channel_id=1, source_target_pairs={{0,1},{1,2},{2,3},{3,0},{4,5},{5,6},{6,7},{7,4},{8,9},{9,10},{10,1... | collective-permute-start | bytes 786440 | tf_op jit(solution)/shard_map/ppermute | solution.py:347
  75.9 14.9 %collective-permute-start.11 = (bf16[512,256]{1,0:T(8,128)(2,1)}, bf16[512,256]{1,0:T(8,128)(2,1)}, u32[]{:S(2)}, u32[]{:S(2)}) collective-permute-start(bf16[512,256]{1,0:T(8,128)(2,1)} %get-tuple-element.40), channel_id=1, source_target_pairs={{0,3},{1,0},{2,1},{3,2},{4,7},{5,4},{6,5},{7,6},{8,11},{9,8},{10,9... | collective-permute-start | bytes 786440 | tf_op jit(solution)/shard_map/ppermute | solution.py:347
  80.4 1.0 copy-start.5
  81.4 1.0 copy-start.8
  82.4 1.0 copy-start.20
  83.5 7.3 %copy-start.11 = (bf16[1024,256]{1,0:T(8,128)(2,1)S(1)}, bf16[1024,256]{1,0:T(8,128)(2,1)}, u32[]{:S(2)}) copy-start(bf16[1024,256]{1,0:T(8,128)(2,1)} %copy-done.10) | copy-start | bytes 1572868
  83.5 7.3 %copy-start.14 = (bf16[1024,256]{1,0:T(8,128)(2,1)S(1)}, bf16[1024,256]{1,0:T(8,128)(2,1)}, u32[]{:S(2)}) copy-start(bf16[1024,256]{1,0:T(8,128)(2,1)} %copy-done.13) | copy-start | bytes 1572868
  83.5 7.3 %copy-start.18 = (bf16[256,1024]{1,0:T(8,128)(2,1)S(1)}, bf16[256,1024]{1,0:T(8,128)(2,1)}, u32[]{:S(2)}) copy-start(bf16[256,1024]{1,0:T(8,128)(2,1)} %copy-done.17) | copy-start | bytes 1572868
  87.0 7.2 %collective-permute-start.12 = (bf16[272,256]{1,0:T(8,128)(2,1)S(1)}, bf16[272,256]{1,0:T(8,128)(2,1)S(1)}, u32[]{:S(2)}, u32[]{:S(2)}) collective-permute-start(bf16[272,256]{1,0:T(8,128)(2,1)S(1)} %get-tuple-element.50), channel_id=1, source_target_pairs={{0,1},{1,2},{2,3},{3,0},{4,5},{5,6},{6,7},{7,4},{8,9},{9,10},{10,1... | collective-permute-start | bytes 417800 | tf_op jit(solution)/shard_map/ppermute | solution.py:347
  87.1 7.6 %collective-permute-start.13 = (bf16[272,256]{1,0:T(8,128)(2,1)S(1)}, bf16[272,256]{1,0:T(8,128)(2,1)S(1)}, u32[]{:S(2)}, u32[]{:S(2)}) collective-permute-start(bf16[272,256]{1,0:T(8,128)(2,1)S(1)} %get-tuple-element.51), channel_id=1, source_target_pairs={{0,2},{1,3},{2,0},{3,1},{4,6},{5,7},{6,4},{7,5},{8,10},{9,11},{10,... | collective-permute-start | bytes 417800 | tf_op jit(solution)/shard_map/ppermute | solution.py:347
  90.8 3.9 %collective-permute-start.14 = (bf16[272,256]{1,0:T(8,128)(2,1)S(1)}, bf16[272,256]{1,0:T(8,128)(2,1)S(1)}, u32[]{:S(2)}, u32[]{:S(2)}) collective-permute-start(bf16[272,256]{1,0:T(8,128)(2,1)S(1)} %get-tuple-element.52), channel_id=1, source_target_pairs={{0,3},{1,0},{2,1},{3,2},{4,7},{5,4},{6,5},{7,6},{8,11},{9,8},{10,9... | collective-permute-start | bytes 417800 | tf_op jit(solution)/shard_map/ppermute | solution.py:347
  94.7 25.4 %copy-start.6 = (bf16[1024,256]{1,0:T(8,128)(2,1)S(1)}, bf16[1024,256]{1,0:T(8,128)(2,1)}, u32[]{:S(2)}) copy-start(bf16[1024,256]{1,0:T(8,128)(2,1)} %copy-done.4) | copy-start | bytes 1572868
  94.7 25.4 %copy-start.9 = (bf16[1024,256]{1,0:T(8,128)(2,1)S(1)}, bf16[1024,256]{1,0:T(8,128)(2,1)}, u32[]{:S(2)}) copy-start(bf16[1024,256]{1,0:T(8,128)(2,1)} %copy-done.7) | copy-start | bytes 1572868
  94.7 6.7 %collective-permute-start.15 = (bf16[272,256]{1,0:T(8,128)(2,1)S(1)}, bf16[272,256]{1,0:T(8,128)(2,1)S(1)}, u32[]{:S(2)}, u32[]{:S(2)}) collective-permute-start(bf16[272,256]{1,0:T(8,128)(2,1)S(1)} %get-tuple-element.58), channel_id=1, source_target_pairs={{0,1},{1,2},{2,3},{3,0},{4,5},{5,6},{6,7},{7,4},{8,9},{9,10},{10,1... | collective-permute-start | bytes 417800 | tf_op jit(solution)/shard_map/ppermute | solution.py:347
  95.8 7.0 %collective-permute-start.16 = (bf16[272,256]{1,0:T(8,128)(2,1)S(1)}, bf16[272,256]{1,0:T(8,128)(2,1)S(1)}, u32[]{:S(2)}, u32[]{:S(2)}) collective-permute-start(bf16[272,256]{1,0:T(8,128)(2,1)S(1)} %get-tuple-element.59), channel_id=1, source_target_pairs={{0,2},{1,3},{2,0},{3,1},{4,6},{5,7},{6,4},{7,5},{8,10},{9,11},{10,... | collective-permute-start | bytes 417800 | tf_op jit(solution)/shard_map/ppermute | solution.py:347
  97.9 5.5 %collective-permute-start.17 = (bf16[272,256]{1,0:T(8,128)(2,1)S(1)}, bf16[272,256]{1,0:T(8,128)(2,1)S(1)}, u32[]{:S(2)}, u32[]{:S(2)}) collective-permute-start(bf16[272,256]{1,0:T(8,128)(2,1)S(1)} %get-tuple-element.60), channel_id=1, source_target_pairs={{0,3},{1,0},{2,1},{3,2},{4,7},{5,4},{6,5},{7,6},{8,11},{9,8},{10,9... | collective-permute-start | bytes 417800 | tf_op jit(solution)/shard_map/ppermute | solution.py:347
  104.5 43.5 %all-to-all-start.1 = ((bf16[64,2,16,256]{3,2,1,0:T(8,128)(2,1)}), bf16[64,2,16,256]{3,2,1,0:T(8,128)(2,1)S(1)}, u32[]{:S(2)}, u32[]{:S(2)}) async-start(bf16[64,2,16,256]{3,2,1,0:T(8,128)(2,1)} %scale.1), calls=%async_computation.1 | async-start | bytes 2097152 | tf_op jit(solution)/shard_map/all_to_all | solution.py:351
  120.1 1.0 copy-start.12
  121.2 1.0 copy-start.15
  122.2 25.9 %copy-start.22 = (s32[64]{0:T(128)S(1)}, s32[64]{0:T(128)}, u32[]{:S(2)}) copy-start(s32[64]{0:T(128)} %owner_ref.3) | copy-start | bytes 772

commit v3 on v0

v3 whole, which is shorter than its diff:
```python
import functools

import jax
import jax.numpy as jnp
from jax import lax
from jax.experimental import pallas as pl
from jax.experimental.pallas import tpu as pltpu
from jax.sharding import PartitionSpec as P

DECAY = 0.99
EPSILON = 1e-06
BF16 = jnp.bfloat16
F32 = jnp.float32
VMEM_SPEC = pl.BlockSpec(memory_space=pltpu.VMEM)
SMEM_SPEC = pl.BlockSpec(memory_space=pltpu.SMEM)
HBM_SPEC = pl.BlockSpec(memory_space=pltpu.HBM)
PARAMS = pltpu.CompilerParams(vmem_limit_bytes=20 * 1024 * 1024)
WHOLE = pltpu.CompilerParams(vmem_limit_bytes=63 * 1024 * 1024)


def dot(a, b, ca=1, cb=0):
    return lax.dot_general(a, b, (((ca,), (cb,)), ((), ())), preferred_element_type=F32)


def cost(flops, nbytes):
    return pl.CostEstimate(flops=flops, bytes_accessed=nbytes, transcendentals=0)


def clear_counts(count_ref, owners):
    def clear(i, _):
        count_ref[i] = 0
        return 0

    lax.fori_loop(0, owners, clear, 0, unroll=8)


def route_kernel(
    t_ref, owner_hbm, grad_hbm, root_hbm, out_hbm, c1, c2, c3, grad, out, root, owner_ref, count_ref, sems
):
    bring = [
        pltpu.make_async_copy(owner_hbm, owner_ref, sems.at[0]),
        pltpu.make_async_copy(grad_hbm, grad, sems.at[1]),
        pltpu.make_async_copy(root_hbm, root, sems.at[2]),
    ]
    for c in bring:
        c.start()
    out[...] = jnp.zeros_like(out)
    clear_counts(count_ref, out.shape[0])
    bring[0].wait()
    bring[1].wait()

    def body(b, _):
        o = owner_ref[b]
        c = count_ref[o]
        count_ref[o] = c + 1
        out[o, c] = grad[b]
        return 0

    lax.fori_loop(0, grad.shape[0], body, 0, unroll=8)
    sends = [pltpu.make_async_copy(out, out_hbm, sems.at[3])]
    sends[0].start()
    bring[2].wait()
    width = c1.shape[2]
    for k, c in ((1, c1), (2, c2), (3, c3)):
        s = lax.rem(t_ref[0] + k, 4)
        cols = root.at[:, :, pl.ds(pl.multiple_of(s * width, width), width)]
        sends.append(pltpu.make_async_copy(cols, c, sems.at[3 + k]))
        sends[k].start()
    for c in sends:
        c.wait()


def route(t, block_owner, gradient, right_root, owners):
    blocks, rows, cols = gradient.shape
    shape = (owners, 2, rows, cols)
    cut = jax.ShapeDtypeStruct(right_root.shape[:2] + (cols,), right_root.dtype)
    return pl.pallas_call(
        route_kernel,
        out_shape=(jax.ShapeDtypeStruct(shape, gradient.dtype), cut, cut, cut),
        in_specs=[SMEM_SPEC] + [HBM_SPEC] * 3,
        out_specs=(HBM_SPEC,) * 4,
        scratch_shapes=[
            pltpu.VMEM(gradient.shape, gradient.dtype),
            pltpu.VMEM(shape, gradient.dtype),
            pltpu.VMEM(right_root.shape, right_root.dtype),
            pltpu.SMEM((blocks,), jnp.int32),
            pltpu.SMEM((owners,), jnp.int32),
            pltpu.SemaphoreType.DMA((7,)),
        ],
        compiler_params=WHOLE,
        cost_estimate=cost(0, 3 * gradient.size),
        name="route",
    )(t, block_owner, gradient, right_root)


def collect_kernel(owner_hbm, slots_hbm, out_hbm, slots, out, owner_ref, count_ref, sems):
    bring = [
        pltpu.make_async_copy(owner_hbm, owner_ref, sems.at[0]),
        pltpu.make_async_copy(slots_hbm, slots, sems.at[1]),
    ]
    for c in bring:
        c.start()
    clear_counts(count_ref, slots.shape[0])
    for c in bring:
        c.wait()

    def body(b, _):
        o = owner_ref[b]
        c = count_ref[o]
        count_ref[o] = c + 1
        out[b] = slots[o, c]
        return 0

    lax.fori_loop(0, out.shape[0], body, 0, unroll=8)
    send = pltpu.make_async_copy(out, out_hbm, sems.at[2])
    send.start()
    send.wait()


def collect(block_owner, slots):
    blocks = block_owner.shape[0]
    shape = (blocks,) + slots.shape[2:]
    return pl.pallas_call(
        collect_kernel,
        out_shape=jax.ShapeDtypeStruct(shape, slots.dtype),
        in_specs=[HBM_SPEC] * 2,
        out_specs=HBM_SPEC,
        scratch_shapes=[
            pltpu.VMEM(slots.shape, slots.dtype),
            pltpu.VMEM(shape, slots.dtype),
            pltpu.SMEM((blocks,), jnp.int32),
            pltpu.SMEM((slots.shape[0],), jnp.int32),
            pltpu.SemaphoreType.DMA((3,)),
        ],
        compiler_params=PARAMS,
        cost_estimate=cost(0, 3 * slots.size),
        name="collect",
    )(block_owner, slots)


def through(brings, sends):
    for c in brings:
        c.start()
    for bring, send in zip(brings, sends):
        bring.wait()
        send.start()
    for c in sends:
        c.wait()


def pick_kernel(first, second, below_hbm, above_hbm, first_hbm, second_hbm, held, sems):
    brings = [
        pltpu.make_async_copy(below_hbm.at[first], held.at[0], sems.at[0]),
        pltpu.make_async_copy(above_hbm.at[second], held.at[1], sems.at[1]),
    ]
    sends = [
        pltpu.make_async_copy(held.at[i], out, sems.at[2 + i])
        for i, out in enumerate((first_hbm, second_hbm))
    ]
    through(brings, sends)


def pick(below, above, first, second, shape, flops, params):
    out = jax.ShapeDtypeStruct(shape, below.dtype)
    return pl.pallas_call(
        functools.partial(pick_kernel, first, second),
        out_shape=(out, out),
        in_specs=[HBM_SPEC] * 2,
        out_specs=(HBM_SPEC, HBM_SPEC),
        scratch_shapes=[pltpu.VMEM((2,) + shape, below.dtype), pltpu.SemaphoreType.DMA((4,))],
        compiler_params=params,
        cost_estimate=cost(flops, 4 * below.size),
        name="pick",
    )(below, above)


def bring_left(slot, own, below, above, far, to, sems):
    rows = far.shape[0]
    pieces = (own.at[slot], below.at[slot], above.at[slot], far)
    return [
        pltpu.make_async_copy(x, to.at[pl.ds(i * rows, rows)], sems.at[i])
        for i, x in enumerate(pieces)
    ]


def own_kernel(t_ref, l0, l1, l3, l2_0, l2_1, g0, r0, raw_ref, square_ref, left, grads, roots, sems):
    slots, full, _ = left.shape
    width = grads.shape[3]
    mine = pl.ds(pl.multiple_of(t_ref[0] * width, width), width)
    groups = []
    for slot, far in enumerate((l2_0, l2_1)):
        bring = bring_left(slot, l0, l1, l3, far, left.at[slot], sems.at[slot])
        bring.append(pltpu.make_async_copy(g0.at[:, slot], grads.at[slot], sems.at[slot, 4]))
        bring.append(pltpu.make_async_copy(r0.at[slot, :, mine], roots.at[slot], sems.at[slot, 5]))
        groups.append(bring)
    for bring in groups:
        for c in bring:
            c.start()
    for slot, bring in enumerate(groups):
        for c in bring:
            c.wait()
        grad = grads[slot].reshape(full, width)
        raw_ref[slot] = dot(dot(left[slot], grad).astype(BF16), roots[slot])
        wide = grad.astype(F32)
        square_ref[slot] = jnp.broadcast_to(jnp.sum(wide * wide, keepdims=True), square_ref.shape[1:])


def own_part(t, lefts, lefts_far, owned, right_root):
    owners, slots, height, width = owned.shape
    full = owners * height
    return pl.pallas_call(
        own_kernel,
        out_shape=(
            jax.ShapeDtypeStruct((slots, full, width), F32),
            jax.ShapeDtypeStruct((slots, 8, 128), F32),
            jax.ShapeDtypeStruct((slots, full, full), BF16),
        ),
        in_specs=[SMEM_SPEC] + [HBM_SPEC] * 7,
        out_specs=(VMEM_SPEC,) * 3,
        scratch_shapes=[
            pltpu.VMEM((slots, owners, height, width), BF16),
            pltpu.VMEM((slots, width, width), BF16),
            pltpu.SemaphoreType.DMA((slots, 6)),
        ],
        compiler_params=PARAMS,
        cost_estimate=cost(4 * full * full * width, 12 * full * full),
        name="own_part",
    )(t, *lefts, *lefts_far, owned, right_root)


def near_kernel(own, left, g1, g3, r1, r3, raw_ref, grads, roots, sems):
    slots, full, _ = left.shape
    width = grads.shape[4]
    groups = []
    for slot in range(slots):
        bring = []
        for i, (g, r) in enumerate(((g1, r1), (g3, r3))):
            bring.append(pltpu.make_async_copy(g.at[:, slot], grads.at[slot, i], sems.at[slot, 2 * i]))
            bring.append(pltpu.make_async_copy(r.at[slot], roots.at[slot, i], sems.at[slot, 2 * i + 1]))
        groups.append(bring)
    for bring in groups:
        for c in bring:
            c.start()
    for slot, bring in enumerate(groups):
        raw = own[slot]
        for i in range(2):
            bring[2 * i].wait()
            bring[2 * i + 1].wait()
            part = dot(left[slot], grads[slot, i].reshape(full, width)).astype(BF16)
            raw = raw + dot(part, roots[slot, i])
        raw_ref[slot] = raw


def near_part(own, left, below, above, root_below, root_above):
    owners, slots, height, width = below.shape
    return pl.pallas_call(
        near_kernel,
        out_shape=jax.ShapeDtypeStruct(own.shape, F32),
        in_specs=[VMEM_SPEC] * 2 + [HBM_SPEC] * 4,
        out_specs=VMEM_SPEC,
        scratch_shapes=[
            pltpu.VMEM((slots, 2, owners, height, width), BF16),
            pltpu.VMEM((slots, 2, width, width), BF16),
            pltpu.SemaphoreType.DMA((slots, 4)),
        ],
        compiler_params=PARAMS,
        cost_estimate=cost(8 * own.shape[1] ** 2 * width, 12 * own.shape[1] ** 2),
        name="near_part",
    )(own, left, below, above, root_below, root_above)


def far_kernel(near, square, left, ga, gb, r2, raw_ref, sums_ref):
    row = lax.broadcasted_iota(jnp.int32, sums_ref.shape, 0)
    sums = jnp.zeros(sums_ref.shape, F32)
    half = left.shape[1] // 2
    width = near.shape[2]
    for slot in range(near.shape[0]):
        part = dot(left[slot, :, :half], ga[:, slot].reshape(half, width))
        part += dot(left[slot, :, half:], gb[:, slot].reshape(half, width))
        total = near[slot] + dot(part.astype(BF16), r2[slot])
        raw_ref[slot] = total
        sums = jnp.where(row == slot, jnp.sum(total * total, keepdims=True), sums)
        sums = jnp.where(row == 2 + slot, square[slot], sums)
    sums_ref[...] = sums


def far_part(near, square, left, halves, root_far):
    slots, full, width = near.shape
    return pl.pallas_call(
        far_kernel,
        out_shape=(
            jax.ShapeDtypeStruct(near.shape, F32),
            jax.ShapeDtypeStruct((8, 128), F32),
        ),
        in_specs=[VMEM_SPEC] * 6,
        out_specs=(VMEM_SPEC, VMEM_SPEC),
        compiler_params=PARAMS,
        cost_estimate=cost(4 * full * full * width, 8 * full * full),
        name="far_part",
    )(near, square, left, *halves, root_far)


def scale_kernel(t_ref, raw, s0, s1, s2, s3, out_hbm, ready, sems):
    _, here, slots, height, width = ready.shape
    rows = here * height
    sums = s0[...] + s1[...] + s2[...] + s3[...]
    grafts = [
        jnp.sqrt((sums[2 + slot : 3 + slot, 0:1] + EPSILON) / (sums[slot : slot + 1, 0:1] + EPSILON))
        for slot in range(slots)
    ]
    copies = []
    for i, k in enumerate((0, 1, 3, 2)):
        for slot in range(slots):
            scaled = raw[slot, i * rows : (i + 1) * rows, :] * grafts[slot]
            ready[i, :, slot] = scaled.astype(BF16).reshape(here, height, width)
        s = lax.rem(t_ref[0] + 4 - k, 4)
        to = out_hbm.at[pl.ds(s * here, here)]
        copies.append(pltpu.make_async_copy(ready.at[i], to, sems.at[i]))
        copies[i].start()
    for c in copies:
        c.wait()


def scale(t, raw, sums, shape):
    owners, slots, height, width = shape
    return pl.pallas_call(
        scale_kernel,
        out_shape=jax.ShapeDtypeStruct(shape, BF16),
        in_specs=[SMEM_SPEC] + [VMEM_SPEC] * 5,
        out_specs=HBM_SPEC,
        scratch_shapes=[
            pltpu.VMEM((4, owners // 4, slots, height, width), BF16),
            pltpu.SemaphoreType.DMA((4,)),
        ],
        compiler_params=PARAMS,
        cost_estimate=cost(0, 16 * owners * height * width),
        name="scale",
    )(t, raw, *sums)


def stats_kernel(
    t_ref, g0, g1, g3, ga, gb, left_ref, right_ref, new_left_ref, new_right_ref, far, sems
):
    t = t_ref[0]
    rows, full = left_ref.shape
    here = g0.shape[0] // 4
    half = ga.shape[0]
    mine = pl.ds(pl.multiple_of(t * here, here), here)

    def work(slot):
        copies = []
        for i, g in enumerate((ga, gb)):
            to = far.at[slot, pl.ds(i * half, half)]
            copies.append(pltpu.make_async_copy(g.at[:, slot], to, sems.at[slot, i]))
            copies[i].start()

        def place(k, g):
            s = lax.rem(t + 4 - k, 4)
            cols = pl.ds(pl.multiple_of(s * rows, rows), rows)
            new_right_ref[:, cols] = DECAY * right_ref[:, cols] + (1.0 - DECAY) * dot(own, g)

        own = g0[:, slot].reshape(full, rows).T
        term = None
        for k, g in ((0, g0), (1, g1), (3, g3)):
            whole = g[:, slot].reshape(full, rows)
            part = dot(g[mine, slot].reshape(rows, rows), whole, 1, 1)
            term = part if term is None else term + part
            place(k, whole)
        for c in copies:
            c.wait()
        whole = far[slot].reshape(full, rows)
        term += dot(far[slot, mine].reshape(rows, rows), whole, 1, 1)
        place(2, whole)
        new_left_ref[...] = DECAY * left_ref[...] + (1.0 - DECAY) * term

    for slot in range(2):
        pl.when(pl.program_id(0) == slot)(functools.partial(work, slot))


def statistics(t, grads, halves, left_stat, right_stat):
    slots, rows, full = left_stat.shape
    slot_spec = pl.BlockSpec((None, rows, full), lambda i: (i, 0, 0))
    shape = jax.ShapeDtypeStruct(left_stat.shape, F32)
    owners, _, height, width = grads[0].shape
    return pl.pallas_call(
        stats_kernel,
        grid=(slots,),
        out_shape=(shape, shape),
        in_specs=[SMEM_SPEC] + [VMEM_SPEC] * 3 + [HBM_SPEC] * 2 + [slot_spec] * 2,
        out_specs=(slot_spec, slot_spec),
        scratch_shapes=[
            pltpu.VMEM((slots, owners, height, width), BF16),
            pltpu.SemaphoreType.DMA((slots, 2)),
        ],
        compiler_params=pltpu.CompilerParams(vmem_limit_bytes=32 * 1024 * 1024),
        cost_estimate=cost(8 * rows * full * full, 24 * rows * full),
        name="statistics",
    )(t, *grads, *halves, left_stat, right_stat)


def around(x, k):
    n = lax.axis_size("tensor")
    return lax.ppermute(x, "tensor", [(i, (i + k) % n) for i in range(n)])


def exchange(x):
    return lax.all_to_all(x, "fsdp", split_axis=0, concat_axis=0, tiled=True)


def on_device(gradient, left_stat, right_stat, left_root, right_root, block_owner):
    owners = lax.axis_size("fsdp")
    t = lax.axis_index("tensor").reshape(1)
    left_below, left_above = around(left_root, 1), around(left_root, -1)
    routed, *cuts = route(t, block_owner, gradient, right_root, owners)
    roots = [around(c, k) for c, k in zip(cuts, (1, 2, 3))]
    onward = pick(left_below, left_above, 0, 1, left_root.shape[1:], 2 * 10**11, WHOLE)
    root_below, root_far, root_above = roots
    onward, root_below, root_above = lax.optimization_barrier((onward, root_below, root_above))
    left_far = [around(onward[0], 1), around(onward[1], -1)]
    owned = exchange(routed)
    owned, left_far, root_far = lax.optimization_barrier((owned, left_far, root_far))
    below, above = around(owned, 1), around(owned, -1)
    lefts = (left_root, left_below, left_above)
    raw, square, left = own_part(t, lefts, left_far, owned, right_root)
    below, above, raw = lax.optimization_barrier((below, above, raw))
    half = owners // 2
    shape = (half,) + owned.shape[1:]
    upper, lower = pick(below, above, pl.ds(0, half), pl.ds(half, half), shape, 3 * 10**10, PARAMS)
    halves = around(upper, 1), around(lower, -1)
    grads = (owned, below, above)
    raw = near_part(raw, left, below, above, root_below, root_above)
    raw, sums = far_part(raw, square, left, halves, root_far)
    returned = exchange(scale(t, raw, [sums] + [around(sums, k) for k in (1, 2, 3)], routed.shape))
    new_left, new_right = statistics(t, grads, halves, left_stat, right_stat)
    return (new_left, new_right, collect(block_owner, returned))


def solution(mesh):
    return jax.shard_map(
        on_device,
        mesh=mesh,
        in_specs=(
            P(None, "fsdp", "tensor"),
            P("fsdp", "tensor", None),
            P("fsdp", "tensor", None),
            P("fsdp", "tensor", None),
            P("fsdp", "tensor", None),
            P(),
        ),
        out_specs=(P("fsdp", "tensor", None), P("fsdp", "tensor", None), P(None, "fsdp", "tensor")),
        check_vma=False,
    )
```

time: 258 us -> 146 us (0.57)
  waiting for transfers between devices: 154 us -> 58 us
  starting transfers between devices: 23.7 us -> 51.4 us
  Pallas kernels: 0 us -> 26.8 us
  blocking collectives: 20.9 us -> 0 us
  matrix products: 16.2 us -> 0 us
  local copies, waits for them, and re-layouts: 21.5 us -> 7.72 us
  between operations: 14.1 us -> 0.92 us
  other arithmetic: 6.87 us -> 0 us
    all_to_all x2, waiting for transfers between devices: 113 us -> 18 us  [exchange(): return lax.all_to_all(x, 'fsdp', split_axis=0, concat_axis=0, tiled=True)]
    all_gather x2 -> x0, waiting for transfers between devices: 40.3 us -> none  [the longest x1 40.3 us: on_device(): wide_rows = lax.all_gather(gradient, 'tensor', axis=2, tiled=True)]
    ppermute x0 -> x14, waiting for transfers between devices: none -> 40 us  [around(): return lax.ppermute(x, 'tensor', [(i, (i + k) % n) for i in range(n)])]
    pallas_call x0 -> x9, Pallas kernels: none -> 26.8 us  [the longest x1 6.71 us: near_part(): pl.pallas_call(near_kernel, out_shape=jax.ShapeDtypeStruct(own.shape, F32...]
    ppermute x0 -> x14, starting transfers between devices: none -> 18.2 us  [around(): return lax.ppermute(x, 'tensor', [(i, (i + k) % n) for i in range(n)])]
    dot_general x3 -> x0, matrix products: 16.2 us -> none  [the longest x1 7.31 us: on_device(): jnp.einsum('sik,skj->sij', left_part, lax.all_gather(right_root, 'tensor'...]
    all_to_all x1 -> x0, blocking collectives: 13.1 us -> none  [on_device(): lax.all_to_all(grafted, 'tensor', split_axis=2, concat_axis=1, tiled=True)]
    all_to_all x2, starting transfers between devices: 23.7 us -> 33.3 us  [exchange(): return lax.all_to_all(x, 'fsdp', split_axis=0, concat_axis=0, tiled=True)]
  transfers between devices with their start and end apart: 4 -> 16, of which waited for: 3 -> 13; matrix products, arithmetic and copies ran while one was open for 7% -> 0% of each run, Pallas kernels for 0% -> 15%
where the time goes in v3:
time: 146 us; the launch traced here: 145 us
  waiting for transfers between devices  58 us (40%)
  starting transfers between devices  51.4 us (35%)
  Pallas kernels  26.8 us (18%)
  local copies, waits for them, and re-layouts  7.72 us (5%)
    ppermute x14, waiting for transfers between devices, around(): return lax.ppermute(x, 'tensor', [(i, (i + k) % n) for i in range(n)])  40 us
    all_to_all x2, starting transfers between devices, exchange(): return lax.all_to_all(x, 'fsdp', split_axis=0, concat_axis=0, tiled=True)  33.3 us
    ppermute x14, starting transfers between devices, around(): return lax.ppermute(x, 'tensor', [(i, (i + k) % n) for i in range(n)])  18.2 us
    all_to_all x2, waiting for transfers between devices, exchange(): return lax.all_to_all(x, 'fsdp', split_axis=0, concat_axis=0, tiled=True)  18 us
    unnamed x18, local copies, waits for them, and re-layouts  7.72 us
    pallas_call x1, Pallas kernels, near_part(): pl.pallas_call(near_kernel, out_shape=jax.ShapeDtypeStruct(own.shape, F32...  6.71 us
    pallas_call x1, Pallas kernels, statistics(): pl.pallas_call(stats_kernel, grid=(slots,), out_shape=(shape, shape), in_...  5.62 us
    pallas_call x1, Pallas kernels, own_part(): pl.pallas_call(own_kernel, out_shape=(jax.ShapeDtypeStruct((slots, full,...  4.22 us
  transfers between devices with their start and end apart: 16, of which 13 were waited for; matrix products, arithmetic and copies ran while one was open for 0% of the time, Pallas kernels for 15%

profile of v3, /device:TPU:1, one launch (start us, length us, event | category | flops | bytes accessed | tf_op | source)
XLA Modules:
  0.0 144.9 jit_solution(4078059527654598515)
XLA Ops:
  0.6 2.1 %collective-permute-start = (bf16[2,256,1024]{2,1,0:T(8,128)(2,1)}, bf16[2,256,1024]{2,1,0:T(8,128)(2,1)}, u32[]{:S(2)}, u32[]{:S(2)}) collective-permute-start(bf16[2,256,1024]{2,1,0:T(8,128)(2,1)} %l0.1), channel_id=1, source_target_pairs={{0,1},{1,2},{2,3},{3,0},{4,5},{5,6},{6,7},{7,4},{8,9},{9,10},{10,1... | collective-permute-start | bytes 3145736 | tf_op jit(solution)/shard_map/ppermute | solution.py:403
  2.7 1.4 collective-permute-start.1
  4.1 2.6 %route.1 = (bf16[64,2,16,256]{3,2,1,0:T(8,128)(2,1)}, bf16[2,256,256]{2,1,0:T(8,128)(2,1)}, bf16[2,256,256]{2,1,0:T(8,128)(2,1)}, bf16[2,256,256]{2,1,0:T(8,128)(2,1)}) custom-call(s32[1]{0:T(128)} %bitcast.t_ref, s32[64]{0:T(128)} %owner_hbm.3, bf16[64,16,256]{2,1,0:T(8,128)(2,1)} %grad_hbm.1, bf16[2,256,1024]{2,1,0:T(8,128)(2,1)} %r0.1), custom_call_target="tpu_custom_call" | custom-call | bytes 786432 | tf_op jit(solution)/shard_map/route/pallas_call | solution.py:77
  6.7 0.2 collective-permute-start.2
  6.9 2.6 %collective-permute-start.3 = (bf16[2,256,256]{2,1,0:T(8,128)(2,1)}, bf16[2,256,256]{2,1,0:T(8,128)(2,1)}, u32[]{:S(2)}, u32[]{:S(2)}) collective-permute-start(bf16[2,256,256]{2,1,0:T(8,128)(2,1)} %get-tuple-element.33), channel_id=1, source_target_pairs={{0,3},{1,0},{2,1},{3,2},{4,7},{5,4},{6,5},{7,6},{8,11},{9,8},{10,9... | collective-permute-start | bytes 786440 | tf_op jit(solution)/shard_map/ppermute | solution.py:403
  9.5 13.7 %all-to-all-start = ((bf16[64,2,16,256]{3,2,1,0:T(8,128)(2,1)}), bf16[64,2,16,256]{3,2,1,0:T(8,128)(2,1)}, u32[]{:S(2)}, u32[]{:S(2)}) async-start(bf16[64,2,16,256]{3,2,1,0:T(8,128)(2,1)} %get-tuple-element.29), calls=%async_computation | async-start | bytes 2097152 | tf_op jit(solution)/shard_map/all_to_all | solution.py:407
  23.2 1.7 %collective-permute-done.below_hbm.l1 = bf16[2,256,1024]{2,1,0:T(8,128)(2,1)} collective-permute-done((bf16[2,256,1024]{2,1,0:T(8,128)(2,1)}, bf16[2,256,1024]{2,1,0:T(8,128)(2,1)}, u32[]{:S(2)}, u32[]{:S(2)}) %collective-permute-start) | collective-permute-done | bytes 1048608 | tf_op jit(solution)/shard_map/ppermute | solution.py:403
  24.9 1.5 %collective-permute-done.1.above_hbm.l3 = bf16[2,256,1024]{2,1,0:T(8,128)(2,1)} collective-permute-done((bf16[2,256,1024]{2,1,0:T(8,128)(2,1)}, bf16[2,256,1024]{2,1,0:T(8,128)(2,1)}, u32[]{:S(2)}, u32[]{:S(2)}) %collective-permute-start.1) | collective-permute-done | bytes 1048608 | tf_op jit(solution)/shard_map/ppermute | solution.py:403
  26.4 2.0 %pick.2 = (bf16[256,1024]{1,0:T(8,128)(2,1)}, bf16[256,1024]{1,0:T(8,128)(2,1)}) custom-call(bf16[2,256,1024]{2,1,0:T(8,128)(2,1)} %collective-permute-done.below_hbm.l1, bf16[2,256,1024]{2,1,0:T(8,128)(2,1)} %collective-permute-done.1.above_hbm.l3), custom_call_target="tpu_custom_call" | custom-call | flops 199999995904 | bytes 2097152 | tf_op jit(solution)/shard_map/pick/pallas_call | solution.py:165
  28.5 2.1 %collective-permute-done.2.r1 = bf16[2,256,256]{2,1,0:T(8,128)(2,1)} collective-permute-done((bf16[2,256,256]{2,1,0:T(8,128)(2,1)}, bf16[2,256,256]{2,1,0:T(8,128)(2,1)}, u32[]{:S(2)}, u32[]{:S(2)}) %collective-permute-start.2) | collective-permute-done | bytes 262176 | tf_op jit(solution)/shard_map/ppermute | solution.py:403
  30.5 1.5 %collective-permute-done.3.r3 = bf16[2,256,256]{2,1,0:T(8,128)(2,1)} collective-permute-done((bf16[2,256,256]{2,1,0:T(8,128)(2,1)}, bf16[2,256,256]{2,1,0:T(8,128)(2,1)}, u32[]{:S(2)}, u32[]{:S(2)}) %collective-permute-start.3) | collective-permute-done | bytes 262176 | tf_op jit(solution)/shard_map/ppermute | solution.py:403
  32.0 1.6 %collective-permute-start.4 = (bf16[256,1024]{1,0:T(8,128)(2,1)}, bf16[256,1024]{1,0:T(8,128)(2,1)S(1)}, u32[]{:S(2)}, u32[]{:S(2)}) collective-permute-start(bf16[256,1024]{1,0:T(8,128)(2,1)} %get-tuple-element.34), channel_id=1, source_target_pairs={{0,1},{1,2},{2,3},{3,0},{4,5},{5,6},{6,7},{7,4},{8,9},{9,10},{10,1... | collective-permute-start | bytes 1572872 | tf_op jit(solution)/shard_map/ppermute | solution.py:403
  33.6 1.1 collective-permute-start.5
  34.7 1.4 collective-permute-start.6
  36.1 14.1 %collective-permute-done.6.r2 = bf16[2,256,256]{2,1,0:T(8,128)(2,1)S(1)} collective-permute-done((bf16[2,256,256]{2,1,0:T(8,128)(2,1)}, bf16[2,256,256]{2,1,0:T(8,128)(2,1)S(1)}, u32[]{:S(2)}, u32[]{:S(2)}) %collective-permute-start.6) | collective-permute-done | bytes 262176 | tf_op jit(solution)/shard_map/ppermute | solution.py:403
  50.2 0.0 collective-permute-done.4.l2_0
  50.2 0.0 collective-permute-done.5.l2_1
  50.2 0.9 all-to-all-done.g0
  51.1 0.0 collective-permute-start.7
  51.1 2.7 %collective-permute-start.8 = (bf16[64,2,16,256]{3,2,1,0:T(8,128)(2,1)}, bf16[64,2,16,256]{3,2,1,0:T(8,128)(2,1)S(1)}, u32[]{:S(2)}, u32[]{:S(2)}) collective-permute-start(bf16[64,2,16,256]{3,2,1,0:T(8,128)(2,1)} %all-to-all-done.g0), channel_id=1, source_target_pairs={{0,3},{1,0},{2,1},{3,2},{4,7},{5,4},{6,5},{7,6},{8,11},{9,8},{10,9... | collective-permute-start | bytes 3145736 | tf_op jit(solution)/shard_map/ppermute | solution.py:403
  53.8 1.2 copy-done
  55.0 1.2 copy-done.7
  56.2 4.2 %own_part.1 = (f32[2,1024,256]{2,1,0:T(8,128)S(1)}, f32[2,8,128]{2,1,0:T(8,128)S(1)}, bf16[2,1024,1024]{2,1,0:T(8,128)(2,1)S(1)}) custom-call(s32[1]{0:T(128)} %bitcast.t_ref, bf16[2,256,1024]{2,1,0:T(8,128)(2,1)S(1)} %copy-done.7, bf16[2,256,1024]{2,1,0:T(8,128)(2,1)} %collective-permute-done.below_hbm.l1, ...), custom_call_target="tpu_custom_call" | custom-call | flops 1073741824 | bytes 12582912 | tf_op jit(solution)/shard_map/own_part/pallas_call | solution.py:211
  60.5 13.9 %collective-permute-done.7.below_hbm.g1 = bf16[64,2,16,256]{3,2,1,0:T(8,128)(2,1)S(1)} collective-permute-done((bf16[64,2,16,256]{3,2,1,0:T(8,128)(2,1)}, bf16[64,2,16,256]{3,2,1,0:T(8,128)(2,1)S(1)}, u32[]{:S(2)}, u32[]{:S(2)}) %collective-permute-start.7) | collective-permute-done | bytes 1048608 | tf_op jit(solution)/shard_map/ppermute | solution.py:403
  74.4 0.0 collective-permute-done.8.above_hbm.g3
  74.4 0.2 pick.3
  74.6 2.5 %collective-permute-start.10 = (bf16[32,2,16,256]{3,2,1,0:T(8,128)(2,1)S(1)}, bf16[32,2,16,256]{3,2,1,0:T(8,128)(2,1)S(1)}, u32[]{:S(2)}, u32[]{:S(2)}) collective-permute-start(bf16[32,2,16,256]{3,2,1,0:T(8,128)(2,1)S(1)} %get-tuple-element.44), channel_id=1, source_target_pairs={{0,3},{1,0},{2,1},{3,2},{4,7},{5,4},{6,5},{7,6},{8,11},{9,8},{10,9... | collective-permute-start | bytes 1572872 | tf_op jit(solution)/shard_map/ppermute | solution.py:403
  77.0 0.0 collective-permute-start.9
  77.0 6.7 %near_part.1.near = f32[2,1024,256]{2,1,0:T(8,128)S(1)} custom-call(f32[2,1024,256]{2,1,0:T(8,128)S(1)} %get-tuple-element.47.own, bf16[2,1024,1024]{2,1,0:T(8,128)(2,1)S(1)} %get-tuple-element.48.left, bf16[64,2,16,256]{3,2,1,0:T(8,128)(2,1)S(1)} %collective-permute-done.7.below_hbm.g1, bf16[64,2,16,256]{3,2,1,0:T(8,128)(2,1)S(1)} %collective-permute-done.8.above_hbm.g3, ...), custom_call_target="tpu_custom_call" | custom-call | flops 2147483648 | bytes 12582912 | tf_op jit(solution)/shard_map/near_part/pallas_call | solution.py:256
  83.7 0.5 collective-permute-done.10.gb
  84.3 3.0 %collective-permute-done.9.ga = bf16[32,2,16,256]{3,2,1,0:T(8,128)(2,1)S(1)} collective-permute-done((bf16[32,2,16,256]{3,2,1,0:T(8,128)(2,1)S(1)}, bf16[32,2,16,256]{3,2,1,0:T(8,128)(2,1)S(1)}, u32[]{:S(2)}, u32[]{:S(2)}) %collective-permute-start.9) | collective-permute-done | bytes 524320 | tf_op jit(solution)/shard_map/ppermute | solution.py:403
  87.3 2.7 %far_part.1 = (f32[2,1024,256]{2,1,0:T(8,128)S(1)}, f32[8,128]{1,0:T(8,128)S(1)}) custom-call(f32[2,1024,256]{2,1,0:T(8,128)S(1)} %near_part.1.near, f32[2,8,128]{2,1,0:T(8,128)S(1)} %get-tuple-element.51.square, bf16[2,1024,1024]{2,1,0:T(8,128)(2,1)S(1)} %get-tuple-element.48.left, bf16[32,2,16,256]{3,2,1,0:T(8,128)(2,1)S(1)} %collective-permute-done.9.ga, ...), custom_call_target="tpu_custom_call" | custom-call | flops 1073741824 | bytes 8388608 | tf_op jit(solution)/shard_map/far_part/pallas_call | solution.py:289
  90.1 0.1 collective-permute-start.11
  90.2 1.5 %collective-permute-start.12 = (f32[8,128]{1,0:T(8,128)S(1)}, f32[8,128]{1,0:T(8,128)S(1)}, u32[]{:S(2)}, u32[]{:S(2)}) collective-permute-start(f32[8,128]{1,0:T(8,128)S(1)} %get-tuple-element.54.s0), channel_id=1, source_target_pairs={{0,2},{1,3},{2,0},{3,1},{4,6},{5,7},{6,4},{7,5},{8,10},{9,11},{10,... | collective-permute-start | bytes 12296 | tf_op jit(solution)/shard_map/ppermute | solution.py:403
  91.6 1.2 collective-permute-start.13
  92.8 1.0 collective-permute-done.11.s1
  93.8 0.4 collective-permute-done.12.s2
  94.2 0.2 collective-permute-done.13.s3
  94.4 1.1 scale.1
  95.5 19.5 %all-to-all-start.1 = ((bf16[64,2,16,256]{3,2,1,0:T(8,128)(2,1)}), bf16[64,2,16,256]{3,2,1,0:T(8,128)(2,1)S(1)}, u32[]{:S(2)}, u32[]{:S(2)}) async-start(bf16[64,2,16,256]{3,2,1,0:T(8,128)(2,1)} %scale.1), calls=%async_computation.1 | async-start | bytes 2097152 | tf_op jit(solution)/shard_map/all_to_all | solution.py:407
  115.1 0.0 copy-start.2
  115.1 1.0 copy-done.2
  116.1 1.0 copy-done.4
  117.2 1.6 %copy-done.5 = f32[2,256,1024]{2,1,0:T(8,128)S(1)} copy-done((f32[2,256,1024]{2,1,0:T(8,128)S(1)}, f32[2,256,1024]{2,1,0:T(8,128)}, u32[]{:S(2)}) %copy-start.5) | copy-done | bytes 2097176
  118.7 1.6 %copy-done.6 = f32[2,256,1024]{2,1,0:T(8,128)S(1)} copy-done((f32[2,256,1024]{2,1,0:T(8,128)S(1)}, f32[2,256,1024]{2,1,0:T(8,128)}, u32[]{:S(2)}) %copy-start.6) | copy-done | bytes 2097176
  120.3 5.6 %statistics.1 = (f32[2,256,1024]{2,1,0:T(8,128)}, f32[2,256,1024]{2,1,0:T(8,128)}) custom-call(s32[1]{0:T(128)} %bitcast.t_ref, bf16[64,2,16,256]{3,2,1,0:T(8,128)(2,1)} %all-to-all-done.g0, bf16[64,2,16,256]{3,2,1,0:T(8,128)(2,1)S(1)} %collective-permute-done.7.below_hbm.g1, bf16[64,2,16,256]{3,2,1,0:T(8,128)(2,1)S(1)} %collective-permute-done.8.above_hbm.g3, ...), custom_call_target="tpu_custom_call" | custom-call | flops 2147483648 | bytes 6291456 | tf_op jit(solution)/shard_map/statistics/pallas_call | solution.py:385
  126.0 17.1 %all-to-all-done.1.slots_hbm = bf16[64,2,16,256]{3,2,1,0:T(8,128)(2,1)S(1)} async-done(((bf16[64,2,16,256]{3,2,1,0:T(8,128)(2,1)}), bf16[64,2,16,256]{3,2,1,0:T(8,128)(2,1)S(1)}, u32[]{:S(2)}, u32[]{:S(2)}) %all-to-all-start.1) | async-done | bytes 1048608 | tf_op jit(solution)/shard_map/all_to_all | solution.py:407
  143.1 1.7 %collect.1 = bf16[64,16,256]{2,1,0:T(8,128)(2,1)} custom-call(s32[64]{0:T(128)S(1)} %copy-done.8, bf16[64,2,16,256]{3,2,1,0:T(8,128)(2,1)S(1)} %all-to-all-done.1.slots_hbm), custom_call_target="tpu_custom_call" | custom-call | bytes 1572864 | tf_op jit(solution)/shard_map/collect/pallas_call | solution.py:123
  (11 shorter events, 0.0 us)
Async XLA Ops:
  0.6 24.3 %collective-permute-start = (bf16[2,256,1024]{2,1,0:T(8,128)(2,1)}, bf16[2,256,1024]{2,1,0:T(8,128)(2,1)}, u32[]{:S(2)}, u32[]{:S(2)}) collective-permute-start(bf16[2,256,1024]{2,1,0:T(8,128)(2,1)} %l0.1), channel_id=1, source_target_pairs={{0,1},{1,2},{2,3},{3,0},{4,5},{5,6},{6,7},{7,4},{8,9},{9,10},{10,1... | collective-permute-start | bytes 3145736 | tf_op jit(solution)/shard_map/ppermute | solution.py:403
  2.7 23.7 %collective-permute-start.1 = (bf16[2,256,1024]{2,1,0:T(8,128)(2,1)}, bf16[2,256,1024]{2,1,0:T(8,128)(2,1)}, u32[]{:S(2)}, u32[]{:S(2)}) collective-permute-start(bf16[2,256,1024]{2,1,0:T(8,128)(2,1)} %l0.1), channel_id=1, source_target_pairs={{0,3},{1,0},{2,1},{3,2},{4,7},{5,4},{6,5},{7,6},{8,11},{9,8},{10,9... | collective-permute-start | bytes 3145736 | tf_op jit(solution)/shard_map/ppermute | solution.py:403
  6.7 23.8 %collective-permute-start.2 = (bf16[2,256,256]{2,1,0:T(8,128)(2,1)}, bf16[2,256,256]{2,1,0:T(8,128)(2,1)}, u32[]{:S(2)}, u32[]{:S(2)}) collective-permute-start(bf16[2,256,256]{2,1,0:T(8,128)(2,1)} %get-tuple-element.32), channel_id=1, source_target_pairs={{0,1},{1,2},{2,3},{3,0},{4,5},{5,6},{6,7},{7,4},{8,9},{9,10},{10,1... | collective-permute-start | bytes 786440 | tf_op jit(solution)/shard_map/ppermute | solution.py:403
  6.9 25.1 %collective-permute-start.3 = (bf16[2,256,256]{2,1,0:T(8,128)(2,1)}, bf16[2,256,256]{2,1,0:T(8,128)(2,1)}, u32[]{:S(2)}, u32[]{:S(2)}) collective-permute-start(bf16[2,256,256]{2,1,0:T(8,128)(2,1)} %get-tuple-element.33), channel_id=1, source_target_pairs={{0,3},{1,0},{2,1},{3,2},{4,7},{5,4},{6,5},{7,6},{8,11},{9,8},{10,9... | collective-permute-start | bytes 786440 | tf_op jit(solution)/shard_map/ppermute | solution.py:403
  9.5 41.6 %all-to-all-start = ((bf16[64,2,16,256]{3,2,1,0:T(8,128)(2,1)}), bf16[64,2,16,256]{3,2,1,0:T(8,128)(2,1)}, u32[]{:S(2)}, u32[]{:S(2)}) async-start(bf16[64,2,16,256]{3,2,1,0:T(8,128)(2,1)} %get-tuple-element.29), calls=%async_computation | async-start | bytes 2097152 | tf_op jit(solution)/shard_map/all_to_all | solution.py:407
  32.0 18.2 %collective-permute-start.4 = (bf16[256,1024]{1,0:T(8,128)(2,1)}, bf16[256,1024]{1,0:T(8,128)(2,1)S(1)}, u32[]{:S(2)}, u32[]{:S(2)}) collective-permute-start(bf16[256,1024]{1,0:T(8,128)(2,1)} %get-tuple-element.34), channel_id=1, source_target_pairs={{0,1},{1,2},{2,3},{3,0},{4,5},{5,6},{6,7},{7,4},{8,9},{9,10},{10,1... | collective-permute-start | bytes 1572872 | tf_op jit(solution)/shard_map/ppermute | solution.py:403
  33.6 16.6 %collective-permute-start.5 = (bf16[256,1024]{1,0:T(8,128)(2,1)}, bf16[256,1024]{1,0:T(8,128)(2,1)S(1)}, u32[]{:S(2)}, u32[]{:S(2)}) collective-permute-start(bf16[256,1024]{1,0:T(8,128)(2,1)} %get-tuple-element.35), channel_id=1, source_target_pairs={{0,3},{1,0},{2,1},{3,2},{4,7},{5,4},{6,5},{7,6},{8,11},{9,8},{10,9... | collective-permute-start | bytes 1572872 | tf_op jit(solution)/shard_map/ppermute | solution.py:403
  34.7 15.5 %collective-permute-start.6 = (bf16[2,256,256]{2,1,0:T(8,128)(2,1)}, bf16[2,256,256]{2,1,0:T(8,128)(2,1)S(1)}, u32[]{:S(2)}, u32[]{:S(2)}) collective-permute-start(bf16[2,256,256]{2,1,0:T(8,128)(2,1)} %get-tuple-element.36), channel_id=1, source_target_pairs={{0,2},{1,3},{2,0},{3,1},{4,6},{5,7},{6,4},{7,5},{8,10},{9,11},{10,... | collective-permute-start | bytes 786440 | tf_op jit(solution)/shard_map/ppermute | solution.py:403
  51.1 23.2 %collective-permute-start.7 = (bf16[64,2,16,256]{3,2,1,0:T(8,128)(2,1)}, bf16[64,2,16,256]{3,2,1,0:T(8,128)(2,1)S(1)}, u32[]{:S(2)}, u32[]{:S(2)}) collective-permute-start(bf16[64,2,16,256]{3,2,1,0:T(8,128)(2,1)} %all-to-all-done.g0), channel_id=1, source_target_pairs={{0,1},{1,2},{2,3},{3,0},{4,5},{5,6},{6,7},{7,4},{8,9},{9,10},{10,1... | collective-permute-start | bytes 3145736 | tf_op jit(solution)/shard_map/ppermute | solution.py:403
  51.1 23.2 %collective-permute-start.8 = (bf16[64,2,16,256]{3,2,1,0:T(8,128)(2,1)}, bf16[64,2,16,256]{3,2,1,0:T(8,128)(2,1)S(1)}, u32[]{:S(2)}, u32[]{:S(2)}) collective-permute-start(bf16[64,2,16,256]{3,2,1,0:T(8,128)(2,1)} %all-to-all-done.g0), channel_id=1, source_target_pairs={{0,3},{1,0},{2,1},{3,2},{4,7},{5,4},{6,5},{7,6},{8,11},{9,8},{10,9... | collective-permute-start | bytes 3145736 | tf_op jit(solution)/shard_map/ppermute | solution.py:403
  53.8 1.2 copy-start
  55.0 1.2 copy-start.7
  74.6 9.7 %collective-permute-start.10 = (bf16[32,2,16,256]{3,2,1,0:T(8,128)(2,1)S(1)}, bf16[32,2,16,256]{3,2,1,0:T(8,128)(2,1)S(1)}, u32[]{:S(2)}, u32[]{:S(2)}) collective-permute-start(bf16[32,2,16,256]{3,2,1,0:T(8,128)(2,1)S(1)} %get-tuple-element.44), channel_id=1, source_target_pairs={{0,3},{1,0},{2,1},{3,2},{4,7},{5,4},{6,5},{7,6},{8,11},{9,8},{10,9... | collective-permute-start | bytes 1572872 | tf_op jit(solution)/shard_map/ppermute | solution.py:403
  77.0 10.3 %collective-permute-start.9 = (bf16[32,2,16,256]{3,2,1,0:T(8,128)(2,1)S(1)}, bf16[32,2,16,256]{3,2,1,0:T(8,128)(2,1)S(1)}, u32[]{:S(2)}, u32[]{:S(2)}) collective-permute-start(bf16[32,2,16,256]{3,2,1,0:T(8,128)(2,1)S(1)} %get-tuple-element.43), channel_id=1, source_target_pairs={{0,1},{1,2},{2,3},{3,0},{4,5},{5,6},{6,7},{7,4},{8,9},{9,10},{10,1... | collective-permute-start | bytes 1572872 | tf_op jit(solution)/shard_map/ppermute | solution.py:403
  84.3 5.8 %copy-start.1 = (bf16[32,2,16,256]{3,2,1,0:T(8,128)(2,1)}, bf16[32,2,16,256]{3,2,1,0:T(8,128)(2,1)S(1)}, u32[]{:S(2)}) copy-start(bf16[32,2,16,256]{3,2,1,0:T(8,128)(2,1)S(1)} %collective-permute-done.10.gb) | copy-start | bytes 1572868
  87.3 2.7 %copy-start.3 = (bf16[32,2,16,256]{3,2,1,0:T(8,128)(2,1)}, bf16[32,2,16,256]{3,2,1,0:T(8,128)(2,1)S(1)}, u32[]{:S(2)}) copy-start(bf16[32,2,16,256]{3,2,1,0:T(8,128)(2,1)S(1)} %collective-permute-done.9.ga) | copy-start | bytes 1572868
  90.1 3.7 %collective-permute-start.11 = (f32[8,128]{1,0:T(8,128)S(1)}, f32[8,128]{1,0:T(8,128)S(1)}, u32[]{:S(2)}, u32[]{:S(2)}) collective-permute-start(f32[8,128]{1,0:T(8,128)S(1)} %get-tuple-element.54.s0), channel_id=1, source_target_pairs={{0,1},{1,2},{2,3},{3,0},{4,5},{5,6},{6,7},{7,4},{8,9},{9,10},{10,1... | collective-permute-start | bytes 12296 | tf_op jit(solution)/shard_map/ppermute | solution.py:403
  90.2 4.0 %collective-permute-start.12 = (f32[8,128]{1,0:T(8,128)S(1)}, f32[8,128]{1,0:T(8,128)S(1)}, u32[]{:S(2)}, u32[]{:S(2)}) collective-permute-start(f32[8,128]{1,0:T(8,128)S(1)} %get-tuple-element.54.s0), channel_id=1, source_target_pairs={{0,2},{1,3},{2,0},{3,1},{4,6},{5,7},{6,4},{7,5},{8,10},{9,11},{10,... | collective-permute-start | bytes 12296 | tf_op jit(solution)/shard_map/ppermute | solution.py:403
  91.6 2.8 %collective-permute-start.13 = (f32[8,128]{1,0:T(8,128)S(1)}, f32[8,128]{1,0:T(8,128)S(1)}, u32[]{:S(2)}, u32[]{:S(2)}) collective-permute-start(f32[8,128]{1,0:T(8,128)S(1)} %get-tuple-element.54.s0), channel_id=1, source_target_pairs={{0,3},{1,0},{2,1},{3,2},{4,7},{5,4},{6,5},{7,6},{8,11},{9,8},{10,9... | collective-permute-start | bytes 12296 | tf_op jit(solution)/shard_map/ppermute | solution.py:403
  95.5 47.5 %all-to-all-start.1 = ((bf16[64,2,16,256]{3,2,1,0:T(8,128)(2,1)}), bf16[64,2,16,256]{3,2,1,0:T(8,128)(2,1)S(1)}, u32[]{:S(2)}, u32[]{:S(2)}) async-start(bf16[64,2,16,256]{3,2,1,0:T(8,128)(2,1)} %scale.1), calls=%async_computation.1 | async-start | bytes 2097152 | tf_op jit(solution)/shard_map/all_to_all | solution.py:407
  115.1 1.0 copy-start.2
  116.1 1.0 copy-start.4
  117.2 1.6 %copy-start.5 = (f32[2,256,1024]{2,1,0:T(8,128)S(1)}, f32[2,256,1024]{2,1,0:T(8,128)}, u32[]{:S(2)}) copy-start(f32[2,256,1024]{2,1,0:T(8,128)} %left_ref.1) | copy-start | bytes 6291460
  118.7 1.6 %copy-start.6 = (f32[2,256,1024]{2,1,0:T(8,128)S(1)}, f32[2,256,1024]{2,1,0:T(8,128)}, u32[]{:S(2)}) copy-start(f32[2,256,1024]{2,1,0:T(8,128)} %right_ref.1) | copy-start | bytes 6291460
  120.3 22.7 %copy-start.8 = (s32[64]{0:T(128)S(1)}, s32[64]{0:T(128)}, u32[]{:S(2)}) copy-start(s32[64]{0:T(128)} %owner_hbm.3) | copy-start | bytes 772

commit v4 on v3

v4 whole, which is shorter than its diff:
```python
import functools

import jax
import jax.numpy as jnp
from jax import lax
from jax.experimental import pallas as pl
from jax.experimental.pallas import tpu as pltpu
from jax.sharding import PartitionSpec as P

DECAY = 0.99
EPSILON = 1e-06
BF16 = jnp.bfloat16
F32 = jnp.float32
VMEM_SPEC = pl.BlockSpec(memory_space=pltpu.VMEM)
SMEM_SPEC = pl.BlockSpec(memory_space=pltpu.SMEM)
HBM_SPEC = pl.BlockSpec(memory_space=pltpu.HBM)
PARAMS = pltpu.CompilerParams(vmem_limit_bytes=20 * 1024 * 1024)
WHOLE = pltpu.CompilerParams(vmem_limit_bytes=63 * 1024 * 1024)


def dot(a, b, ca=1, cb=0):
    return lax.dot_general(a, b, (((ca,), (cb,)), ((), ())), preferred_element_type=F32)


def cost(flops, nbytes):
    return pl.CostEstimate(flops=flops, bytes_accessed=nbytes, transcendentals=0)


def clear_counts(count_ref, owners):
    def clear(i, _):
        count_ref[i] = 0
        return 0

    lax.fori_loop(0, owners, clear, 0, unroll=8)


def route_kernel(
    t_ref, owner_hbm, grad_hbm, left_hbm, right_hbm, out_hbm, c1, c2, c3,
    grad, out, left, right, owner_ref, count_ref, sems,
):
    bring = [
        pltpu.make_async_copy(owner_hbm, owner_ref, sems.at[0]),
        pltpu.make_async_copy(grad_hbm, grad, sems.at[1]),
        pltpu.make_async_copy(left_hbm, left, sems.at[2]),
        pltpu.make_async_copy(right_hbm, right, sems.at[3]),
    ]
    for c in bring:
        c.start()
    out[...] = jnp.zeros_like(out)
    clear_counts(count_ref, out.shape[0])
    for c in bring:
        c.wait()
    rows = left.shape[1]
    half = rows // 2
    width = right.shape[2] // 4
    sends = []
    for k, cut in ((1, c1), (2, c2), (3, c3)):
        d = lax.rem(t_ref[0] + k, 4)
        slot = d // 2
        pieces = [(left.at[slot], cut.at[pl.ds(0, rows)])]
        for i, group in enumerate((d, 3 - d)):
            cols = pl.ds(pl.multiple_of(group * width, width), width)
            for j in range(2):
                source = right.at[slot, pl.ds(j * half, half), cols]
                place = cut.at[pl.ds(rows, half), pl.ds((2 * i + j) * width, width)]
                pieces.append((source, place))
        for i, (source, place) in enumerate(pieces):
            sends.append(pltpu.make_async_copy(source, place, sems.at[4 + 5 * (k - 1) + i]))
    for c in sends:
        c.start()

    def body(b, _):
        o = owner_ref[b]
        c = count_ref[o]
        count_ref[o] = c + 1
        out[o, c] = grad[b]
        return 0

    lax.fori_loop(0, grad.shape[0], body, 0, unroll=8)
    sends.append(pltpu.make_async_copy(out, out_hbm, sems.at[19]))
    sends[-1].start()
    for c in sends:
        c.wait()


def route(t, block_owner, gradient, left_root, right_root, owners):
    blocks, rows, cols = gradient.shape
    shape = (owners, 2, rows, cols)
    _, held, full = left_root.shape
    cut = jax.ShapeDtypeStruct((held + held // 2, full), BF16)
    return pl.pallas_call(
        route_kernel,
        out_shape=(jax.ShapeDtypeStruct(shape, gradient.dtype), cut, cut, cut),
        in_specs=[SMEM_SPEC] + [HBM_SPEC] * 4,
        out_specs=(HBM_SPEC,) * 4,
        scratch_shapes=[
            pltpu.VMEM(gradient.shape, BF16),
            pltpu.VMEM(shape, BF16),
            pltpu.VMEM(left_root.shape, BF16),
            pltpu.VMEM(right_root.shape, BF16),
            pltpu.SMEM((blocks,), jnp.int32),
            pltpu.SMEM((owners,), jnp.int32),
            pltpu.SemaphoreType.DMA((20,)),
        ],
        compiler_params=WHOLE,
        cost_estimate=cost(0, 3 * gradient.size),
        name="route",
    )(t, block_owner, gradient, left_root, right_root)


def collect_kernel(owner_hbm, slots_hbm, out_hbm, slots, out, owner_ref, count_ref, sems):
    bring = [
        pltpu.make_async_copy(owner_hbm, owner_ref, sems.at[0]),
        pltpu.make_async_copy(slots_hbm, slots, sems.at[1]),
    ]
    for c in bring:
        c.start()
    clear_counts(count_ref, slots.shape[0])
    for c in bring:
        c.wait()

    def body(b, _):
        o = owner_ref[b]
        c = count_ref[o]
        count_ref[o] = c + 1
        out[b] = slots[o, c]
        return 0

    lax.fori_loop(0, out.shape[0], body, 0, unroll=8)
    send = pltpu.make_async_copy(out, out_hbm, sems.at[2])
    send.start()
    send.wait()


def collect(block_owner, slots):
    blocks = block_owner.shape[0]
    shape = (blocks,) + slots.shape[2:]
    return pl.pallas_call(
        collect_kernel,
        out_shape=jax.ShapeDtypeStruct(shape, slots.dtype),
        in_specs=[HBM_SPEC] * 2,
        out_specs=HBM_SPEC,
        scratch_shapes=[
            pltpu.VMEM(slots.shape, slots.dtype),
            pltpu.VMEM(shape, slots.dtype),
            pltpu.SMEM((blocks,), jnp.int32),
            pltpu.SMEM((slots.shape[0],), jnp.int32),
            pltpu.SemaphoreType.DMA((3,)),
        ],
        compiler_params=PARAMS,
        cost_estimate=cost(0, 3 * slots.size),
        name="collect",
    )(block_owner, slots)


def select_kernel(t_ref, both_hbm, s1, s2, s3, both, sems):
    bring = pltpu.make_async_copy(both_hbm, both, sems.at[0])
    bring.start()
    bring.wait()
    sends = []
    for k, out in ((1, s1), (2, s2), (3, s3)):
        slot = lax.rem(t_ref[0] + k, 4) // 2
        sends.append(pltpu.make_async_copy(both.at[:, slot], out, sems.at[k]))
        sends[-1].start()
    for c in sends:
        c.wait()


def select(t, both):
    owners, _, height, width = both.shape
    out = jax.ShapeDtypeStruct((owners, height, width), BF16)
    return pl.pallas_call(
        select_kernel,
        out_shape=(out,) * 3,
        in_specs=[SMEM_SPEC, HBM_SPEC],
        out_specs=(HBM_SPEC,) * 3,
        scratch_shapes=[pltpu.VMEM(both.shape, BF16), pltpu.SemaphoreType.DMA((4,))],
        compiler_params=PARAMS,
        cost_estimate=cost(0, 6 * both.size),
        name="select",
    )(t, both)


def bring_right(cut, to, sems):
    _, rows, width = to.shape
    half = rows // 2
    return [
        pltpu.make_async_copy(
            cut.at[pl.ds(rows, half), pl.ds((2 * i + j) * width, width)],
            to.at[i, pl.ds(j * half, half)],
            sems.at[2 * i + j],
        )
        for i in range(2)
        for j in range(2)
    ]


def hold_kernel(a, b, out_ref):
    out_ref[...] = jnp.zeros_like(out_ref)


def hold(first, second):
    return pl.pallas_call(
        hold_kernel,
        out_shape=jax.ShapeDtypeStruct((8, 128), F32),
        in_specs=[HBM_SPEC] * 2,
        out_specs=VMEM_SPEC,
        compiler_params=WHOLE,
        cost_estimate=cost(2 * 10**11, 8 * 128),
        name="hold",
    )(first, second)


def own_kernel(
    t_ref, token, left_hbm, right_hbm, c1, c3, c2, both_hbm, raw_ref, square_ref, left, both, roots, sems
):
    t = t_ref[0]
    slot = t // 2
    rows = left_hbm.shape[1]
    full = left.shape[0]
    width = roots.shape[2]
    bring = [
        pltpu.make_async_copy(both_hbm, both, sems.at[0]),
        pltpu.make_async_copy(left_hbm.at[slot], left.at[pl.ds(0, rows)], sems.at[1]),
    ]
    for i, c in enumerate((c1, c3, c2)):
        to = left.at[pl.ds((i + 1) * rows, rows)]
        bring.append(pltpu.make_async_copy(c.at[pl.ds(0, rows)], to, sems.at[2 + i]))
    for i, group in enumerate((t, 3 - t)):
        cols = pl.ds(pl.multiple_of(group * width, width), width)
        bring.append(pltpu.make_async_copy(right_hbm.at[slot, :, cols], roots.at[i], sems.at[5 + i]))
    for c in bring:
        c.start()
    for c in bring:
        c.wait()
    part = dot(left[...], both[:, slot].reshape(full, width)).astype(BF16)
    for i in range(2):
        raw_ref[i] = dot(part, roots[i])
    for i in range(2):
        wide = both[:, i].reshape(full, width).astype(F32)
        square_ref[i] = jnp.broadcast_to(jnp.sum(wide * wide, keepdims=True), square_ref.shape[1:])


def own_part(t, token, left_root, right_root, cuts, owned):
    owners, slots, height, width = owned.shape
    full = owners * height
    return pl.pallas_call(
        own_kernel,
        out_shape=(
            jax.ShapeDtypeStruct((2, full, width), F32),
            jax.ShapeDtypeStruct((slots, 8, 128), F32),
            jax.ShapeDtypeStruct((full, full), BF16),
        ),
        in_specs=[SMEM_SPEC, VMEM_SPEC] + [HBM_SPEC] * 6,
        out_specs=(VMEM_SPEC,) * 3,
        scratch_shapes=[
            pltpu.VMEM(owned.shape, BF16),
            pltpu.VMEM((2, width, width), BF16),
            pltpu.SemaphoreType.DMA((7,)),
        ],
        compiler_params=PARAMS,
        cost_estimate=cost(4 * full * full * width, 12 * full * full),
        name="own_part",
    )(t, token, left_root, right_root, *cuts, owned)


def near_kernel(own, left, g1, g3, c1, c3, raw_ref, grads, roots, sems):
    full = left.shape[0]
    width = roots.shape[3]
    groups = []
    for i, (g, c) in enumerate(((g1, c1), (g3, c3))):
        bring = [pltpu.make_async_copy(g, grads.at[i], sems.at[i, 4])]
        groups.append(bring + bring_right(c, roots.at[i], sems.at[i]))
    for bring in groups:
        for c in bring:
            c.start()
    raw = [own[0], own[1]]
    for i, bring in enumerate(groups):
        for c in bring:
            c.wait()
        part = dot(left[...], grads[i].reshape(full, width)).astype(BF16)
        for j in range(2):
            raw[j] = raw[j] + dot(part, roots[i, j])
    for j in range(2):
        raw_ref[j] = raw[j]


def near_part(own, left, below, above, cut_below, cut_above):
    owners, height, width = below.shape
    full = left.shape[0]
    return pl.pallas_call(
        near_kernel,
        out_shape=jax.ShapeDtypeStruct(own.shape, F32),
        in_specs=[VMEM_SPEC] * 2 + [HBM_SPEC] * 4,
        out_specs=VMEM_SPEC,
        scratch_shapes=[
            pltpu.VMEM((2, owners, height, width), BF16),
            pltpu.VMEM((2, 2, width, width), BF16),
            pltpu.SemaphoreType.DMA((2, 5)),
        ],
        compiler_params=PARAMS,
        cost_estimate=cost(6 * full * full * width, 10 * full * full),
        name="near_part",
    )(own, left, below, above, cut_below, cut_above)


def far_kernel(
    t_ref, near, square, left, g2, c2, mine_ref, other_ref, sums_ref, roots, sems
):
    bring = bring_right(c2, roots, sems)
    for c in bring:
        c.start()
    full = left.shape[0]
    width = roots.shape[2]
    part = dot(left[...], g2[...].reshape(full, width)).astype(BF16)
    for c in bring:
        c.wait()
    mine = near[0] + dot(part, roots[0])
    other = near[1] + dot(part, roots[1])
    mine_ref[...] = mine
    other_ref[...] = other.astype(BF16)
    total = jnp.sum(mine * mine, keepdims=True) + jnp.sum(other * other, keepdims=True)
    row = lax.broadcasted_iota(jnp.int32, sums_ref.shape, 0)
    sums = jnp.where(row == t_ref[0] // 2, total, jnp.zeros(sums_ref.shape, F32))
    for slot in range(2):
        sums = jnp.where(row == 2 + slot, square[slot], sums)
    sums_ref[...] = sums


def far_part(t, near, square, left, far, cut_far):
    _, full, width = near.shape
    return pl.pallas_call(
        far_kernel,
        out_shape=(
            jax.ShapeDtypeStruct((full, width), F32),
            jax.ShapeDtypeStruct((full, width), BF16),
            jax.ShapeDtypeStruct((8, 128), F32),
        ),
        in_specs=[SMEM_SPEC] + [VMEM_SPEC] * 4 + [HBM_SPEC],
        out_specs=(VMEM_SPEC,) * 3,
        scratch_shapes=[pltpu.VMEM((2, width, width), BF16), pltpu.SemaphoreType.DMA((4,))],
        compiler_params=PARAMS,
        cost_estimate=cost(4 * full * full * width, 8 * full * full),
        name="far_part",
    )(t, near, square, left, far, cut_far)


def scale_kernel(t_ref, mine, other, s0, s1, s2, s3, out_hbm, ready, sems):
    _, _, here, height, width = ready.shape
    rows = here * height
    t = t_ref[0]
    sums = s0[...] + s1[...] + s2[...] + s3[...]
    first, second = (
        jnp.sqrt((sums[2 + slot : 3 + slot, 0:1] + EPSILON) / (sums[slot : slot + 1, 0:1] + EPSILON))
        for slot in range(2)
    )
    copies = []
    for j, (raw, member) in enumerate(((mine, t), (other, 3 - t))):
        slot = member // 2
        graft = jnp.where(slot == 0, first, second)
        for i, k in enumerate((0, 1, 3, 2)):
            scaled = raw[i * rows : (i + 1) * rows, :].astype(F32) * graft
            ready[j, i] = scaled.astype(BF16).reshape(here, height, width)
            s = lax.rem(member + 4 - k, 4)
            to = out_hbm.at[pl.ds(s * here, here), slot]
            copies.append(pltpu.make_async_copy(ready.at[j, i], to, sems.at[j, i]))
            copies[-1].start()
    for c in copies:
        c.wait()


def scale(t, mine, other, sums, shape):
    owners, _, height, width = shape
    return pl.pallas_call(
        scale_kernel,
        out_shape=jax.ShapeDtypeStruct(shape, BF16),
        in_specs=[SMEM_SPEC] + [VMEM_SPEC] * 6,
        out_specs=HBM_SPEC,
        scratch_shapes=[
            pltpu.VMEM((2, 4, owners // 4, height, width), BF16),
            pltpu.SemaphoreType.DMA((2, 4)),
        ],
        compiler_params=PARAMS,
        cost_estimate=cost(0, 16 * owners * height * width),
        name="scale",
    )(t, mine, other, *sums)


def terms_kernel(t_ref, g0_hbm, g1, g3, g2, out_ref, own, turned, sems):
    t = t_ref[0]
    bring = pltpu.make_async_copy(g0_hbm.at[:, t // 2], own, sems.at[0])
    bring.start()
    owners, height, rows = own.shape
    full = owners * height
    here = owners // 4
    theirs = pl.ds(pl.multiple_of((3 - t) * here, here), here)

    def turn(g):
        turned[...] = g[...].reshape(full, rows).T

    pl.when(lax.rem(t, 2) == 0)(lambda: turn(g1))
    pl.when(lax.rem(t, 2) == 1)(lambda: turn(g3))
    bring.wait()
    term = None
    for k, g in ((0, own), (1, g1), (3, g3), (2, g2)):
        whole = g[...].reshape(full, rows)
        part = dot(g[theirs].reshape(rows, rows), whole, 1, 1)
        term = part if term is None else term + part
        s = lax.rem(t + 4 - k, 4)
        cols = pl.ds(pl.multiple_of(s * rows, rows), rows)
        out_ref[1, :, cols] = dot(turned[...], whole).astype(BF16)
    out_ref[0] = term.astype(BF16)


def terms_across(t, owned, others):
    owners, _, height, rows = owned.shape
    full = owners * height
    return pl.pallas_call(
        terms_kernel,
        out_shape=jax.ShapeDtypeStruct((2, rows, full), BF16),
        in_specs=[SMEM_SPEC, HBM_SPEC] + [VMEM_SPEC] * 3,
        out_specs=VMEM_SPEC,
        scratch_shapes=[
            pltpu.VMEM((owners, height, rows), BF16),
            pltpu.VMEM((rows, full), BF16),
            pltpu.SemaphoreType.DMA((1,)),
        ],
        compiler_params=PARAMS,
        cost_estimate=cost(4 * rows * full * full, 6 * rows * full),
        name="terms_across",
    )(t, owned, *others)


def stats_kernel(t_ref, g0_hbm, g1, g3, g2, left_ref, right_ref, new_left_ref, new_right_ref, own, sems):
    t = t_ref[0]
    rows, full = left_ref.shape
    here = own.shape[0] // 4
    mine = pl.ds(pl.multiple_of(t * here, here), here)
    bring = pltpu.make_async_copy(g0_hbm.at[:, t // 2], own, sems.at[0])
    bring.start()
    bring.wait()
    turned = own[...].reshape(full, rows).T
    term = None
    for k, g in ((0, own), (1, g1), (3, g3), (2, g2)):
        whole = g[...].reshape(full, rows)
        part = dot(g[mine].reshape(rows, rows), whole, 1, 1)
        term = part if term is None else term + part
        s = lax.rem(t + 4 - k, 4)
        cols = pl.ds(pl.multiple_of(s * rows, rows), rows)
        new_right_ref[:, cols] = DECAY * right_ref[:, cols] + (1.0 - DECAY) * dot(turned, whole)
    new_left_ref[...] = DECAY * left_ref[...] + (1.0 - DECAY) * term


def statistics(t, owned, others, left_stat, right_stat):
    _, rows, full = left_stat.shape
    owners, _, height, width = owned.shape
    slot_spec = pl.BlockSpec((None, rows, full), lambda i, t_ref: (t_ref[0] // 2, 0, 0))
    shape = jax.ShapeDtypeStruct(left_stat.shape, F32)
    return pl.pallas_call(
        stats_kernel,
        out_shape=(shape, shape),
        grid_spec=pltpu.PrefetchScalarGridSpec(
            num_scalar_prefetch=1,
            grid=(1,),
            in_specs=[HBM_SPEC] + [VMEM_SPEC] * 3 + [slot_spec] * 2,
            out_specs=(slot_spec, slot_spec),
            scratch_shapes=[pltpu.VMEM((owners, height, width), BF16), pltpu.SemaphoreType.DMA((1,))],
        ),
        compiler_params=pltpu.CompilerParams(vmem_limit_bytes=32 * 1024 * 1024),
        cost_estimate=cost(4 * rows * full * full, 12 * rows * full),
        name="statistics",
    )(t, owned, *others, left_stat, right_stat)


def blend_kernel(t_ref, terms, left_ref, right_ref, _, __, new_left_ref, new_right_ref):
    new_left_ref[...] = DECAY * left_ref[...] + (1.0 - DECAY) * terms[0].astype(F32)
    new_right_ref[...] = DECAY * right_ref[...] + (1.0 - DECAY) * terms[1].astype(F32)


def blend(t, terms, left_stat, right_stat, done):
    _, rows, full = left_stat.shape
    slot_spec = pl.BlockSpec((None, rows, full), lambda i, t_ref: (1 - t_ref[0] // 2, 0, 0))
    shape = jax.ShapeDtypeStruct(left_stat.shape, F32)
    return pl.pallas_call(
        blend_kernel,
        out_shape=(shape, shape),
        grid_spec=pltpu.PrefetchScalarGridSpec(
            num_scalar_prefetch=1,
            grid=(1,),
            in_specs=[VMEM_SPEC] + [slot_spec] * 2 + [HBM_SPEC] * 2,
            out_specs=(slot_spec, slot_spec),
        ),
        input_output_aliases={4: 0, 5: 1},
        compiler_params=pltpu.CompilerParams(vmem_limit_bytes=32 * 1024 * 1024),
        cost_estimate=cost(4 * rows * full, 18 * rows * full),
        name="blend",
    )(t, terms, left_stat, right_stat, *done)


def around(x, k):
    n = lax.axis_size("tensor")
    return lax.ppermute(x, "tensor", [(i, (i + k) % n) for i in range(n)])


def across(x):
    n = lax.axis_size("tensor")
    return lax.ppermute(x, "tensor", [(i, n - 1 - i) for i in range(n)])


def exchange(x):
    return lax.all_to_all(x, "fsdp", split_axis=0, concat_axis=0, tiled=True)


def on_device(gradient, left_stat, right_stat, left_root, right_root, block_owner):
    owners = lax.axis_size("fsdp")
    t = lax.axis_index("tensor").reshape(1)
    routed, *cuts = route(t, block_owner, gradient, left_root, right_root, owners)
    cut_below, cut_far, cut_above = (around(c, k) for c, k in zip(cuts, (1, 2, 3)))
    owned = exchange(routed)
    owned, token = lax.optimization_barrier((owned, hold(cut_below, cut_above)))
    below, far, above = (around(x, k) for x, k in zip(select(t, owned), (1, 2, 3)))
    cuts = (cut_below, cut_above, cut_far)
    raw, square, left = own_part(t, token, left_root, right_root, cuts, owned)
    raw = near_part(raw, left, below, above, cut_below, cut_above)
    mine, other, sums = far_part(t, raw, square, left, far, cut_far)
    other = across(other)
    everyone = [sums] + [around(sums, k) for k in (1, 2, 3)]
    others = (below, above, far)
    terms = terms_across(t, owned, others)
    everyone, terms = lax.optimization_barrier((everyone, terms))
    terms = across(terms)
    returned = exchange(scale(t, mine, other, everyone, routed.shape))
    done = statistics(t, owned, others, left_stat, right_stat)
    new_left, new_right = blend(t, terms, left_stat, right_stat, done)
    return (new_left, new_right, collect(block_owner, returned))


def solution(mesh):
    return jax.shard_map(
        on_device,
        mesh=mesh,
        in_specs=(
            P(None, "fsdp", "tensor"),
            P("fsdp", "tensor", None),
            P("fsdp", "tensor", None),
            P("fsdp", "tensor", None),
            P("fsdp", "tensor", None),
            P(),
        ),
        out_specs=(P("fsdp", "tensor", None), P("fsdp", "tensor", None), P(None, "fsdp", "tensor")),
        check_vma=False,
    )
```

time: 146 us -> 136 us (0.932)
  starting transfers between devices: 51.4 us -> 45.5 us
  waiting for transfers between devices: 58 us -> 52.5 us
  local copies, waits for them, and re-layouts: 7.72 us -> 10 us
    ppermute x14 -> x9, waiting for transfers between devices: 40 us -> 13.6 us  [around(): return lax.ppermute(x, 'tensor', [(i, (i + k) % n) for i in range(n)])]
    ppermute x0 -> x2, waiting for transfers between devices: none -> 14.5 us  [across(): return lax.ppermute(x, 'tensor', [(i, n - 1 - i) for i in range(n)])]
    ppermute x14 -> x9, starting transfers between devices: 18.2 us -> 11.2 us  [around(): return lax.ppermute(x, 'tensor', [(i, (i + k) % n) for i in range(n)])]
    all_to_all x2, waiting for transfers between devices: 18 us -> 24.4 us  [exchange(): return lax.all_to_all(x, 'fsdp', split_axis=0, concat_axis=0, tiled=True)]
    ppermute x0 -> x2, starting transfers between devices: none -> 4.13 us  [across(): return lax.ppermute(x, 'tensor', [(i, n - 1 - i) for i in range(n)])]
    all_to_all x2, starting transfers between devices: 33.3 us -> 30.1 us  [exchange(): return lax.all_to_all(x, 'fsdp', split_axis=0, concat_axis=0, tiled=True)]
    pallas_call x1, Pallas kernels: 6.71 us -> 3.91 us  [near_part(): pl.pallas_call(near_kernel, out_shape=jax.ShapeDtypeStruct(own.shape, F32...]
    unnamed x18 -> x34, local copies, waits for them, and re-layouts: 7.72 us -> 10 us
  transfers between devices with their start and end apart: 16 -> 13, of which waited for: 13 -> 8; matrix products, arithmetic and copies ran while one was open for 0% -> 0% of each run, Pallas kernels for 15% -> 12%
where the time goes in v4:
time: 136 us; the launch traced here: 135 us
  waiting for transfers between devices  52.5 us (39%)
  starting transfers between devices  45.5 us (33%)
  Pallas kernels  25.8 us (19%)
  local copies, waits for them, and re-layouts  10 us (7%)
    all_to_all x2, starting transfers between devices, exchange(): return lax.all_to_all(x, 'fsdp', split_axis=0, concat_axis=0, tiled=True)  30.1 us
    all_to_all x2, waiting for transfers between devices, exchange(): return lax.all_to_all(x, 'fsdp', split_axis=0, concat_axis=0, tiled=True)  24.4 us
    ppermute x2, waiting for transfers between devices, across(): return lax.ppermute(x, 'tensor', [(i, n - 1 - i) for i in range(n)])  14.5 us
    ppermute x9, waiting for transfers between devices, around(): return lax.ppermute(x, 'tensor', [(i, (i + k) % n) for i in range(n)])  13.6 us
    ppermute x9, starting transfers between devices, around(): return lax.ppermute(x, 'tensor', [(i, (i + k) % n) for i in range(n)])  11.2 us
    unnamed x34, local copies, waits for them, and re-layouts  10 us
    ppermute x2, starting transfers between devices, across(): return lax.ppermute(x, 'tensor', [(i, n - 1 - i) for i in range(n)])  4.13 us
    pallas_call x1, Pallas kernels, near_part(): pl.pallas_call(near_kernel, out_shape=jax.ShapeDtypeStruct(own.shape, F32...  3.91 us
  transfers between devices with their start and end apart: 13, of which 8 were waited for; matrix products, arithmetic and copies ran while one was open for 0% of the time, Pallas kernels for 12%

profile of v4, /device:TPU:1, one launch (start us, length us, event | category | flops | bytes accessed | tf_op | source)
XLA Modules:
  0.0 134.8 jit_solution(11118570381596834916)
XLA Ops:
  0.6 3.6 %route.1 = (bf16[64,2,16,256]{3,2,1,0:T(8,128)(2,1)}, bf16[384,1024]{1,0:T(8,128)(2,1)}, bf16[384,1024]{1,0:T(8,128)(2,1)}, bf16[384,1024]{1,0:T(8,128)(2,1)}) custom-call(s32[1]{0:T(128)} %bitcast.t_ref, s32[64]{0:T(128)} %owner_hbm.3, bf16[64,16,256]{2,1,0:T(8,128)(2,1)} %grad_hbm.1, bf16[2,256,1024]{2,1,0:T(8,128)(2,1)} %left_hbm.3, ...), custom_call_target="tpu_custom_call" | custom-call | bytes 786432 | tf_op jit(solution)/shard_map/route/pallas_call | solution.py:91
  4.3 2.1 %collective-permute-start = (bf16[384,1024]{1,0:T(8,128)(2,1)}, bf16[384,1024]{1,0:T(8,128)(2,1)S(1)}, u32[]{:S(2)}, u32[]{:S(2)}) collective-permute-start(bf16[384,1024]{1,0:T(8,128)(2,1)} %get-tuple-element.28), channel_id=1, source_target_pairs={{0,1},{1,2},{2,3},{3,0},{4,5},{5,6},{6,7},{7,4},{8,9},{9,10},{10,1... | collective-permute-start | bytes 2359304 | tf_op jit(solution)/shard_map/ppermute | solution.py:502
  6.4 1.4 %collective-permute-start.1 = (bf16[384,1024]{1,0:T(8,128)(2,1)}, bf16[384,1024]{1,0:T(8,128)(2,1)}, u32[]{:S(2)}, u32[]{:S(2)}) collective-permute-start(bf16[384,1024]{1,0:T(8,128)(2,1)} %get-tuple-element.29), channel_id=1, source_target_pairs={{0,3},{1,0},{2,1},{3,2},{4,7},{5,4},{6,5},{7,6},{8,11},{9,8},{10,9... | collective-permute-start | bytes 2359304 | tf_op jit(solution)/shard_map/ppermute | solution.py:502
  7.7 13.2 %all-to-all-start = ((bf16[64,2,16,256]{3,2,1,0:T(8,128)(2,1)}), bf16[64,2,16,256]{3,2,1,0:T(8,128)(2,1)}, u32[]{:S(2)}, u32[]{:S(2)}) async-start(bf16[64,2,16,256]{3,2,1,0:T(8,128)(2,1)} %get-tuple-element.27), calls=%async_computation | async-start | bytes 2097152 | tf_op jit(solution)/shard_map/all_to_all | solution.py:511
  20.9 1.6 %collective-permute-start.2 = (bf16[384,1024]{1,0:T(8,128)(2,1)}, bf16[384,1024]{1,0:T(8,128)(2,1)}, u32[]{:S(2)}, u32[]{:S(2)}) collective-permute-start(bf16[384,1024]{1,0:T(8,128)(2,1)} %get-tuple-element.31), channel_id=1, source_target_pairs={{0,2},{1,3},{2,0},{3,1},{4,6},{5,7},{6,4},{7,5},{8,10},{9,11},{10,... | collective-permute-start | bytes 2359304 | tf_op jit(solution)/shard_map/ppermute | solution.py:502
  22.6 0.3 collective-permute-done.a.c1
  22.8 1.6 %collective-permute-done.1.b.c3 = bf16[384,1024]{1,0:T(8,128)(2,1)} collective-permute-done((bf16[384,1024]{1,0:T(8,128)(2,1)}, bf16[384,1024]{1,0:T(8,128)(2,1)}, u32[]{:S(2)}, u32[]{:S(2)}) %collective-permute-start.1) | collective-permute-done | bytes 786464 | tf_op jit(solution)/shard_map/ppermute | solution.py:502
  24.4 0.6 hold.1.token
  25.0 23.8 %all-to-all-done.both_hbm.g0_hbm = bf16[64,2,16,256]{3,2,1,0:T(8,128)(2,1)} async-done(((bf16[64,2,16,256]{3,2,1,0:T(8,128)(2,1)}), bf16[64,2,16,256]{3,2,1,0:T(8,128)(2,1)}, u32[]{:S(2)}, u32[]{:S(2)}) %all-to-all-start) | async-done | bytes 1048608 | tf_op jit(solution)/shard_map/all_to_all | solution.py:511
  48.8 1.5 %select.1 = (bf16[64,16,256]{2,1,0:T(8,128)(2,1)S(1)}, bf16[64,16,256]{2,1,0:T(8,128)(2,1)S(1)}, bf16[64,16,256]{2,1,0:T(8,128)(2,1)S(1)}) custom-call(s32[1]{0:T(128)} %bitcast.t_ref, bf16[64,2,16,256]{3,2,1,0:T(8,128)(2,1)} %all-to-all-done.both_hbm.g0_hbm), custom_call_target="tpu_custom_call" | custom-call | bytes 3145728 | tf_op jit(solution)/shard_map/select/pallas_call | solution.py:172
  50.3 0.1 collective-permute-start.3
  50.4 2.7 %collective-permute-start.4 = (bf16[64,16,256]{2,1,0:T(8,128)(2,1)S(1)}, bf16[64,16,256]{2,1,0:T(8,128)(2,1)S(1)}, u32[]{:S(2)}, u32[]{:S(2)}) collective-permute-start(bf16[64,16,256]{2,1,0:T(8,128)(2,1)S(1)} %get-tuple-element.36), channel_id=1, source_target_pairs={{0,3},{1,0},{2,1},{3,2},{4,7},{5,4},{6,5},{7,6},{8,11},{9,8},{10,9... | collective-permute-start | bytes 1572872 | tf_op jit(solution)/shard_map/ppermute | solution.py:502
  53.1 0.3 collective-permute-start.5
  53.4 0.0 collective-permute-done.2.c2
  53.4 1.2 copy-done.3
  54.6 1.2 copy-done.4
  55.9 1.1 copy-done.6
  57.0 0.7 copy-done.14
  57.7 3.0 %own_part.1 = (f32[2,1024,256]{2,1,0:T(8,128)S(1)}, f32[2,8,128]{2,1,0:T(8,128)S(1)}, bf16[1024,1024]{1,0:T(8,128)(2,1)S(1)}) custom-call(s32[1]{0:T(128)} %bitcast.t_ref, f32[8,128]{1,0:T(8,128)S(1)} %copy-done.14, bf16[2,256,1024]{2,1,0:T(8,128)(2,1)S(1)} %copy-done.3, bf16[2,256,1024]{2,1,0:T(8,128)(2,1)S(1)} %copy-done.4, ...), custom_call_target="tpu_custom_call" | custom-call | flops 1073741824 | bytes 12582912 | tf_op jit(solution)/shard_map/own_part/pallas_call | solution.py:247
  60.7 3.2 %collective-permute-done.3.g1 = bf16[64,16,256]{2,1,0:T(8,128)(2,1)S(1)} collective-permute-done((bf16[64,16,256]{2,1,0:T(8,128)(2,1)S(1)}, bf16[64,16,256]{2,1,0:T(8,128)(2,1)S(1)}, u32[]{:S(2)}, u32[]{:S(2)}) %collective-permute-start.3) | collective-permute-done | bytes 524320 | tf_op jit(solution)/shard_map/ppermute | solution.py:502
  63.9 0.0 collective-permute-done.4.g3
  63.9 3.9 %near_part.1.near = f32[2,1024,256]{2,1,0:T(8,128)S(1)} custom-call(f32[2,1024,256]{2,1,0:T(8,128)S(1)} %get-tuple-element.33.own, bf16[1024,1024]{1,0:T(8,128)(2,1)S(1)} %get-tuple-element.34.left, bf16[64,16,256]{2,1,0:T(8,128)(2,1)S(1)} %collective-permute-done.3.g1, bf16[64,16,256]{2,1,0:T(8,128)(2,1)S(1)} %collective-permute-done.4.g3, ...), custom_call_target="tpu_custom_call" | custom-call | flops 1610612736 | bytes 10485760 | tf_op jit(solution)/shard_map/near_part/pallas_call | solution.py:291
  67.8 6.9 %collective-permute-done.5.g2 = bf16[64,16,256]{2,1,0:T(8,128)(2,1)S(1)} collective-permute-done((bf16[64,16,256]{2,1,0:T(8,128)(2,1)S(1)}, bf16[64,16,256]{2,1,0:T(8,128)(2,1)S(1)}, u32[]{:S(2)}, u32[]{:S(2)}) %collective-permute-start.5) | collective-permute-done | bytes 524320 | tf_op jit(solution)/shard_map/ppermute | solution.py:502
  74.7 2.6 %far_part.1 = (f32[1024,256]{1,0:T(8,128)S(1)}, bf16[1024,256]{1,0:T(8,128)(2,1)S(1)}, f32[8,128]{1,0:T(8,128)S(1)}) custom-call(s32[1]{0:T(128)} %bitcast.t_ref, f32[2,1024,256]{2,1,0:T(8,128)S(1)} %near_part.1.near, f32[2,8,128]{2,1,0:T(8,128)S(1)} %get-tuple-element.37.square, bf16[1024,1024]{1,0:T(8,128)(2,1)S(1)} %get-tuple-element.34.left, ...), custom_call_target="tpu_custom_call" | custom-call | flops 1073741824 | bytes 8388608 | tf_op jit(solution)/shard_map/far_part/pallas_call | solution.py:332
  77.4 1.4 %collective-permute-start.10 = (bf16[1024,256]{1,0:T(8,128)(2,1)S(1)}, bf16[1024,256]{1,0:T(8,128)(2,1)S(1)}, u32[]{:S(2)}, u32[]{:S(2)}) collective-permute-start(bf16[1024,256]{1,0:T(8,128)(2,1)S(1)} %get-tuple-element.46), channel_id=1, source_target_pairs={{0,3},{1,2},{2,1},{3,0},{4,7},{5,6},{6,5},{7,4},{8,11},{9,10},{10,... | collective-permute-start | bytes 1572872 | tf_op jit(solution)/shard_map/ppermute | solution.py:507
  78.8 0.0 collective-permute-start.6
  78.8 2.5 %collective-permute-start.7 = (f32[8,128]{1,0:T(8,128)S(1)}, f32[8,128]{1,0:T(8,128)S(1)}, u32[]{:S(2)}, u32[]{:S(2)}) collective-permute-start(f32[8,128]{1,0:T(8,128)S(1)} %get-tuple-element.47.s0), channel_id=1, source_target_pairs={{0,2},{1,3},{2,0},{3,1},{4,6},{5,7},{6,4},{7,5},{8,10},{9,11},{10,... | collective-permute-start | bytes 12296 | tf_op jit(solution)/shard_map/ppermute | solution.py:502
  81.3 0.5 collective-permute-start.8
  81.9 0.0 copy-done.8
  81.9 2.3 %terms_across.1 = bf16[2,256,1024]{2,1,0:T(8,128)(2,1)S(1)} custom-call(s32[1]{0:T(128)} %bitcast.t_ref, bf16[64,2,16,256]{3,2,1,0:T(8,128)(2,1)} %all-to-all-done.both_hbm.g0_hbm, bf16[64,16,256]{2,1,0:T(8,128)(2,1)S(1)} %collective-permute-done.3.g1, bf16[64,16,256]{2,1,0:T(8,128)(2,1)S(1)} %collective-permute-done.4.g3, ...), custom_call_target="tpu_custom_call" | custom-call | flops 1073741824 | bytes 1572864 | tf_op jit(solution)/shard_map/terms_across/pallas_call | solution.py:418
  84.2 1.0 copy-done.16
  85.2 1.6 %collective-permute-done.6.s1 = f32[8,128]{1,0:T(8,128)S(1)} collective-permute-done((f32[8,128]{1,0:T(8,128)S(1)}, f32[8,128]{1,0:T(8,128)S(1)}, u32[]{:S(2)}, u32[]{:S(2)}) %collective-permute-start.6) | collective-permute-done | bytes 4128 | tf_op jit(solution)/shard_map/ppermute | solution.py:502
  86.8 0.0 collective-permute-done.7.s2
  86.8 0.0 collective-permute-done.8.s3
  86.8 0.0 collective-permute-done.10.other
  86.8 0.0 copy-start
  86.8 1.2 scale.1
  88.0 16.9 %all-to-all-start.1 = ((bf16[64,2,16,256]{3,2,1,0:T(8,128)(2,1)}), bf16[64,2,16,256]{3,2,1,0:T(8,128)(2,1)S(1)}, u32[]{:S(2)}, u32[]{:S(2)}) async-start(bf16[64,2,16,256]{3,2,1,0:T(8,128)(2,1)} %scale.1), calls=%async_computation.1 | async-start | bytes 2097152 | tf_op jit(solution)/shard_map/all_to_all | solution.py:511
  104.9 2.7 %collective-permute-start.9 = (bf16[2,256,1024]{2,1,0:T(8,128)(2,1)}, bf16[2,256,1024]{2,1,0:T(8,128)(2,1)S(1)}, u32[]{:S(2)}, u32[]{:S(2)}) collective-permute-start(bf16[2,256,1024]{2,1,0:T(8,128)(2,1)} %copy-done.16), channel_id=1, source_target_pairs={{0,3},{1,2},{2,1},{3,0},{4,7},{5,6},{6,5},{7,4},{8,11},{9,10},{10,... | collective-permute-start | bytes 3145736 | tf_op jit(solution)/shard_map/ppermute | solution.py:507
  107.7 1.6 %copy-done.1 = f32[2,256,1024]{2,1,0:T(8,128)S(1)} copy-done((f32[2,256,1024]{2,1,0:T(8,128)S(1)}, f32[2,256,1024]{2,1,0:T(8,128)}, u32[]{:S(2)}) %copy-start.1) | copy-done | bytes 2097176
  109.3 1.0 copy-done.9
  110.3 1.0 copy-done.11
  111.4 1.0 copy-done.13
  112.4 3.8 %statistics.1 = (f32[2,256,1024]{2,1,0:T(8,128)}, f32[2,256,1024]{2,1,0:T(8,128)}) custom-call(s32[1]{0:T(128)} %bitcast.t_ref, bf16[64,2,16,256]{3,2,1,0:T(8,128)(2,1)} %all-to-all-done.both_hbm.g0_hbm, bf16[64,16,256]{2,1,0:T(8,128)(2,1)S(1)} %copy-done.9, bf16[64,16,256]{2,1,0:T(8,128)(2,1)S(1)} %copy-done.11, bf16[64,16,256]{2,1,0:T(8,128)(2,1)S(1)} %copy-done.13, ...), custom_call_target="tpu_custom_call" | custom-call | flops 1073741824 | bytes 3145728 | tf_op jit(solution)/shard_map/statistics/pallas_call | solution.py:459
  116.2 14.5 %collective-permute-done.9.terms = bf16[2,256,1024]{2,1,0:T(8,128)(2,1)S(1)} collective-permute-done((bf16[2,256,1024]{2,1,0:T(8,128)(2,1)}, bf16[2,256,1024]{2,1,0:T(8,128)(2,1)S(1)}, u32[]{:S(2)}, u32[]{:S(2)}) %collective-permute-start.9) | collective-permute-done | bytes 1048608 | tf_op jit(solution)/shard_map/ppermute | solution.py:507
  130.7 1.6 %blend.1 = (f32[2,256,1024]{2,1,0:T(8,128)}, f32[2,256,1024]{2,1,0:T(8,128)}) custom-call(s32[1]{0:T(128)} %bitcast.t_ref, bf16[2,256,1024]{2,1,0:T(8,128)(2,1)S(1)} %collective-permute-done.9.terms, f32[2,256,1024]{2,1,0:T(8,128)S(1)} %copy-done, f32[2,256,1024]{2,1,0:T(8,128)S(1)} %copy-done.2, ...), custom_call_target="tpu_custom_call", output_to_operand_aliasing={{0}: (4, {}), {1}: (5, {})} | custom-call | flops 1048576 | bytes 4718592 | tf_op jit(solution)/shard_map/blend/pallas_call | solution.py:484
  132.3 0.6 all-to-all-done.1.slots_hbm
  132.9 1.7 %collect.1 = bf16[64,16,256]{2,1,0:T(8,128)(2,1)} custom-call(s32[64]{0:T(128)S(1)} %copy-done.15, bf16[64,2,16,256]{3,2,1,0:T(8,128)(2,1)S(1)} %all-to-all-done.1.slots_hbm), custom_call_target="tpu_custom_call" | custom-call | bytes 1572864 | tf_op jit(solution)/shard_map/collect/pallas_call | solution.py:138
  (23 shorter events, 0.0 us)
Async XLA Ops:
  4.3 18.6 %collective-permute-start = (bf16[384,1024]{1,0:T(8,128)(2,1)}, bf16[384,1024]{1,0:T(8,128)(2,1)S(1)}, u32[]{:S(2)}, u32[]{:S(2)}) collective-permute-start(bf16[384,1024]{1,0:T(8,128)(2,1)} %get-tuple-element.28), channel_id=1, source_target_pairs={{0,1},{1,2},{2,3},{3,0},{4,5},{5,6},{6,7},{7,4},{8,9},{9,10},{10,1... | collective-permute-start | bytes 2359304 | tf_op jit(solution)/shard_map/ppermute | solution.py:502
  6.4 18.1 %collective-permute-start.1 = (bf16[384,1024]{1,0:T(8,128)(2,1)}, bf16[384,1024]{1,0:T(8,128)(2,1)}, u32[]{:S(2)}, u32[]{:S(2)}) collective-permute-start(bf16[384,1024]{1,0:T(8,128)(2,1)} %get-tuple-element.29), channel_id=1, source_target_pairs={{0,3},{1,0},{2,1},{3,2},{4,7},{5,4},{6,5},{7,6},{8,11},{9,8},{10,9... | collective-permute-start | bytes 2359304 | tf_op jit(solution)/shard_map/ppermute | solution.py:502
  7.7 41.1 %all-to-all-start = ((bf16[64,2,16,256]{3,2,1,0:T(8,128)(2,1)}), bf16[64,2,16,256]{3,2,1,0:T(8,128)(2,1)}, u32[]{:S(2)}, u32[]{:S(2)}) async-start(bf16[64,2,16,256]{3,2,1,0:T(8,128)(2,1)} %get-tuple-element.27), calls=%async_computation | async-start | bytes 2097152 | tf_op jit(solution)/shard_map/all_to_all | solution.py:511
  20.9 32.5 %collective-permute-start.2 = (bf16[384,1024]{1,0:T(8,128)(2,1)}, bf16[384,1024]{1,0:T(8,128)(2,1)}, u32[]{:S(2)}, u32[]{:S(2)}) collective-permute-start(bf16[384,1024]{1,0:T(8,128)(2,1)} %get-tuple-element.31), channel_id=1, source_target_pairs={{0,2},{1,3},{2,0},{3,1},{4,6},{5,7},{6,4},{7,5},{8,10},{9,11},{10,... | collective-permute-start | bytes 2359304 | tf_op jit(solution)/shard_map/ppermute | solution.py:502
  22.8 1.6 %copy-start.5 = (bf16[384,1024]{1,0:T(8,128)(2,1)}, bf16[384,1024]{1,0:T(8,128)(2,1)S(1)}, u32[]{:S(2)}) copy-start(bf16[384,1024]{1,0:T(8,128)(2,1)S(1)} %collective-permute-done.a.c1) | copy-start | bytes 2359300
  50.3 13.6 %collective-permute-start.3 = (bf16[64,16,256]{2,1,0:T(8,128)(2,1)S(1)}, bf16[64,16,256]{2,1,0:T(8,128)(2,1)S(1)}, u32[]{:S(2)}, u32[]{:S(2)}) collective-permute-start(bf16[64,16,256]{2,1,0:T(8,128)(2,1)S(1)} %get-tuple-element.35), channel_id=1, source_target_pairs={{0,1},{1,2},{2,3},{3,0},{4,5},{5,6},{6,7},{7,4},{8,9},{9,10},{10,1... | collective-permute-start | bytes 1572872 | tf_op jit(solution)/shard_map/ppermute | solution.py:502
  50.4 13.5 %collective-permute-start.4 = (bf16[64,16,256]{2,1,0:T(8,128)(2,1)S(1)}, bf16[64,16,256]{2,1,0:T(8,128)(2,1)S(1)}, u32[]{:S(2)}, u32[]{:S(2)}) collective-permute-start(bf16[64,16,256]{2,1,0:T(8,128)(2,1)S(1)} %get-tuple-element.36), channel_id=1, source_target_pairs={{0,3},{1,0},{2,1},{3,2},{4,7},{5,4},{6,5},{7,6},{8,11},{9,8},{10,9... | collective-permute-start | bytes 1572872 | tf_op jit(solution)/shard_map/ppermute | solution.py:502
  53.1 21.6 %collective-permute-start.5 = (bf16[64,16,256]{2,1,0:T(8,128)(2,1)S(1)}, bf16[64,16,256]{2,1,0:T(8,128)(2,1)S(1)}, u32[]{:S(2)}, u32[]{:S(2)}) collective-permute-start(bf16[64,16,256]{2,1,0:T(8,128)(2,1)S(1)} %get-tuple-element.38), channel_id=1, source_target_pairs={{0,2},{1,3},{2,0},{3,1},{4,6},{5,7},{6,4},{7,5},{8,10},{9,11},{10,... | collective-permute-start | bytes 1572872 | tf_op jit(solution)/shard_map/ppermute | solution.py:502
  53.4 1.2 copy-start.3
  54.6 1.2 copy-start.4
  55.9 1.1 copy-start.6
  57.0 0.7 copy-start.14
  57.7 6.2 %copy-start.7 = (bf16[384,1024]{1,0:T(8,128)(2,1)S(1)}, bf16[384,1024]{1,0:T(8,128)(2,1)}, u32[]{:S(2)}) copy-start(bf16[384,1024]{1,0:T(8,128)(2,1)} %copy-done.5) | copy-start | bytes 2359300
  63.9 18.0 %copy-start.8 = (bf16[64,16,256]{2,1,0:T(8,128)(2,1)}, bf16[64,16,256]{2,1,0:T(8,128)(2,1)S(1)}, u32[]{:S(2)}) copy-start(bf16[64,16,256]{2,1,0:T(8,128)(2,1)S(1)} %collective-permute-done.3.g1) | copy-start | bytes 1572868
  63.9 18.0 %copy-start.10 = (bf16[64,16,256]{2,1,0:T(8,128)(2,1)}, bf16[64,16,256]{2,1,0:T(8,128)(2,1)S(1)}, u32[]{:S(2)}) copy-start(bf16[64,16,256]{2,1,0:T(8,128)(2,1)S(1)} %collective-permute-done.4.g3) | copy-start | bytes 1572868
  74.7 7.1 %copy-start.12 = (bf16[64,16,256]{2,1,0:T(8,128)(2,1)}, bf16[64,16,256]{2,1,0:T(8,128)(2,1)S(1)}, u32[]{:S(2)}) copy-start(bf16[64,16,256]{2,1,0:T(8,128)(2,1)S(1)} %collective-permute-done.5.g2) | copy-start | bytes 1572868
  77.4 9.4 %collective-permute-start.10 = (bf16[1024,256]{1,0:T(8,128)(2,1)S(1)}, bf16[1024,256]{1,0:T(8,128)(2,1)S(1)}, u32[]{:S(2)}, u32[]{:S(2)}) collective-permute-start(bf16[1024,256]{1,0:T(8,128)(2,1)S(1)} %get-tuple-element.46), channel_id=1, source_target_pairs={{0,3},{1,2},{2,1},{3,0},{4,7},{5,6},{6,5},{7,4},{8,11},{9,10},{10,... | collective-permute-start | bytes 1572872 | tf_op jit(solution)/shard_map/ppermute | solution.py:507
  78.8 8.0 %collective-permute-start.6 = (f32[8,128]{1,0:T(8,128)S(1)}, f32[8,128]{1,0:T(8,128)S(1)}, u32[]{:S(2)}, u32[]{:S(2)}) collective-permute-start(f32[8,128]{1,0:T(8,128)S(1)} %get-tuple-element.47.s0), channel_id=1, source_target_pairs={{0,1},{1,2},{2,3},{3,0},{4,5},{5,6},{6,7},{7,4},{8,9},{9,10},{10,1... | collective-permute-start | bytes 12296 | tf_op jit(solution)/shard_map/ppermute | solution.py:502
  78.8 8.0 %collective-permute-start.7 = (f32[8,128]{1,0:T(8,128)S(1)}, f32[8,128]{1,0:T(8,128)S(1)}, u32[]{:S(2)}, u32[]{:S(2)}) collective-permute-start(f32[8,128]{1,0:T(8,128)S(1)} %get-tuple-element.47.s0), channel_id=1, source_target_pairs={{0,2},{1,3},{2,0},{3,1},{4,6},{5,7},{6,4},{7,5},{8,10},{9,11},{10,... | collective-permute-start | bytes 12296 | tf_op jit(solution)/shard_map/ppermute | solution.py:502
  81.3 5.5 %collective-permute-start.8 = (f32[8,128]{1,0:T(8,128)S(1)}, f32[8,128]{1,0:T(8,128)S(1)}, u32[]{:S(2)}, u32[]{:S(2)}) collective-permute-start(f32[8,128]{1,0:T(8,128)S(1)} %get-tuple-element.47.s0), channel_id=1, source_target_pairs={{0,3},{1,0},{2,1},{3,2},{4,7},{5,4},{6,5},{7,6},{8,11},{9,8},{10,9... | collective-permute-start | bytes 12296 | tf_op jit(solution)/shard_map/ppermute | solution.py:502
  84.2 1.0 copy-start.16
  86.8 20.9 %copy-start = (f32[2,256,1024]{2,1,0:T(8,128)S(1)}, f32[2,256,1024]{2,1,0:T(8,128)}, u32[]{:S(2)}) copy-start(f32[2,256,1024]{2,1,0:T(8,128)} %left_ref.3) | copy-start | bytes 6291460
  88.0 44.9 %all-to-all-start.1 = ((bf16[64,2,16,256]{3,2,1,0:T(8,128)(2,1)}), bf16[64,2,16,256]{3,2,1,0:T(8,128)(2,1)S(1)}, u32[]{:S(2)}, u32[]{:S(2)}) async-start(bf16[64,2,16,256]{3,2,1,0:T(8,128)(2,1)} %scale.1), calls=%async_computation.1 | async-start | bytes 2097152 | tf_op jit(solution)/shard_map/all_to_all | solution.py:511
  104.9 25.8 %collective-permute-start.9 = (bf16[2,256,1024]{2,1,0:T(8,128)(2,1)}, bf16[2,256,1024]{2,1,0:T(8,128)(2,1)S(1)}, u32[]{:S(2)}, u32[]{:S(2)}) collective-permute-start(bf16[2,256,1024]{2,1,0:T(8,128)(2,1)} %copy-done.16), channel_id=1, source_target_pairs={{0,3},{1,2},{2,1},{3,0},{4,7},{5,6},{6,5},{7,4},{8,11},{9,10},{10,... | collective-permute-start | bytes 3145736 | tf_op jit(solution)/shard_map/ppermute | solution.py:507
  107.7 1.6 %copy-start.1 = (f32[2,256,1024]{2,1,0:T(8,128)S(1)}, f32[2,256,1024]{2,1,0:T(8,128)}, u32[]{:S(2)}) copy-start(f32[2,256,1024]{2,1,0:T(8,128)} %right_ref.3) | copy-start | bytes 6291460
  109.3 1.0 copy-start.9
  110.3 1.0 copy-start.11
  111.4 1.0 copy-start.13
  112.4 18.3 %copy-start.2 = (f32[2,256,1024]{2,1,0:T(8,128)S(1)}, f32[2,256,1024]{2,1,0:T(8,128)}, u32[]{:S(2)}) copy-start(f32[2,256,1024]{2,1,0:T(8,128)} %right_ref.3) | copy-start | bytes 6291460
  130.7 2.2 %copy-start.15 = (s32[64]{0:T(128)S(1)}, s32[64]{0:T(128)}, u32[]{:S(2)}) copy-start(s32[64]{0:T(128)} %owner_hbm.3) | copy-start | bytes 772

commit v5 on v4

--- a/solution.py
+++ b/solution.py
@@ -32,6 +32,12 @@
         return 0
 
     lax.fori_loop(0, owners, clear, 0, unroll=8)
+
+
+def column_groups(member, width):
+    half = width // 2
+    after, before = lax.rem(member + 1, 4), lax.rem(member + 3, 4)
+    return (member * width, width, 0), (after * width, half, width), (before * width + half, half, width + half)
 
 
 def route_kernel(
@@ -56,16 +62,15 @@
     sends = []
     for k, cut in ((1, c1), (2, c2), (3, c3)):
         d = lax.rem(t_ref[0] + k, 4)
-        slot = d // 2
+        slot = lax.rem(d, 2)
         pieces = [(left.at[slot], cut.at[pl.ds(0, rows)])]
-        for i, group in enumerate((d, 3 - d)):
-            cols = pl.ds(pl.multiple_of(group * width, width), width)
-            for j in range(2):
-                source = right.at[slot, pl.ds(j * half, half), cols]
-                place = cut.at[pl.ds(rows, half), pl.ds((2 * i + j) * width, width)]
-                pieces.append((source, place))
+        for j in range(2):
+            for start, size, at in column_groups(d, width):
+                source = right.at[slot, pl.ds(j * half, half), pl.ds(pl.multiple_of(start, 128), size)]
+                at = at + j * width if size == width else at + (j + 1) * width
+                pieces.append((source, cut.at[pl.ds(rows, half), pl.ds(at, size)]))
         for i, (source, place) in enumerate(pieces):
-            sends.append(pltpu.make_async_copy(source, place, sems.at[4 + 5 * (k - 1) + i]))
+            sends.append(pltpu.make_async_copy(source, place, sems.at[4 + 7 * (k - 1) + i]))
     for c in sends:
         c.start()
 
@@ -77,7 +82,7 @@
         return 0
 
     lax.fori_loop(0, grad.shape[0], body, 0, unroll=8)
-    sends.append(pltpu.make_async_copy(out, out_hbm, sems.at[19]))
+    sends.append(pltpu.make_async_copy(out, out_hbm, sems.at[25]))
     sends[-1].start()
     for c in sends:
         c.wait()
@@ -100,7 +105,7 @@
             pltpu.VMEM(right_root.shape, BF16),
             pltpu.SMEM((blocks,), jnp.int32),
             pltpu.SMEM((owners,), jnp.int32),
-            pltpu.SemaphoreType.DMA((20,)),
+            pltpu.SemaphoreType.DMA((26,)),
         ],
         compiler_params=WHOLE,
         cost_estimate=cost(0, 3 * gradient.size),
@@ -153,15 +158,17 @@
     )(block_owner, slots)
 
 
-def select_kernel(t_ref, both_hbm, s1, s2, s3, both, sems):
+def select_kernel(t_ref, both_hbm, other_hbm, same_hbm, both, sems):
     bring = pltpu.make_async_copy(both_hbm, both, sems.at[0])
     bring.start()
     bring.wait()
-    sends = []
-    for k, out in ((1, s1), (2, s2), (3, s3)):
-        slot = lax.rem(t_ref[0] + k, 4) // 2
-        sends.append(pltpu.make_async_copy(both.at[:, slot], out, sems.at[k]))
-        sends[-1].start()
+    slot = lax.rem(t_ref[0], 2)
+    sends = [
+        pltpu.make_async_copy(both.at[:, 1 - slot], other_hbm, sems.at[1]),
+        pltpu.make_async_copy(both.at[:, slot], same_hbm, sems.at[2]),
+    ]
+    for c in sends:
+        c.start()
     for c in sends:
         c.wait()
 
@@ -171,12 +178,12 @@
     out = jax.ShapeDtypeStruct((owners, height, width), BF16)
     return pl.pallas_call(
         select_kernel,
-        out_shape=(out,) * 3,
+        out_shape=(out,) * 2,
         in_specs=[SMEM_SPEC, HBM_SPEC],
-        out_specs=(HBM_SPEC,) * 3,
-        scratch_shapes=[pltpu.VMEM(both.shape, BF16), pltpu.SemaphoreType.DMA((4,))],
-        compiler_params=PARAMS,
-        cost_estimate=cost(0, 6 * both.size),
+        out_specs=(HBM_SPEC,) * 2,
+        scratch_shapes=[pltpu.VMEM(both.shape, BF16), pltpu.SemaphoreType.DMA((3,))],
+        compiler_params=PARAMS,
+        cost_estimate=cost(0, 4 * both.size),
         name="select",
     )(t, both)
 
@@ -215,7 +222,7 @@
     t_ref, token, left_hbm, right_hbm, c1, c3, c2, both_hbm, raw_ref, square_ref, left, both, roots, sems
 ):
     t = t_ref[0]
-    slot = t // 2
+    slot = lax.rem(t, 2)
     rows = left_hbm.shape[1]
     full = left.shape[0]
     width = roots.shape[2]
@@ -226,9 +233,10 @@
     for i, c in enumerate((c1, c3, c2)):
         to = left.at[pl.ds((i + 1) * rows, rows)]
         bring.append(pltpu.make_async_copy(c.at[pl.ds(0, rows)], to, sems.at[2 + i]))
-    for i, group in enumerate((t, 3 - t)):
-        cols = pl.ds(pl.multiple_of(group * width, width), width)
-        bring.append(pltpu.make_async_copy(right_hbm.at[slot, :, cols], roots.at[i], sems.at[5 + i]))
+    for i, (start, size, at) in enumerate(column_groups(t, width)):
+        source = right_hbm.at[slot, :, pl.ds(pl.multiple_of(start, 128), size)]
+        to = roots.at[at // width, :, pl.ds(at % width, size)]
+        bring.append(pltpu.make_async_copy(source, to, sems.at[5 + i]))
     for c in bring:
         c.start()
     for c in bring:
@@ -256,7 +264,7 @@
         scratch_shapes=[
             pltpu.VMEM(owned.shape, BF16),
             pltpu.VMEM((2, width, width), BF16),
-            pltpu.SemaphoreType.DMA((7,)),
+            pltpu.SemaphoreType.DMA((8,)),
         ],
         compiler_params=PARAMS,
         cost_estimate=cost(4 * full * full * width, 12 * full * full),
@@ -305,7 +313,7 @@
 
 
 def far_kernel(
-    t_ref, near, square, left, g2, c2, mine_ref, other_ref, sums_ref, roots, sems
+    t_ref, near, square, left, g2, c2, mine_ref, after_ref, before_ref, sums_ref, roots, sems
 ):
     bring = bring_right(c2, roots, sems)
     for c in bring:
@@ -318,10 +326,11 @@
     mine = near[0] + dot(part, roots[0])
     other = near[1] + dot(part, roots[1])
     mine_ref[...] = mine
-    other_ref[...] = other.astype(BF16)
+    after_ref[...] = other[:, : width // 2].astype(BF16)
+    before_ref[...] = other[:, width // 2 :].astype(BF16)
     total = jnp.sum(mine * mine, keepdims=True) + jnp.sum(other * other, keepdims=True)
     row = lax.broadcasted_iota(jnp.int32, sums_ref.shape, 0)
-    sums = jnp.where(row == t_ref[0] // 2, total, jnp.zeros(sums_ref.shape, F32))
+    sums = jnp.where(row == lax.rem(t_ref[0], 2), total, jnp.zeros(sums_ref.shape, F32))
     for slot in range(2):
         sums = jnp.where(row == 2 + slot, square[slot], sums)
     sums_ref[...] = sums
@@ -329,15 +338,17 @@
 
 def far_part(t, near, square, left, far, cut_far):
     _, full, width = near.shape
+    half = jax.ShapeDtypeStruct((full, width // 2), BF16)
     return pl.pallas_call(
         far_kernel,
         out_shape=(
             jax.ShapeDtypeStruct((full, width), F32),
-            jax.ShapeDtypeStruct((full, width), BF16),
+            half,
+            half,
             jax.ShapeDtypeStruct((8, 128), F32),
         ),
         in_specs=[SMEM_SPEC] + [VMEM_SPEC] * 4 + [HBM_SPEC],
-        out_specs=(VMEM_SPEC,) * 3,
+        out_specs=(VMEM_SPEC,) * 4,
         scratch_shapes=[pltpu.VMEM((2, width, width), BF16), pltpu.SemaphoreType.DMA((4,))],
         compiler_params=PARAMS,
         cost_estimate=cost(4 * full * full * width, 8 * full * full),
@@ -345,89 +356,90 @@
     )(t, near, square, left, far, cut_far)
 
 
-def scale_kernel(t_ref, mine, other, s0, s1, s2, s3, out_hbm, ready, sems):
-    _, _, here, height, width = ready.shape
+def scale_kernel(t_ref, mine, first, second, s0, s1, s2, s3, out_hbm, ready, halves, sems):
+    _, here, height, width = ready.shape
     rows = here * height
     t = t_ref[0]
     sums = s0[...] + s1[...] + s2[...] + s3[...]
-    first, second = (
+    grafts = [
         jnp.sqrt((sums[2 + slot : 3 + slot, 0:1] + EPSILON) / (sums[slot : slot + 1, 0:1] + EPSILON))
         for slot in range(2)
+    ]
+    even = lax.rem(t, 2) == 0
+    own_graft = jnp.where(even, grafts[0], grafts[1])
+    other_graft = jnp.where(even, grafts[1], grafts[0])
+    slot = lax.rem(t, 2)
+    half = width // 2
+    parts = (
+        (mine, t, own_graft, slot, ready, pl.ds(0, width)),
+        (first, t + 3, other_graft, 1 - slot, halves.at[0], pl.ds(0, half)),
+        (second, t + 1, other_graft, 1 - slot, halves.at[1], pl.ds(half, half)),
     )
     copies = []
-    for j, (raw, member) in enumerate(((mine, t), (other, 3 - t))):
-        slot = member // 2
-        graft = jnp.where(slot == 0, first, second)
+    for j, (raw, member, graft, slot, held, cols) in enumerate(parts):
         for i, k in enumerate((0, 1, 3, 2)):
             scaled = raw[i * rows : (i + 1) * rows, :].astype(F32) * graft
-            ready[j, i] = scaled.astype(BF16).reshape(here, height, width)
+            held[i] = scaled.astype(BF16).reshape(here, height, held.shape[3])
             s = lax.rem(member + 4 - k, 4)
-            to = out_hbm.at[pl.ds(s * here, here), slot]
-            copies.append(pltpu.make_async_copy(ready.at[j, i], to, sems.at[j, i]))
+            to = out_hbm.at[pl.ds(s * here, here), slot, :, cols]
+            copies.append(pltpu.make_async_copy(held.at[i], to, sems.at[j, i]))
             copies[-1].start()
     for c in copies:
         c.wait()
 
 
-def scale(t, mine, other, sums, shape):
+def scale(t, mine, first, second, sums, shape):
     owners, _, height, width = shape
+    here = owners // 4
     return pl.pallas_call(
         scale_kernel,
         out_shape=jax.ShapeDtypeStruct(shape, BF16),
-        in_specs=[SMEM_SPEC] + [VMEM_SPEC] * 6,
+        in_specs=[SMEM_SPEC] + [VMEM_SPEC] * 7,
         out_specs=HBM_SPEC,
         scratch_shapes=[
-            pltpu.VMEM((2, 4, owners // 4, height, width), BF16),
-            pltpu.SemaphoreType.DMA((2, 4)),
+            pltpu.VMEM((4, here, height, width), BF16),
+            pltpu.VMEM((2, 4, here, height, width // 2), BF16),
+            pltpu.SemaphoreType.DMA((3, 4)),
         ],
         compiler_params=PARAMS,
         cost_estimate=cost(0, 16 * owners * height * width),
         name="scale",
-    )(t, mine, other, *sums)
-
-
-def terms_kernel(t_ref, g0_hbm, g1, g3, g2, out_ref, own, turned, sems):
+    )(t, mine, first, second, *sums)
+
+
+def terms_kernel(t_ref, g0_hbm, g1, g3, g2, left_ref, right_ref, own, sems):
     t = t_ref[0]
-    bring = pltpu.make_async_copy(g0_hbm.at[:, t // 2], own, sems.at[0])
+    bring = pltpu.make_async_copy(g0_hbm.at[:, lax.rem(t, 2)], own, sems.at[0])
     bring.start()
     owners, height, rows = own.shape
     full = owners * height
     here = owners // 4
-    theirs = pl.ds(pl.multiple_of((3 - t) * here, here), here)
-
-    def turn(g):
-        turned[...] = g[...].reshape(full, rows).T
-
-    pl.when(lax.rem(t, 2) == 0)(lambda: turn(g1))
-    pl.when(lax.rem(t, 2) == 1)(lambda: turn(g3))
+    after = pl.ds(pl.multiple_of(lax.rem(t + 1, 4) * here, here), here)
+    turned = g1[...].reshape(full, rows).T
     bring.wait()
     term = None
     for k, g in ((0, own), (1, g1), (3, g3), (2, g2)):
         whole = g[...].reshape(full, rows)
-        part = dot(g[theirs].reshape(rows, rows), whole, 1, 1)
+        part = dot(g[after].reshape(rows, rows), whole, 1, 1)
         term = part if term is None else term + part
         s = lax.rem(t + 4 - k, 4)
         cols = pl.ds(pl.multiple_of(s * rows, rows), rows)
-        out_ref[1, :, cols] = dot(turned[...], whole).astype(BF16)
-    out_ref[0] = term.astype(BF16)
-
-
-def terms_across(t, owned, others):
+        right_ref[:, cols] = dot(turned, whole).astype(BF16)
+    left_ref[...] = term.astype(BF16)
+
+
+def neighbour_terms(t, owned, others):
     owners, _, height, rows = owned.shape
-    full = owners * height
+    out = jax.ShapeDtypeStruct((rows, owners * height), BF16)
     return pl.pallas_call(
         terms_kernel,
-        out_shape=jax.ShapeDtypeStruct((2, rows, full), BF16),
+        out_shape=(out, out),
         in_specs=[SMEM_SPEC, HBM_SPEC] + [VMEM_SPEC] * 3,
-        out_specs=VMEM_SPEC,
-        scratch_shapes=[
-            pltpu.VMEM((owners, height, rows), BF16),
-            pltpu.VMEM((rows, full), BF16),
-            pltpu.SemaphoreType.DMA((1,)),
-        ],
-        compiler_params=PARAMS,
-        cost_estimate=cost(4 * rows * full * full, 6 * rows * full),
-        name="terms_across",
+        out_specs=(VMEM_SPEC, VMEM_SPEC),
+        scratch_shapes=[pltpu.VMEM((owners, height, rows), BF16), pltpu.SemaphoreType.DMA((1,))],
+        compiler_params=PARAMS,
+        cost_estimate=cost(4 * rows * (owners * height) ** 2, 6 * rows * owners * height),
+        name="neighbour_terms",
     )(t, owned, *others)
 
 
@@ -436,7 +448,7 @@
     rows, full = left_ref.shape
     here = own.shape[0] // 4
     mine = pl.ds(pl.multiple_of(t * here, here), here)
-    bring = pltpu.make_async_copy(g0_hbm.at[:, t // 2], own, sems.at[0])
+    bring = pltpu.make_async_copy(g0_hbm.at[:, lax.rem(t, 2)], own, sems.at[0])
     bring.start()
     bring.wait()
     turned = own[...].reshape(full, rows).T
@@ -454,7 +466,7 @@
 def statistics(t, owned, others, left_stat, right_stat):
     _, rows, full = left_stat.shape
     owners, _, height, width = owned.shape
-    slot_spec = pl.BlockSpec((None, rows, full), lambda i, t_ref: (t_ref[0] // 2, 0, 0))
+    slot_spec = pl.BlockSpec((None, rows, full), lambda i, t_ref: (lax.rem(t_ref[0], 2), 0, 0))
     shape = jax.ShapeDtypeStruct(left_stat.shape, F32)
     return pl.pallas_call(
         stats_kernel,
@@ -472,14 +484,14 @@
     )(t, owned, *others, left_stat, right_stat)
 
 
-def blend_kernel(t_ref, terms, left_ref, right_ref, _, __, new_left_ref, new_right_ref):
-    new_left_ref[...] = DECAY * left_ref[...] + (1.0 - DECAY) * terms[0].astype(F32)
-    new_right_ref[...] = DECAY * right_ref[...] + (1.0 - DECAY) * terms[1].astype(F32)
+def blend_kernel(t_ref, left_term, right_term, left_ref, right_ref, _, __, new_left_ref, new_right_ref):
+    new_left_ref[...] = DECAY * left_ref[...] + (1.0 - DECAY) * left_term[...].astype(F32)
+    new_right_ref[...] = DECAY * right_ref[...] + (1.0 - DECAY) * right_term[...].astype(F32)
 
 
 def blend(t, terms, left_stat, right_stat, done):
     _, rows, full = left_stat.shape
-    slot_spec = pl.BlockSpec((None, rows, full), lambda i, t_ref: (1 - t_ref[0] // 2, 0, 0))
+    slot_spec = pl.BlockSpec((None, rows, full), lambda i, t_ref: (1 - lax.rem(t_ref[0], 2), 0, 0))
     shape = jax.ShapeDtypeStruct(left_stat.shape, F32)
     return pl.pallas_call(
         blend_kernel,
@@ -487,24 +499,19 @@
         grid_spec=pltpu.PrefetchScalarGridSpec(
             num_scalar_prefetch=1,
             grid=(1,),
-            in_specs=[VMEM_SPEC] + [slot_spec] * 2 + [HBM_SPEC] * 2,
+            in_specs=[VMEM_SPEC] * 2 + [slot_spec] * 2 + [HBM_SPEC] * 2,
             out_specs=(slot_spec, slot_spec),
         ),
-        input_output_aliases={4: 0, 5: 1},
+        input_output_aliases={5: 0, 6: 1},
         compiler_params=pltpu.CompilerParams(vmem_limit_bytes=32 * 1024 * 1024),
         cost_estimate=cost(4 * rows * full, 18 * rows * full),
         name="blend",
-    )(t, terms, left_stat, right_stat, *done)
+    )(t, *terms, left_stat, right_stat, *done)
 
 
 def around(x, k):
     n = lax.axis_size("tensor")
     return lax.ppermute(x, "tensor", [(i, (i + k) % n) for i in range(n)])
-
-
-def across(x):
-    n = lax.axis_size("tensor")
-    return lax.ppermute(x, "tensor", [(i, n - 1 - i) for i in range(n)])
 
 
 def exchange(x):
@@ -518,18 +525,21 @@
     cut_below, cut_far, cut_above = (around(c, k) for c, k in zip(cuts, (1, 2, 3)))
     owned = exchange(routed)
     owned, token = lax.optimization_barrier((owned, hold(cut_below, cut_above)))
-    below, far, above = (around(x, k) for x, k in zip(select(t, owned), (1, 2, 3)))
+    for_neighbours, for_opposite = select(t, owned)
+    below, above = around(for_neighbours, 1), around(for_neighbours, -1)
     cuts = (cut_below, cut_above, cut_far)
     raw, square, left = own_part(t, token, left_root, right_root, cuts, owned)
+    raw, for_opposite = lax.optimization_barrier((raw, for_opposite))
+    far = around(for_opposite, 2)
     raw = near_part(raw, left, below, above, cut_below, cut_above)
-    mine, other, sums = far_part(t, raw, square, left, far, cut_far)
-    other = across(other)
+    mine, after, before, sums = far_part(t, raw, square, left, far, cut_far)
+    first, second = around(after, 1), around(before, -1)
     everyone = [sums] + [around(sums, k) for k in (1, 2, 3)]
     others = (below, above, far)
-    terms = terms_across(t, owned, others)
+    terms = neighbour_terms(t, owned, others)
     everyone, terms = lax.optimization_barrier((everyone, terms))
-    terms = across(terms)
-    returned = exchange(scale(t, mine, other, everyone, routed.shape))
+    terms = around(terms[0], 1), around(terms[1], -1)
+    returned = exchange(scale(t, mine, first, second, everyone, routed.shape))
     done = statistics(t, owned, others, left_stat, right_stat)
     new_left, new_right = blend(t, terms, left_stat, right_stat, done)
     return (new_left, new_right, collect(block_owner, returned))

time: 136 us -> 133 us (0.978)
  starting transfers between devices: 45.5 us -> 42.9 us
    ppermute x2 -> x0, waiting for transfers between devices: 14.5 us -> none  [across(): return lax.ppermute(x, 'tensor', [(i, n - 1 - i) for i in range(n)])]
    all_to_all x2, waiting for transfers between devices: 24.4 us -> 35.1 us  [exchange(): return lax.all_to_all(x, 'fsdp', split_axis=0, concat_axis=0, tiled=True)]
    ppermute x2 -> x0, starting transfers between devices: 4.13 us -> none  [across(): return lax.ppermute(x, 'tensor', [(i, n - 1 - i) for i in range(n)])]
    ppermute x9 -> x13, starting transfers between devices: 11.2 us -> 15.2 us  [around(): return lax.ppermute(x, 'tensor', [(i, (i + k) % n) for i in range(n)])]
    ppermute x9 -> x13, waiting for transfers between devices: 13.6 us -> 16.1 us  [around(): return lax.ppermute(x, 'tensor', [(i, (i + k) % n) for i in range(n)])]
    all_to_all x2, starting transfers between devices: 30.1 us -> 27.7 us  [exchange(): return lax.all_to_all(x, 'fsdp', split_axis=0, concat_axis=0, tiled=True)]
    unnamed x34 -> x36, local copies, waits for them, and re-layouts: 10 us -> 10.6 us
  transfers between devices with their start and end apart: 13 -> 15, of which waited for: 8 -> 9; matrix products, arithmetic and copies ran while one was open for 0% -> 0% of each run, Pallas kernels for 12% -> 13%
where the time goes in v5:
time: 133 us; the launch traced here: 131 us
  waiting for transfers between devices  51.2 us (38%)
  starting transfers between devices  42.9 us (32%)
  Pallas kernels  25.8 us (19%)
  local copies, waits for them, and re-layouts  10.6 us (8%)
    all_to_all x2, waiting for transfers between devices, exchange(): return lax.all_to_all(x, 'fsdp', split_axis=0, concat_axis=0, tiled=True)  35.1 us
    all_to_all x2, starting transfers between devices, exchange(): return lax.all_to_all(x, 'fsdp', split_axis=0, concat_axis=0, tiled=True)  27.7 us
    ppermute x13, waiting for transfers between devices, around(): return lax.ppermute(x, 'tensor', [(i, (i + k) % n) for i in range(n)])  16.1 us
    ppermute x13, starting transfers between devices, around(): return lax.ppermute(x, 'tensor', [(i, (i + k) % n) for i in range(n)])  15.2 us
    unnamed x36, local copies, waits for them, and re-layouts  10.6 us
    pallas_call x1, Pallas kernels, near_part(): pl.pallas_call(near_kernel, out_shape=jax.ShapeDtypeStruct(own.shape, F32...  3.9 us
    pallas_call x1, Pallas kernels, statistics(): pl.pallas_call(stats_kernel, out_shape=(shape, shape), grid_spec=pltpu.Pr...  3.8 us
    pallas_call x1, Pallas kernels, route(): pl.pallas_call(route_kernel, out_shape=(jax.ShapeDtypeStruct(shape, gradi...  3.68 us
  transfers between devices with their start and end apart: 15, of which 9 were waited for; matrix products, arithmetic and copies ran while one was open for 0% of the time, Pallas kernels for 13%

profile of v5, /device:TPU:1, one launch (start us, length us, event | category | flops | bytes accessed | tf_op | source)
XLA Modules:
  0.0 131.4 jit_solution(3462928883371784082)
XLA Ops:
  0.6 3.7 %route.1 = (bf16[64,2,16,256]{3,2,1,0:T(8,128)(2,1)}, bf16[384,1024]{1,0:T(8,128)(2,1)}, bf16[384,1024]{1,0:T(8,128)(2,1)}, bf16[384,1024]{1,0:T(8,128)(2,1)}) custom-call(s32[1]{0:T(128)} %bitcast.t_ref, s32[64]{0:T(128)} %owner_hbm.3, bf16[64,16,256]{2,1,0:T(8,128)(2,1)} %grad_hbm.1, bf16[2,256,1024]{2,1,0:T(8,128)(2,1)} %left_hbm.3, ...), custom_call_target="tpu_custom_call" | custom-call | bytes 786432 | tf_op jit(solution)/shard_map/route/pallas_call | solution.py:96
  4.3 2.1 %collective-permute-start = (bf16[384,1024]{1,0:T(8,128)(2,1)}, bf16[384,1024]{1,0:T(8,128)(2,1)S(1)}, u32[]{:S(2)}, u32[]{:S(2)}) collective-permute-start(bf16[384,1024]{1,0:T(8,128)(2,1)} %get-tuple-element.33), channel_id=1, source_target_pairs={{0,1},{1,2},{2,3},{3,0},{4,5},{5,6},{6,7},{7,4},{8,9},{9,10},{10,1... | collective-permute-start | bytes 2359304 | tf_op jit(solution)/shard_map/ppermute | solution.py:514
  6.4 1.4 %collective-permute-start.1 = (bf16[384,1024]{1,0:T(8,128)(2,1)}, bf16[384,1024]{1,0:T(8,128)(2,1)}, u32[]{:S(2)}, u32[]{:S(2)}) collective-permute-start(bf16[384,1024]{1,0:T(8,128)(2,1)} %get-tuple-element.34), channel_id=1, source_target_pairs={{0,3},{1,0},{2,1},{3,2},{4,7},{5,4},{6,5},{7,6},{8,11},{9,8},{10,9... | collective-permute-start | bytes 2359304 | tf_op jit(solution)/shard_map/ppermute | solution.py:514
  7.8 13.2 %all-to-all-start = ((bf16[64,2,16,256]{3,2,1,0:T(8,128)(2,1)}), bf16[64,2,16,256]{3,2,1,0:T(8,128)(2,1)}, u32[]{:S(2)}, u32[]{:S(2)}) async-start(bf16[64,2,16,256]{3,2,1,0:T(8,128)(2,1)} %get-tuple-element.32), calls=%async_computation | async-start | bytes 2097152 | tf_op jit(solution)/shard_map/all_to_all | solution.py:518
  21.0 1.6 %collective-permute-start.2 = (bf16[384,1024]{1,0:T(8,128)(2,1)}, bf16[384,1024]{1,0:T(8,128)(2,1)}, u32[]{:S(2)}, u32[]{:S(2)}) collective-permute-start(bf16[384,1024]{1,0:T(8,128)(2,1)} %get-tuple-element.36), channel_id=1, source_target_pairs={{0,2},{1,3},{2,0},{3,1},{4,6},{5,7},{6,4},{7,5},{8,10},{9,11},{10,... | collective-permute-start | bytes 2359304 | tf_op jit(solution)/shard_map/ppermute | solution.py:514
  22.6 0.3 collective-permute-done.a.c1
  22.9 1.6 %collective-permute-done.1.b.c3 = bf16[384,1024]{1,0:T(8,128)(2,1)} collective-permute-done((bf16[384,1024]{1,0:T(8,128)(2,1)}, bf16[384,1024]{1,0:T(8,128)(2,1)}, u32[]{:S(2)}, u32[]{:S(2)}) %collective-permute-start.1) | collective-permute-done | bytes 786464 | tf_op jit(solution)/shard_map/ppermute | solution.py:514
  24.5 0.6 hold.1.token
  25.1 23.8 %all-to-all-done.both_hbm.g0_hbm = bf16[64,2,16,256]{3,2,1,0:T(8,128)(2,1)} async-done(((bf16[64,2,16,256]{3,2,1,0:T(8,128)(2,1)}), bf16[64,2,16,256]{3,2,1,0:T(8,128)(2,1)}, u32[]{:S(2)}, u32[]{:S(2)}) %all-to-all-start) | async-done | bytes 1048608 | tf_op jit(solution)/shard_map/all_to_all | solution.py:518
  48.9 1.5 %select.1 = (bf16[64,16,256]{2,1,0:T(8,128)(2,1)S(1)}, bf16[64,16,256]{2,1,0:T(8,128)(2,1)S(1)}) custom-call(s32[1]{0:T(128)} %bitcast.t_ref, bf16[64,2,16,256]{3,2,1,0:T(8,128)(2,1)} %all-to-all-done.both_hbm.g0_hbm), custom_call_target="tpu_custom_call" | custom-call | bytes 2097152 | tf_op jit(solution)/shard_map/select/pallas_call | solution.py:179
  50.4 1.3 %collective-permute-start.4 = (bf16[64,16,256]{2,1,0:T(8,128)(2,1)S(1)}, bf16[64,16,256]{2,1,0:T(8,128)(2,1)S(1)}, u32[]{:S(2)}, u32[]{:S(2)}) collective-permute-start(bf16[64,16,256]{2,1,0:T(8,128)(2,1)S(1)} %get-tuple-element.42), channel_id=1, source_target_pairs={{0,3},{1,0},{2,1},{3,2},{4,7},{5,4},{6,5},{7,6},{8,11},{9,8},{10,9... | collective-permute-start | bytes 1572872 | tf_op jit(solution)/shard_map/ppermute | solution.py:514
  51.7 0.2 collective-permute-start.3
  51.9 1.2 copy-done.3
  53.1 1.2 copy-done.4
  54.4 1.1 copy-done.6
  55.5 0.7 copy-done.14
  56.2 3.0 %own_part.1 = (f32[2,1024,256]{2,1,0:T(8,128)S(1)}, f32[2,8,128]{2,1,0:T(8,128)S(1)}, bf16[1024,1024]{1,0:T(8,128)(2,1)S(1)}) custom-call(s32[1]{0:T(128)} %bitcast.t_ref, f32[8,128]{1,0:T(8,128)S(1)} %copy-done.14, bf16[2,256,1024]{2,1,0:T(8,128)(2,1)S(1)} %copy-done.3, bf16[2,256,1024]{2,1,0:T(8,128)(2,1)S(1)} %copy-done.4, ...), custom_call_target="tpu_custom_call" | custom-call | flops 1073741824 | bytes 12582912 | tf_op jit(solution)/shard_map/own_part/pallas_call | solution.py:255
  59.2 1.6 %collective-permute-start.5 = (bf16[64,16,256]{2,1,0:T(8,128)(2,1)S(1)}, bf16[64,16,256]{2,1,0:T(8,128)(2,1)S(1)}, u32[]{:S(2)}, u32[]{:S(2)}) collective-permute-start(bf16[64,16,256]{2,1,0:T(8,128)(2,1)S(1)} %get-tuple-element.44), channel_id=1, source_target_pairs={{0,2},{1,3},{2,0},{3,1},{4,6},{5,7},{6,4},{7,5},{8,10},{9,11},{10,... | collective-permute-start | bytes 1572872 | tf_op jit(solution)/shard_map/ppermute | solution.py:514
  60.8 1.7 %collective-permute-done.4.g3 = bf16[64,16,256]{2,1,0:T(8,128)(2,1)S(1)} collective-permute-done((bf16[64,16,256]{2,1,0:T(8,128)(2,1)S(1)}, bf16[64,16,256]{2,1,0:T(8,128)(2,1)S(1)}, u32[]{:S(2)}, u32[]{:S(2)}) %collective-permute-start.4) | collective-permute-done | bytes 524320 | tf_op jit(solution)/shard_map/ppermute | solution.py:514
  62.5 3.1 %collective-permute-done.3.g1 = bf16[64,16,256]{2,1,0:T(8,128)(2,1)S(1)} collective-permute-done((bf16[64,16,256]{2,1,0:T(8,128)(2,1)S(1)}, bf16[64,16,256]{2,1,0:T(8,128)(2,1)S(1)}, u32[]{:S(2)}, u32[]{:S(2)}) %collective-permute-start.3) | collective-permute-done | bytes 524320 | tf_op jit(solution)/shard_map/ppermute | solution.py:514
  65.6 3.9 %near_part.1.near = f32[2,1024,256]{2,1,0:T(8,128)S(1)} custom-call(f32[2,1024,256]{2,1,0:T(8,128)S(1)} %get-tuple-element.40.own, bf16[1024,1024]{1,0:T(8,128)(2,1)S(1)} %get-tuple-element.41.left, bf16[64,16,256]{2,1,0:T(8,128)(2,1)S(1)} %collective-permute-done.3.g1, bf16[64,16,256]{2,1,0:T(8,128)(2,1)S(1)} %collective-permute-done.4.g3, ...), custom_call_target="tpu_custom_call" | custom-call | flops 1610612736 | bytes 10485760 | tf_op jit(solution)/shard_map/near_part/pallas_call | solution.py:299
  69.6 5.5 %collective-permute-done.5.g2 = bf16[64,16,256]{2,1,0:T(8,128)(2,1)S(1)} collective-permute-done((bf16[64,16,256]{2,1,0:T(8,128)(2,1)S(1)}, bf16[64,16,256]{2,1,0:T(8,128)(2,1)S(1)}, u32[]{:S(2)}, u32[]{:S(2)}) %collective-permute-start.5) | collective-permute-done | bytes 524320 | tf_op jit(solution)/shard_map/ppermute | solution.py:514
  75.0 2.6 %far_part.1 = (f32[1024,256]{1,0:T(8,128)S(1)}, bf16[1024,128]{1,0:T(8,128)(2,1)S(1)}, bf16[1024,128]{1,0:T(8,128)(2,1)S(1)}, f32[8,128]{1,0:T(8,128)S(1)}) custom-call(s32[1]{0:T(128)} %bitcast.t_ref, f32[2,1024,256]{2,1,0:T(8,128)S(1)} %near_part.1.near, f32[2,8,128]{2,1,0:T(8,128)S(1)} %get-tuple-element.43.square, ...), custom_call_target="tpu_custom_call" | custom-call | flops 1073741824 | bytes 8388608 | tf_op jit(solution)/shard_map/far_part/pallas_call | solution.py:342
  77.7 0.1 collective-permute-start.11
  77.8 2.7 %collective-permute-start.12 = (bf16[1024,128]{1,0:T(8,128)(2,1)S(1)}, bf16[1024,128]{1,0:T(8,128)(2,1)S(1)}, u32[]{:S(2)}, u32[]{:S(2)}) collective-permute-start(bf16[1024,128]{1,0:T(8,128)(2,1)S(1)} %get-tuple-element.56), channel_id=1, source_target_pairs={{0,3},{1,0},{2,1},{3,2},{4,7},{5,4},{6,5},{7,6},{8,11},{9,8},{10,9... | collective-permute-start | bytes 786440 | tf_op jit(solution)/shard_map/ppermute | solution.py:514
  80.4 0.2 collective-permute-start.8
  80.6 0.6 collective-permute-start.7
  81.3 0.6 collective-permute-start.6
  81.9 2.3 %neighbour_terms.1 = (bf16[256,1024]{1,0:T(8,128)(2,1)S(1)}, bf16[256,1024]{1,0:T(8,128)(2,1)S(1)}) custom-call(s32[1]{0:T(128)} %bitcast.t_ref, bf16[64,2,16,256]{3,2,1,0:T(8,128)(2,1)} %all-to-all-done.both_hbm.g0_hbm, bf16[64,16,256]{2,1,0:T(8,128)(2,1)S(1)} %collective-permute-done.3.g1, bf16[64,16,256]{2,1,0:T(8,128)(2,1)S(1)} %collective-permute-done.4.g3, ...), custom_call_target="tpu_custom_call" | custom-call | flops 1073741824 | bytes 1572864 | tf_op jit(solution)/shard_map/neighbour_terms/pallas_call | solution.py:434
  84.3 0.8 copy-done.16
  85.1 0.8 copy-done.17
  85.9 0.0 collective-permute-done.11.first
  85.9 0.0 collective-permute-done.12.second
  85.9 0.0 copy-start
  85.9 1.2 scale.1
  87.1 14.5 %all-to-all-start.1 = ((bf16[64,2,16,256]{3,2,1,0:T(8,128)(2,1)}), bf16[64,2,16,256]{3,2,1,0:T(8,128)(2,1)S(1)}, u32[]{:S(2)}, u32[]{:S(2)}) async-start(bf16[64,2,16,256]{3,2,1,0:T(8,128)(2,1)} %scale.1), calls=%async_computation.1 | async-start | bytes 2097152 | tf_op jit(solution)/shard_map/all_to_all | solution.py:518
  101.6 1.0 collective-permute-start.9
  102.6 1.7 %collective-permute-start.10 = (bf16[256,1024]{1,0:T(8,128)(2,1)}, bf16[256,1024]{1,0:T(8,128)(2,1)S(1)}, u32[]{:S(2)}, u32[]{:S(2)}) collective-permute-start(bf16[256,1024]{1,0:T(8,128)(2,1)} %copy-done.16), channel_id=1, source_target_pairs={{0,3},{1,0},{2,1},{3,2},{4,7},{5,4},{6,5},{7,6},{8,11},{9,8},{10,9... | collective-permute-start | bytes 1572872 | tf_op jit(solution)/shard_map/ppermute | solution.py:514
  104.3 1.6 %copy-done.1 = f32[2,256,1024]{2,1,0:T(8,128)S(1)} copy-done((f32[2,256,1024]{2,1,0:T(8,128)S(1)}, f32[2,256,1024]{2,1,0:T(8,128)}, u32[]{:S(2)}) %copy-start.1) | copy-done | bytes 2097176
  105.9 1.0 copy-done.9
  107.0 1.0 copy-done.11
  108.0 1.0 copy-done.13
  109.1 3.8 %statistics.1 = (f32[2,256,1024]{2,1,0:T(8,128)}, f32[2,256,1024]{2,1,0:T(8,128)}) custom-call(s32[1]{0:T(128)} %bitcast.t_ref, bf16[64,2,16,256]{3,2,1,0:T(8,128)(2,1)} %all-to-all-done.both_hbm.g0_hbm, bf16[64,16,256]{2,1,0:T(8,128)(2,1)S(1)} %copy-done.11, bf16[64,16,256]{2,1,0:T(8,128)(2,1)S(1)} %copy-done.9, bf16[64,16,256]{2,1,0:T(8,128)(2,1)S(1)} %copy-done.13, ...), custom_call_target="tpu_custom_call" | custom-call | flops 1073741824 | bytes 3145728 | tf_op jit(solution)/shard_map/statistics/pallas_call | solution.py:471
  112.9 3.3 %collective-permute-done.9.left_term = bf16[256,1024]{1,0:T(8,128)(2,1)S(1)} collective-permute-done((bf16[256,1024]{1,0:T(8,128)(2,1)}, bf16[256,1024]{1,0:T(8,128)(2,1)S(1)}, u32[]{:S(2)}, u32[]{:S(2)}) %collective-permute-start.9) | collective-permute-done | bytes 524320 | tf_op jit(solution)/shard_map/ppermute | solution.py:514
  116.1 0.6 collective-permute-done.10.right_term
  116.7 1.5 %blend.1 = (f32[2,256,1024]{2,1,0:T(8,128)}, f32[2,256,1024]{2,1,0:T(8,128)}) custom-call(s32[1]{0:T(128)} %bitcast.t_ref, bf16[256,1024]{1,0:T(8,128)(2,1)S(1)} %collective-permute-done.9.left_term, bf16[256,1024]{1,0:T(8,128)(2,1)S(1)} %collective-permute-done.10.right_term, ...), custom_call_target="tpu_custom_call", output_to_operand_aliasing={{0}: (5, {}), {1}: (6, {})} | custom-call | flops 1048576 | bytes 4718592 | tf_op jit(solution)/shard_map/blend/pallas_call | solution.py:496
  118.3 11.3 %all-to-all-done.1.slots_hbm = bf16[64,2,16,256]{3,2,1,0:T(8,128)(2,1)S(1)} async-done(((bf16[64,2,16,256]{3,2,1,0:T(8,128)(2,1)}), bf16[64,2,16,256]{3,2,1,0:T(8,128)(2,1)S(1)}, u32[]{:S(2)}, u32[]{:S(2)}) %all-to-all-start.1) | async-done | bytes 1048608 | tf_op jit(solution)/shard_map/all_to_all | solution.py:518
  129.6 1.7 %collect.1 = bf16[64,16,256]{2,1,0:T(8,128)(2,1)} custom-call(s32[64]{0:T(128)S(1)} %copy-done.15, bf16[64,2,16,256]{3,2,1,0:T(8,128)(2,1)S(1)} %all-to-all-done.1.slots_hbm), custom_call_target="tpu_custom_call" | custom-call | bytes 1572864 | tf_op jit(solution)/shard_map/collect/pallas_call | solution.py:143
  (29 shorter events, 0.1 us)
Async XLA Ops:
  4.3 18.6 %collective-permute-start = (bf16[384,1024]{1,0:T(8,128)(2,1)}, bf16[384,1024]{1,0:T(8,128)(2,1)S(1)}, u32[]{:S(2)}, u32[]{:S(2)}) collective-permute-start(bf16[384,1024]{1,0:T(8,128)(2,1)} %get-tuple-element.33), channel_id=1, source_target_pairs={{0,1},{1,2},{2,3},{3,0},{4,5},{5,6},{6,7},{7,4},{8,9},{9,10},{10,1... | collective-permute-start | bytes 2359304 | tf_op jit(solution)/shard_map/ppermute | solution.py:514
  6.4 18.1 %collective-permute-start.1 = (bf16[384,1024]{1,0:T(8,128)(2,1)}, bf16[384,1024]{1,0:T(8,128)(2,1)}, u32[]{:S(2)}, u32[]{:S(2)}) collective-permute-start(bf16[384,1024]{1,0:T(8,128)(2,1)} %get-tuple-element.34), channel_id=1, source_target_pairs={{0,3},{1,0},{2,1},{3,2},{4,7},{5,4},{6,5},{7,6},{8,11},{9,8},{10,9... | collective-permute-start | bytes 2359304 | tf_op jit(solution)/shard_map/ppermute | solution.py:514
  7.8 41.1 %all-to-all-start = ((bf16[64,2,16,256]{3,2,1,0:T(8,128)(2,1)}), bf16[64,2,16,256]{3,2,1,0:T(8,128)(2,1)}, u32[]{:S(2)}, u32[]{:S(2)}) async-start(bf16[64,2,16,256]{3,2,1,0:T(8,128)(2,1)} %get-tuple-element.32), calls=%async_computation | async-start | bytes 2097152 | tf_op jit(solution)/shard_map/all_to_all | solution.py:518
  21.0 30.9 %collective-permute-start.2 = (bf16[384,1024]{1,0:T(8,128)(2,1)}, bf16[384,1024]{1,0:T(8,128)(2,1)}, u32[]{:S(2)}, u32[]{:S(2)}) collective-permute-start(bf16[384,1024]{1,0:T(8,128)(2,1)} %get-tuple-element.36), channel_id=1, source_target_pairs={{0,2},{1,3},{2,0},{3,1},{4,6},{5,7},{6,4},{7,5},{8,10},{9,11},{10,... | collective-permute-start | bytes 2359304 | tf_op jit(solution)/shard_map/ppermute | solution.py:514
  22.9 1.6 %copy-start.5 = (bf16[384,1024]{1,0:T(8,128)(2,1)}, bf16[384,1024]{1,0:T(8,128)(2,1)S(1)}, u32[]{:S(2)}) copy-start(bf16[384,1024]{1,0:T(8,128)(2,1)S(1)} %collective-permute-done.a.c1) | copy-start | bytes 2359300
  48.9 16.8 %copy-start.7 = (bf16[384,1024]{1,0:T(8,128)(2,1)S(1)}, bf16[384,1024]{1,0:T(8,128)(2,1)}, u32[]{:S(2)}) copy-start(bf16[384,1024]{1,0:T(8,128)(2,1)} %copy-done.5) | copy-start | bytes 2359300
  50.4 12.1 %collective-permute-start.4 = (bf16[64,16,256]{2,1,0:T(8,128)(2,1)S(1)}, bf16[64,16,256]{2,1,0:T(8,128)(2,1)S(1)}, u32[]{:S(2)}, u32[]{:S(2)}) collective-permute-start(bf16[64,16,256]{2,1,0:T(8,128)(2,1)S(1)} %get-tuple-element.42), channel_id=1, source_target_pairs={{0,3},{1,0},{2,1},{3,2},{4,7},{5,4},{6,5},{7,6},{8,11},{9,8},{10,9... | collective-permute-start | bytes 1572872 | tf_op jit(solution)/shard_map/ppermute | solution.py:514
  51.7 13.9 %collective-permute-start.3 = (bf16[64,16,256]{2,1,0:T(8,128)(2,1)S(1)}, bf16[64,16,256]{2,1,0:T(8,128)(2,1)S(1)}, u32[]{:S(2)}, u32[]{:S(2)}) collective-permute-start(bf16[64,16,256]{2,1,0:T(8,128)(2,1)S(1)} %get-tuple-element.42), channel_id=1, source_target_pairs={{0,1},{1,2},{2,3},{3,0},{4,5},{5,6},{6,7},{7,4},{8,9},{9,10},{10,1... | collective-permute-start | bytes 1572872 | tf_op jit(solution)/shard_map/ppermute | solution.py:514
  51.9 1.2 copy-start.3
  53.1 1.2 copy-start.4
  54.4 1.1 copy-start.6
  55.5 0.7 copy-start.14
  59.2 15.9 %collective-permute-start.5 = (bf16[64,16,256]{2,1,0:T(8,128)(2,1)S(1)}, bf16[64,16,256]{2,1,0:T(8,128)(2,1)S(1)}, u32[]{:S(2)}, u32[]{:S(2)}) collective-permute-start(bf16[64,16,256]{2,1,0:T(8,128)(2,1)S(1)} %get-tuple-element.44), channel_id=1, source_target_pairs={{0,2},{1,3},{2,0},{3,1},{4,6},{5,7},{6,4},{7,5},{8,10},{9,11},{10,... | collective-permute-start | bytes 1572872 | tf_op jit(solution)/shard_map/ppermute | solution.py:514
  62.5 19.4 %copy-start.8 = (bf16[64,16,256]{2,1,0:T(8,128)(2,1)}, bf16[64,16,256]{2,1,0:T(8,128)(2,1)S(1)}, u32[]{:S(2)}) copy-start(bf16[64,16,256]{2,1,0:T(8,128)(2,1)S(1)} %collective-permute-done.4.g3) | copy-start | bytes 1572868
  65.6 16.3 %copy-start.10 = (bf16[64,16,256]{2,1,0:T(8,128)(2,1)}, bf16[64,16,256]{2,1,0:T(8,128)(2,1)S(1)}, u32[]{:S(2)}) copy-start(bf16[64,16,256]{2,1,0:T(8,128)(2,1)S(1)} %collective-permute-done.3.g1) | copy-start | bytes 1572868
  75.0 6.9 %copy-start.12 = (bf16[64,16,256]{2,1,0:T(8,128)(2,1)}, bf16[64,16,256]{2,1,0:T(8,128)(2,1)S(1)}, u32[]{:S(2)}) copy-start(bf16[64,16,256]{2,1,0:T(8,128)(2,1)S(1)} %collective-permute-done.5.g2) | copy-start | bytes 1572868
  77.7 8.2 %collective-permute-start.11 = (bf16[1024,128]{1,0:T(8,128)(2,1)S(1)}, bf16[1024,128]{1,0:T(8,128)(2,1)S(1)}, u32[]{:S(2)}, u32[]{:S(2)}) collective-permute-start(bf16[1024,128]{1,0:T(8,128)(2,1)S(1)} %get-tuple-element.55), channel_id=1, source_target_pairs={{0,1},{1,2},{2,3},{3,0},{4,5},{5,6},{6,7},{7,4},{8,9},{9,10},{10,1... | collective-permute-start | bytes 786440 | tf_op jit(solution)/shard_map/ppermute | solution.py:514
  77.8 8.1 %collective-permute-start.12 = (bf16[1024,128]{1,0:T(8,128)(2,1)S(1)}, bf16[1024,128]{1,0:T(8,128)(2,1)S(1)}, u32[]{:S(2)}, u32[]{:S(2)}) collective-permute-start(bf16[1024,128]{1,0:T(8,128)(2,1)S(1)} %get-tuple-element.56), channel_id=1, source_target_pairs={{0,3},{1,0},{2,1},{3,2},{4,7},{5,4},{6,5},{7,6},{8,11},{9,8},{10,9... | collective-permute-start | bytes 786440 | tf_op jit(solution)/shard_map/ppermute | solution.py:514
  80.4 5.4 %collective-permute-start.8 = (f32[8,128]{1,0:T(8,128)S(1)}, f32[8,128]{1,0:T(8,128)S(1)}, u32[]{:S(2)}, u32[]{:S(2)}) collective-permute-start(f32[8,128]{1,0:T(8,128)S(1)} %get-tuple-element.57.s0), channel_id=1, source_target_pairs={{0,3},{1,0},{2,1},{3,2},{4,7},{5,4},{6,5},{7,6},{8,11},{9,8},{10,9... | collective-permute-start | bytes 12296 | tf_op jit(solution)/shard_map/ppermute | solution.py:514
  80.6 5.2 %collective-permute-start.7 = (f32[8,128]{1,0:T(8,128)S(1)}, f32[8,128]{1,0:T(8,128)S(1)}, u32[]{:S(2)}, u32[]{:S(2)}) collective-permute-start(f32[8,128]{1,0:T(8,128)S(1)} %get-tuple-element.57.s0), channel_id=1, source_target_pairs={{0,2},{1,3},{2,0},{3,1},{4,6},{5,7},{6,4},{7,5},{8,10},{9,11},{10,... | collective-permute-start | bytes 12296 | tf_op jit(solution)/shard_map/ppermute | solution.py:514
  81.3 4.6 %collective-permute-start.6 = (f32[8,128]{1,0:T(8,128)S(1)}, f32[8,128]{1,0:T(8,128)S(1)}, u32[]{:S(2)}, u32[]{:S(2)}) collective-permute-start(f32[8,128]{1,0:T(8,128)S(1)} %get-tuple-element.57.s0), channel_id=1, source_target_pairs={{0,1},{1,2},{2,3},{3,0},{4,5},{5,6},{6,7},{7,4},{8,9},{9,10},{10,1... | collective-permute-start | bytes 12296 | tf_op jit(solution)/shard_map/ppermute | solution.py:514
  84.3 0.8 copy-start.16
  85.1 0.8 copy-start.17
  85.9 18.4 %copy-start = (f32[2,256,1024]{2,1,0:T(8,128)S(1)}, f32[2,256,1024]{2,1,0:T(8,128)}, u32[]{:S(2)}) copy-start(f32[2,256,1024]{2,1,0:T(8,128)} %left_ref.3) | copy-start | bytes 6291460
  87.1 42.5 %all-to-all-start.1 = ((bf16[64,2,16,256]{3,2,1,0:T(8,128)(2,1)}), bf16[64,2,16,256]{3,2,1,0:T(8,128)(2,1)S(1)}, u32[]{:S(2)}, u32[]{:S(2)}) async-start(bf16[64,2,16,256]{3,2,1,0:T(8,128)(2,1)} %scale.1), calls=%async_computation.1 | async-start | bytes 2097152 | tf_op jit(solution)/shard_map/all_to_all | solution.py:518
  101.6 14.5 %collective-permute-start.9 = (bf16[256,1024]{1,0:T(8,128)(2,1)}, bf16[256,1024]{1,0:T(8,128)(2,1)S(1)}, u32[]{:S(2)}, u32[]{:S(2)}) collective-permute-start(bf16[256,1024]{1,0:T(8,128)(2,1)} %copy-done.17), channel_id=1, source_target_pairs={{0,1},{1,2},{2,3},{3,0},{4,5},{5,6},{6,7},{7,4},{8,9},{9,10},{10,1... | collective-permute-start | bytes 1572872 | tf_op jit(solution)/shard_map/ppermute | solution.py:514
  102.6 14.1 %collective-permute-start.10 = (bf16[256,1024]{1,0:T(8,128)(2,1)}, bf16[256,1024]{1,0:T(8,128)(2,1)S(1)}, u32[]{:S(2)}, u32[]{:S(2)}) collective-permute-start(bf16[256,1024]{1,0:T(8,128)(2,1)} %copy-done.16), channel_id=1, source_target_pairs={{0,3},{1,0},{2,1},{3,2},{4,7},{5,4},{6,5},{7,6},{8,11},{9,8},{10,9... | collective-permute-start | bytes 1572872 | tf_op jit(solution)/shard_map/ppermute | solution.py:514
  104.3 1.6 %copy-start.1 = (f32[2,256,1024]{2,1,0:T(8,128)S(1)}, f32[2,256,1024]{2,1,0:T(8,128)}, u32[]{:S(2)}) copy-start(f32[2,256,1024]{2,1,0:T(8,128)} %right_ref.3) | copy-start | bytes 6291460
  105.9 1.0 copy-start.9
  107.0 1.0 copy-start.11
  108.0 1.0 copy-start.13
  109.1 7.7 %copy-start.2 = (f32[2,256,1024]{2,1,0:T(8,128)S(1)}, f32[2,256,1024]{2,1,0:T(8,128)}, u32[]{:S(2)}) copy-start(f32[2,256,1024]{2,1,0:T(8,128)} %right_ref.3) | copy-start | bytes 6291460
  116.7 12.9 %copy-start.15 = (s32[64]{0:T(128)S(1)}, s32[64]{0:T(128)}, u32[]{:S(2)}) copy-start(s32[64]{0:T(128)} %owner_hbm.3) | copy-start | bytes 772

commit v6 on v5

--- a/solution.py
+++ b/solution.py
@@ -272,59 +272,22 @@
     )(t, token, left_root, right_root, *cuts, owned)
 
 
-def near_kernel(own, left, g1, g3, c1, c3, raw_ref, grads, roots, sems):
-    full = left.shape[0]
-    width = roots.shape[3]
-    groups = []
-    for i, (g, c) in enumerate(((g1, c1), (g3, c3))):
-        bring = [pltpu.make_async_copy(g, grads.at[i], sems.at[i, 4])]
-        groups.append(bring + bring_right(c, roots.at[i], sems.at[i]))
+def rest_kernel(
+    t_ref, own, square, left, g1, g3, g2, c1, c3, c2, mine_ref, after_ref, before_ref, sums_ref, roots, sems
+):
+    groups = [bring_right(c, roots.at[i], sems.at[i]) for i, c in enumerate((c1, c3, c2))]
     for bring in groups:
         for c in bring:
             c.start()
-    raw = [own[0], own[1]]
-    for i, bring in enumerate(groups):
-        for c in bring:
+    full = left.shape[0]
+    width = roots.shape[3]
+    mine, other = own[0], own[1]
+    for i, g in enumerate((g1, g3, g2)):
+        part = dot(left[...], g[...].reshape(full, width)).astype(BF16)
+        for c in groups[i]:
             c.wait()
-        part = dot(left[...], grads[i].reshape(full, width)).astype(BF16)
-        for j in range(2):
-            raw[j] = raw[j] + dot(part, roots[i, j])
-    for j in range(2):
-        raw_ref[j] = raw[j]
-
-
-def near_part(own, left, below, above, cut_below, cut_above):
-    owners, height, width = below.shape
-    full = left.shape[0]
-    return pl.pallas_call(
-        near_kernel,
-        out_shape=jax.ShapeDtypeStruct(own.shape, F32),
-        in_specs=[VMEM_SPEC] * 2 + [HBM_SPEC] * 4,
-        out_specs=VMEM_SPEC,
-        scratch_shapes=[
-            pltpu.VMEM((2, owners, height, width), BF16),
-            pltpu.VMEM((2, 2, width, width), BF16),
-            pltpu.SemaphoreType.DMA((2, 5)),
-        ],
-        compiler_params=PARAMS,
-        cost_estimate=cost(6 * full * full * width, 10 * full * full),
-        name="near_part",
-    )(own, left, below, above, cut_below, cut_above)
-
-
-def far_kernel(
-    t_ref, near, square, left, g2, c2, mine_ref, after_ref, before_ref, sums_ref, roots, sems
-):
-    bring = bring_right(c2, roots, sems)
-    for c in bring:
-        c.start()
-    full = left.shape[0]
-    width = roots.shape[2]
-    part = dot(left[...], g2[...].reshape(full, width)).astype(BF16)
-    for c in bring:
-        c.wait()
-    mine = near[0] + dot(part, roots[0])
-    other = near[1] + dot(part, roots[1])
+        mine = mine + dot(part, roots[i, 0])
+        other = other + dot(part, roots[i, 1])
     mine_ref[...] = mine
     after_ref[...] = other[:, : width // 2].astype(BF16)
     before_ref[...] = other[:, width // 2 :].astype(BF16)
@@ -336,24 +299,24 @@
     sums_ref[...] = sums
 
 
-def far_part(t, near, square, left, far, cut_far):
-    _, full, width = near.shape
+def rest_part(t, own, square, left, grads, cuts):
+    _, full, width = own.shape
     half = jax.ShapeDtypeStruct((full, width // 2), BF16)
     return pl.pallas_call(
-        far_kernel,
+        rest_kernel,
         out_shape=(
             jax.ShapeDtypeStruct((full, width), F32),
             half,
             half,
             jax.ShapeDtypeStruct((8, 128), F32),
         ),
-        in_specs=[SMEM_SPEC] + [VMEM_SPEC] * 4 + [HBM_SPEC],
+        in_specs=[SMEM_SPEC] + [VMEM_SPEC] * 6 + [HBM_SPEC] * 3,
         out_specs=(VMEM_SPEC,) * 4,
-        scratch_shapes=[pltpu.VMEM((2, width, width), BF16), pltpu.SemaphoreType.DMA((4,))],
+        scratch_shapes=[pltpu.VMEM((3, 2, width, width), BF16), pltpu.SemaphoreType.DMA((3, 4))],
         compiler_params=PARAMS,
-        cost_estimate=cost(4 * full * full * width, 8 * full * full),
-        name="far_part",
-    )(t, near, square, left, far, cut_far)
+        cost_estimate=cost(9 * full * full * width, 12 * full * full),
+        name="rest_part",
+    )(t, own, square, left, *grads, *cuts)
 
 
 def scale_kernel(t_ref, mine, first, second, s0, s1, s2, s3, out_hbm, ready, halves, sems):
@@ -529,17 +492,16 @@
     below, above = around(for_neighbours, 1), around(for_neighbours, -1)
     cuts = (cut_below, cut_above, cut_far)
     raw, square, left = own_part(t, token, left_root, right_root, cuts, owned)
-    raw, for_opposite = lax.optimization_barrier((raw, for_opposite))
     far = around(for_opposite, 2)
-    raw = near_part(raw, left, below, above, cut_below, cut_above)
-    mine, after, before, sums = far_part(t, raw, square, left, far, cut_far)
+    mine, after, before, sums = rest_part(t, raw, square, left, (below, above, far), cuts)
     first, second = around(after, 1), around(before, -1)
     everyone = [sums] + [around(sums, k) for k in (1, 2, 3)]
     others = (below, above, far)
-    terms = neighbour_terms(t, owned, others)
-    everyone, terms = lax.optimization_barrier((everyone, terms))
+    scaled = scale(t, mine, first, second, everyone, routed.shape)
+    scaled, late = lax.optimization_barrier((scaled, owned))
+    returned = exchange(scaled)
+    terms = neighbour_terms(t, late, others)
     terms = around(terms[0], 1), around(terms[1], -1)
-    returned = exchange(scale(t, mine, first, second, everyone, routed.shape))
     done = statistics(t, owned, others, left_stat, right_stat)
     new_left, new_right = blend(t, terms, left_stat, right_stat, done)
     return (new_left, new_right, collect(block_owner, returned))

time: 133 us -> 130 us (0.977)
  waiting for transfers between devices: 51.2 us -> 56 us
  local copies, waits for them, and re-layouts: 10.6 us -> 7.43 us
  starting transfers between devices: 42.9 us -> 40.6 us
  Pallas kernels: 25.8 us -> 24.3 us
    ppermute x13, waiting for transfers between devices: 16.1 us -> 25.7 us  [around(): return lax.ppermute(x, 'tensor', [(i, (i + k) % n) for i in range(n)])]
    all_to_all x2, waiting for transfers between devices: 35.1 us -> 30.3 us  [exchange(): return lax.all_to_all(x, 'fsdp', split_axis=0, concat_axis=0, tiled=True)]
    all_to_all x2, starting transfers between devices: 27.7 us -> 24.2 us  [exchange(): return lax.all_to_all(x, 'fsdp', split_axis=0, concat_axis=0, tiled=True)]
    unnamed x36, local copies, waits for them, and re-layouts: 10.6 us -> 7.43 us
    pallas_call x2 -> x1, Pallas kernels: 6.54 us -> 5.09 us  [rest_part(): pl.pallas_call(rest_kernel, out_shape=(jax.ShapeDtypeStruct((full, width)...]
  transfers between devices with their start and end apart: 15 -> 15, of which waited for: 9 -> 10; matrix products, arithmetic and copies ran while one was open for 0% -> 0% of each run, Pallas kernels for 13% -> 10%
where the time goes in v6:
time: 130 us; the launch traced here: 129 us
  waiting for transfers between devices  56 us (43%)
  starting transfers between devices  40.6 us (31%)
  Pallas kernels  24.3 us (19%)
  local copies, waits for them, and re-layouts  7.43 us (6%)
    all_to_all x2, waiting for transfers between devices, exchange(): return lax.all_to_all(x, 'fsdp', split_axis=0, concat_axis=0, tiled=True)  30.3 us
    ppermute x13, waiting for transfers between devices, around(): return lax.ppermute(x, 'tensor', [(i, (i + k) % n) for i in range(n)])  25.7 us
    all_to_all x2, starting transfers between devices, exchange(): return lax.all_to_all(x, 'fsdp', split_axis=0, concat_axis=0, tiled=True)  24.2 us
    ppermute x13, starting transfers between devices, around(): return lax.ppermute(x, 'tensor', [(i, (i + k) % n) for i in range(n)])  16.4 us
    unnamed x36, local copies, waits for them, and re-layouts  7.43 us
    pallas_call x1, Pallas kernels, rest_part(): pl.pallas_call(rest_kernel, out_shape=(jax.ShapeDtypeStruct((full, width)...  5.09 us
    pallas_call x1, Pallas kernels, route(): pl.pallas_call(route_kernel, out_shape=(jax.ShapeDtypeStruct(shape, gradi...  3.68 us
    pallas_call x1, Pallas kernels, statistics(): pl.pallas_call(stats_kernel, out_shape=(shape, shape), grid_spec=pltpu.Pr...  3.66 us
  transfers between devices with their start and end apart: 15, of which 10 were waited for; matrix products, arithmetic and copies ran while one was open for 0% of the time, Pallas kernels for 10%

profile of v6, /device:TPU:1, one launch (start us, length us, event | category | flops | bytes accessed | tf_op | source)
XLA Modules:
  0.0 129.3 jit_solution(16306313436279178191)
XLA Ops:
  0.6 3.7 %route.1 = (bf16[64,2,16,256]{3,2,1,0:T(8,128)(2,1)}, bf16[384,1024]{1,0:T(8,128)(2,1)}, bf16[384,1024]{1,0:T(8,128)(2,1)}, bf16[384,1024]{1,0:T(8,128)(2,1)}) custom-call(s32[1]{0:T(128)} %bitcast.t_ref, s32[64]{0:T(128)} %owner_hbm.3, bf16[64,16,256]{2,1,0:T(8,128)(2,1)} %grad_hbm.1, bf16[2,256,1024]{2,1,0:T(8,128)(2,1)} %left_hbm.3, ...), custom_call_target="tpu_custom_call" | custom-call | bytes 786432 | tf_op jit(solution)/shard_map/route/pallas_call | solution.py:96
  4.3 2.1 %collective-permute-start = (bf16[384,1024]{1,0:T(8,128)(2,1)}, bf16[384,1024]{1,0:T(8,128)(2,1)S(1)}, u32[]{:S(2)}, u32[]{:S(2)}) collective-permute-start(bf16[384,1024]{1,0:T(8,128)(2,1)} %get-tuple-element.27), channel_id=1, source_target_pairs={{0,1},{1,2},{2,3},{3,0},{4,5},{5,6},{6,7},{7,4},{8,9},{9,10},{10,1... | collective-permute-start | bytes 2359304 | tf_op jit(solution)/shard_map/ppermute | solution.py:477
  6.4 1.4 %collective-permute-start.1 = (bf16[384,1024]{1,0:T(8,128)(2,1)}, bf16[384,1024]{1,0:T(8,128)(2,1)}, u32[]{:S(2)}, u32[]{:S(2)}) collective-permute-start(bf16[384,1024]{1,0:T(8,128)(2,1)} %get-tuple-element.28), channel_id=1, source_target_pairs={{0,3},{1,0},{2,1},{3,2},{4,7},{5,4},{6,5},{7,6},{8,11},{9,8},{10,9... | collective-permute-start | bytes 2359304 | tf_op jit(solution)/shard_map/ppermute | solution.py:477
  7.8 13.2 %all-to-all-start = ((bf16[64,2,16,256]{3,2,1,0:T(8,128)(2,1)}), bf16[64,2,16,256]{3,2,1,0:T(8,128)(2,1)}, u32[]{:S(2)}, u32[]{:S(2)}) async-start(bf16[64,2,16,256]{3,2,1,0:T(8,128)(2,1)} %get-tuple-element.26), calls=%async_computation | async-start | bytes 2097152 | tf_op jit(solution)/shard_map/all_to_all | solution.py:481
  21.0 1.6 %collective-permute-start.2 = (bf16[384,1024]{1,0:T(8,128)(2,1)}, bf16[384,1024]{1,0:T(8,128)(2,1)}, u32[]{:S(2)}, u32[]{:S(2)}) collective-permute-start(bf16[384,1024]{1,0:T(8,128)(2,1)} %get-tuple-element.30), channel_id=1, source_target_pairs={{0,2},{1,3},{2,0},{3,1},{4,6},{5,7},{6,4},{7,5},{8,10},{9,11},{10,... | collective-permute-start | bytes 2359304 | tf_op jit(solution)/shard_map/ppermute | solution.py:477
  22.6 0.3 collective-permute-done.a.c1
  22.9 1.6 %collective-permute-done.1.b.c3 = bf16[384,1024]{1,0:T(8,128)(2,1)} collective-permute-done((bf16[384,1024]{1,0:T(8,128)(2,1)}, bf16[384,1024]{1,0:T(8,128)(2,1)}, u32[]{:S(2)}, u32[]{:S(2)}) %collective-permute-start.1) | collective-permute-done | bytes 786464 | tf_op jit(solution)/shard_map/ppermute | solution.py:477
  24.5 0.6 hold.1.token
  25.1 23.8 %all-to-all-done.both_hbm.g0_hbm = bf16[64,2,16,256]{3,2,1,0:T(8,128)(2,1)} async-done(((bf16[64,2,16,256]{3,2,1,0:T(8,128)(2,1)}), bf16[64,2,16,256]{3,2,1,0:T(8,128)(2,1)}, u32[]{:S(2)}, u32[]{:S(2)}) %all-to-all-start) | async-done | bytes 1048608 | tf_op jit(solution)/shard_map/all_to_all | solution.py:481
  48.9 1.4 %select.1 = (bf16[64,16,256]{2,1,0:T(8,128)(2,1)S(1)}, bf16[64,16,256]{2,1,0:T(8,128)(2,1)S(1)}) custom-call(s32[1]{0:T(128)} %bitcast.t_ref, bf16[64,2,16,256]{3,2,1,0:T(8,128)(2,1)} %all-to-all-done.both_hbm.g0_hbm), custom_call_target="tpu_custom_call" | custom-call | bytes 2097152 | tf_op jit(solution)/shard_map/select/pallas_call | solution.py:179
  50.3 0.1 collective-permute-start.3
  50.4 2.7 %collective-permute-start.4 = (bf16[64,16,256]{2,1,0:T(8,128)(2,1)S(1)}, bf16[64,16,256]{2,1,0:T(8,128)(2,1)S(1)}, u32[]{:S(2)}, u32[]{:S(2)}) collective-permute-start(bf16[64,16,256]{2,1,0:T(8,128)(2,1)S(1)} %get-tuple-element.35), channel_id=1, source_target_pairs={{0,3},{1,0},{2,1},{3,2},{4,7},{5,4},{6,5},{7,6},{8,11},{9,8},{10,9... | collective-permute-start | bytes 1572872 | tf_op jit(solution)/shard_map/ppermute | solution.py:477
  53.0 0.3 collective-permute-start.5
  53.4 0.0 collective-permute-done.2.c2
  53.4 1.2 copy-done.2
  54.6 1.2 copy-done.3
  55.8 1.1 copy-done.5
  57.0 0.7 copy-done.16
  57.6 3.0 %own_part.1 = (f32[2,1024,256]{2,1,0:T(8,128)S(1)}, f32[2,8,128]{2,1,0:T(8,128)S(1)}, bf16[1024,1024]{1,0:T(8,128)(2,1)S(1)}) custom-call(s32[1]{0:T(128)} %bitcast.t_ref, f32[8,128]{1,0:T(8,128)S(1)} %copy-done.16, bf16[2,256,1024]{2,1,0:T(8,128)(2,1)S(1)} %copy-done.2, bf16[2,256,1024]{2,1,0:T(8,128)(2,1)S(1)} %copy-done.3, ...), custom_call_target="tpu_custom_call" | custom-call | flops 1073741824 | bytes 12582912 | tf_op jit(solution)/shard_map/own_part/pallas_call | solution.py:255
  60.7 3.2 %collective-permute-done.3.g1 = bf16[64,16,256]{2,1,0:T(8,128)(2,1)S(1)} collective-permute-done((bf16[64,16,256]{2,1,0:T(8,128)(2,1)S(1)}, bf16[64,16,256]{2,1,0:T(8,128)(2,1)S(1)}, u32[]{:S(2)}, u32[]{:S(2)}) %collective-permute-start.3) | collective-permute-done | bytes 524320 | tf_op jit(solution)/shard_map/ppermute | solution.py:477
  63.9 0.0 collective-permute-done.4.g3
  63.9 10.8 %collective-permute-done.5.g2 = bf16[64,16,256]{2,1,0:T(8,128)(2,1)S(1)} collective-permute-done((bf16[64,16,256]{2,1,0:T(8,128)(2,1)S(1)}, bf16[64,16,256]{2,1,0:T(8,128)(2,1)S(1)}, u32[]{:S(2)}, u32[]{:S(2)}) %collective-permute-start.5) | collective-permute-done | bytes 524320 | tf_op jit(solution)/shard_map/ppermute | solution.py:477
  74.7 5.1 %rest_part.1 = (f32[1024,256]{1,0:T(8,128)S(1)}, bf16[1024,128]{1,0:T(8,128)(2,1)S(1)}, bf16[1024,128]{1,0:T(8,128)(2,1)S(1)}, f32[8,128]{1,0:T(8,128)S(1)}) custom-call(s32[1]{0:T(128)} %bitcast.t_ref, f32[2,1024,256]{2,1,0:T(8,128)S(1)} %get-tuple-element.32.own, f32[2,8,128]{2,1,0:T(8,128)S(1)} %get-tuple-element.33.square, ...), custom_call_target="tpu_custom_call" | custom-call | flops 2415919104 | bytes 12582912 | tf_op jit(solution)/shard_map/rest_part/pallas_call | solution.py:305
  79.8 0.6 collective-permute-start.6
  80.4 2.1 %collective-permute-start.7 = (bf16[1024,128]{1,0:T(8,128)(2,1)S(1)}, bf16[1024,128]{1,0:T(8,128)(2,1)S(1)}, u32[]{:S(2)}, u32[]{:S(2)}) collective-permute-start(bf16[1024,128]{1,0:T(8,128)(2,1)S(1)} %get-tuple-element.39), channel_id=1, source_target_pairs={{0,3},{1,0},{2,1},{3,2},{4,7},{5,4},{6,5},{7,6},{8,11},{9,8},{10,9... | collective-permute-start | bytes 786440 | tf_op jit(solution)/shard_map/ppermute | solution.py:477
  82.6 0.0 collective-permute-start.8
  82.6 1.3 collective-permute-start.9
  83.9 1.4 %collective-permute-start.10 = (f32[8,128]{1,0:T(8,128)S(1)}, f32[8,128]{1,0:T(8,128)S(1)}, u32[]{:S(2)}, u32[]{:S(2)}) collective-permute-start(f32[8,128]{1,0:T(8,128)S(1)} %get-tuple-element.40.s0), channel_id=1, source_target_pairs={{0,3},{1,0},{2,1},{3,2},{4,7},{5,4},{6,5},{7,6},{8,11},{9,8},{10,9... | collective-permute-start | bytes 12296 | tf_op jit(solution)/shard_map/ppermute | solution.py:477
  85.3 1.1 collective-permute-done.8.s1
  86.4 0.3 collective-permute-done.9.s2
  86.6 0.5 collective-permute-done.10.s3
  87.2 0.0 collective-permute-done.6.first
  87.2 1.2 scale.1
  88.4 0.0 copy-start.1
  88.4 11.1 %all-to-all-start.1 = ((bf16[64,2,16,256]{3,2,1,0:T(8,128)(2,1)}), bf16[64,2,16,256]{3,2,1,0:T(8,128)(2,1)S(1)}, u32[]{:S(2)}, u32[]{:S(2)}) async-start(bf16[64,2,16,256]{3,2,1,0:T(8,128)(2,1)} %scale.1), calls=%async_computation.1 | async-start | bytes 2097152 | tf_op jit(solution)/shard_map/all_to_all | solution.py:481
  99.5 0.0 copy-start.8
  99.5 1.0 copy-done.8
  100.5 1.0 copy-done.11
  101.6 1.0 copy-done.14
  102.6 2.5 %neighbour_terms.1 = (bf16[256,1024]{1,0:T(8,128)(2,1)S(1)}, bf16[256,1024]{1,0:T(8,128)(2,1)S(1)}) custom-call(s32[1]{0:T(128)} %bitcast.t_ref, bf16[64,2,16,256]{3,2,1,0:T(8,128)(2,1)} %all-to-all-done.both_hbm.g0_hbm, bf16[64,16,256]{2,1,0:T(8,128)(2,1)S(1)} %copy-done.8, bf16[64,16,256]{2,1,0:T(8,128)(2,1)S(1)} %copy-done.11, ...), custom_call_target="tpu_custom_call" | custom-call | flops 1073741824 | bytes 1572864 | tf_op jit(solution)/shard_map/neighbour_terms/pallas_call | solution.py:397
  105.1 0.7 collective-permute-start.11
  105.8 2.0 %collective-permute-start.12 = (bf16[256,1024]{1,0:T(8,128)(2,1)S(1)}, bf16[256,1024]{1,0:T(8,128)(2,1)S(1)}, u32[]{:S(2)}, u32[]{:S(2)}) collective-permute-start(bf16[256,1024]{1,0:T(8,128)(2,1)S(1)} %get-tuple-element.43), channel_id=1, source_target_pairs={{0,3},{1,0},{2,1},{3,2},{4,7},{5,4},{6,5},{7,6},{8,11},{9,8},{10,9... | collective-permute-start | bytes 1572872 | tf_op jit(solution)/shard_map/ppermute | solution.py:477
  107.9 3.7 %statistics.1 = (f32[2,256,1024]{2,1,0:T(8,128)}, f32[2,256,1024]{2,1,0:T(8,128)}) custom-call(s32[1]{0:T(128)} %bitcast.t_ref, bf16[64,2,16,256]{3,2,1,0:T(8,128)(2,1)} %all-to-all-done.both_hbm.g0_hbm, bf16[64,16,256]{2,1,0:T(8,128)(2,1)S(1)} %copy-done.9, bf16[64,16,256]{2,1,0:T(8,128)(2,1)S(1)} %copy-done.12, bf16[64,16,256]{2,1,0:T(8,128)(2,1)S(1)} %copy-done.15, ...), custom_call_target="tpu_custom_call" | custom-call | flops 1073741824 | bytes 3145728 | tf_op jit(solution)/shard_map/statistics/pallas_call | solution.py:434
  111.6 7.9 %collective-permute-done.11.left_term = bf16[256,1024]{1,0:T(8,128)(2,1)S(1)} collective-permute-done((bf16[256,1024]{1,0:T(8,128)(2,1)S(1)}, bf16[256,1024]{1,0:T(8,128)(2,1)S(1)}, u32[]{:S(2)}, u32[]{:S(2)}) %collective-permute-start.11) | collective-permute-done | bytes 524320 | tf_op jit(solution)/shard_map/ppermute | solution.py:477
  119.4 0.0 collective-permute-done.12.right_term
  119.4 1.5 %blend.1 = (f32[2,256,1024]{2,1,0:T(8,128)}, f32[2,256,1024]{2,1,0:T(8,128)}) custom-call(s32[1]{0:T(128)} %bitcast.t_ref, bf16[256,1024]{1,0:T(8,128)(2,1)S(1)} %collective-permute-done.11.left_term, bf16[256,1024]{1,0:T(8,128)(2,1)S(1)} %collective-permute-done.12.right_term, ...), custom_call_target="tpu_custom_call", output_to_operand_aliasing={{0}: (5, {}), {1}: (6, {})} | custom-call | flops 1048576 | bytes 4718592 | tf_op jit(solution)/shard_map/blend/pallas_call | solution.py:459
  121.0 6.5 %all-to-all-done.1.slots_hbm = bf16[64,2,16,256]{3,2,1,0:T(8,128)(2,1)S(1)} async-done(((bf16[64,2,16,256]{3,2,1,0:T(8,128)(2,1)}), bf16[64,2,16,256]{3,2,1,0:T(8,128)(2,1)S(1)}, u32[]{:S(2)}, u32[]{:S(2)}) %all-to-all-start.1) | async-done | bytes 1048608 | tf_op jit(solution)/shard_map/all_to_all | solution.py:481
  127.5 1.7 %collect.1 = bf16[64,16,256]{2,1,0:T(8,128)(2,1)} custom-call(s32[64]{0:T(128)S(1)} %copy-done.17, bf16[64,2,16,256]{3,2,1,0:T(8,128)(2,1)S(1)} %all-to-all-done.1.slots_hbm), custom_call_target="tpu_custom_call" | custom-call | bytes 1572864 | tf_op jit(solution)/shard_map/collect/pallas_call | solution.py:143
  (28 shorter events, 0.1 us)
Async XLA Ops:
  4.3 18.6 %collective-permute-start = (bf16[384,1024]{1,0:T(8,128)(2,1)}, bf16[384,1024]{1,0:T(8,128)(2,1)S(1)}, u32[]{:S(2)}, u32[]{:S(2)}) collective-permute-start(bf16[384,1024]{1,0:T(8,128)(2,1)} %get-tuple-element.27), channel_id=1, source_target_pairs={{0,1},{1,2},{2,3},{3,0},{4,5},{5,6},{6,7},{7,4},{8,9},{9,10},{10,1... | collective-permute-start | bytes 2359304 | tf_op jit(solution)/shard_map/ppermute | solution.py:477
  6.4 18.1 %collective-permute-start.1 = (bf16[384,1024]{1,0:T(8,128)(2,1)}, bf16[384,1024]{1,0:T(8,128)(2,1)}, u32[]{:S(2)}, u32[]{:S(2)}) collective-permute-start(bf16[384,1024]{1,0:T(8,128)(2,1)} %get-tuple-element.28), channel_id=1, source_target_pairs={{0,3},{1,0},{2,1},{3,2},{4,7},{5,4},{6,5},{7,6},{8,11},{9,8},{10,9... | collective-permute-start | bytes 2359304 | tf_op jit(solution)/shard_map/ppermute | solution.py:477
  7.8 41.1 %all-to-all-start = ((bf16[64,2,16,256]{3,2,1,0:T(8,128)(2,1)}), bf16[64,2,16,256]{3,2,1,0:T(8,128)(2,1)}, u32[]{:S(2)}, u32[]{:S(2)}) async-start(bf16[64,2,16,256]{3,2,1,0:T(8,128)(2,1)} %get-tuple-element.26), calls=%async_computation | async-start | bytes 2097152 | tf_op jit(solution)/shard_map/all_to_all | solution.py:481
  21.0 32.4 %collective-permute-start.2 = (bf16[384,1024]{1,0:T(8,128)(2,1)}, bf16[384,1024]{1,0:T(8,128)(2,1)}, u32[]{:S(2)}, u32[]{:S(2)}) collective-permute-start(bf16[384,1024]{1,0:T(8,128)(2,1)} %get-tuple-element.30), channel_id=1, source_target_pairs={{0,2},{1,3},{2,0},{3,1},{4,6},{5,7},{6,4},{7,5},{8,10},{9,11},{10,... | collective-permute-start | bytes 2359304 | tf_op jit(solution)/shard_map/ppermute | solution.py:477
  22.9 1.6 %copy-start.4 = (bf16[384,1024]{1,0:T(8,128)(2,1)}, bf16[384,1024]{1,0:T(8,128)(2,1)S(1)}, u32[]{:S(2)}) copy-start(bf16[384,1024]{1,0:T(8,128)(2,1)S(1)} %collective-permute-done.a.c1) | copy-start | bytes 2359300
  50.3 13.6 %collective-permute-start.3 = (bf16[64,16,256]{2,1,0:T(8,128)(2,1)S(1)}, bf16[64,16,256]{2,1,0:T(8,128)(2,1)S(1)}, u32[]{:S(2)}, u32[]{:S(2)}) collective-permute-start(bf16[64,16,256]{2,1,0:T(8,128)(2,1)S(1)} %get-tuple-element.35), channel_id=1, source_target_pairs={{0,1},{1,2},{2,3},{3,0},{4,5},{5,6},{6,7},{7,4},{8,9},{9,10},{10,1... | collective-permute-start | bytes 1572872 | tf_op jit(solution)/shard_map/ppermute | solution.py:477
  50.4 13.5 %collective-permute-start.4 = (bf16[64,16,256]{2,1,0:T(8,128)(2,1)S(1)}, bf16[64,16,256]{2,1,0:T(8,128)(2,1)S(1)}, u32[]{:S(2)}, u32[]{:S(2)}) collective-permute-start(bf16[64,16,256]{2,1,0:T(8,128)(2,1)S(1)} %get-tuple-element.35), channel_id=1, source_target_pairs={{0,3},{1,0},{2,1},{3,2},{4,7},{5,4},{6,5},{7,6},{8,11},{9,8},{10,9... | collective-permute-start | bytes 1572872 | tf_op jit(solution)/shard_map/ppermute | solution.py:477
  53.0 21.6 %collective-permute-start.5 = (bf16[64,16,256]{2,1,0:T(8,128)(2,1)S(1)}, bf16[64,16,256]{2,1,0:T(8,128)(2,1)S(1)}, u32[]{:S(2)}, u32[]{:S(2)}) collective-permute-start(bf16[64,16,256]{2,1,0:T(8,128)(2,1)S(1)} %get-tuple-element.36), channel_id=1, source_target_pairs={{0,2},{1,3},{2,0},{3,1},{4,6},{5,7},{6,4},{7,5},{8,10},{9,11},{10,... | collective-permute-start | bytes 1572872 | tf_op jit(solution)/shard_map/ppermute | solution.py:477
  53.4 1.2 copy-start.2
  54.6 1.2 copy-start.3
  55.8 1.1 copy-start.5
  57.0 0.7 copy-start.16
  57.6 17.0 %copy-start.6 = (bf16[384,1024]{1,0:T(8,128)(2,1)S(1)}, bf16[384,1024]{1,0:T(8,128)(2,1)}, u32[]{:S(2)}) copy-start(bf16[384,1024]{1,0:T(8,128)(2,1)} %copy-done.4) | copy-start | bytes 2359300
  63.9 15.9 %copy-start.7 = (bf16[64,16,256]{2,1,0:T(8,128)(2,1)}, bf16[64,16,256]{2,1,0:T(8,128)(2,1)S(1)}, u32[]{:S(2)}) copy-start(bf16[64,16,256]{2,1,0:T(8,128)(2,1)S(1)} %collective-permute-done.3.g1) | copy-start | bytes 1572868
  63.9 15.9 %copy-start.10 = (bf16[64,16,256]{2,1,0:T(8,128)(2,1)}, bf16[64,16,256]{2,1,0:T(8,128)(2,1)S(1)}, u32[]{:S(2)}) copy-start(bf16[64,16,256]{2,1,0:T(8,128)(2,1)S(1)} %collective-permute-done.4.g3) | copy-start | bytes 1572868
  74.7 5.1 %copy-start.13 = (bf16[64,16,256]{2,1,0:T(8,128)(2,1)}, bf16[64,16,256]{2,1,0:T(8,128)(2,1)S(1)}, u32[]{:S(2)}) copy-start(bf16[64,16,256]{2,1,0:T(8,128)(2,1)S(1)} %collective-permute-done.5.g2) | copy-start | bytes 1572868
  79.8 7.4 %collective-permute-start.6 = (bf16[1024,128]{1,0:T(8,128)(2,1)S(1)}, bf16[1024,128]{1,0:T(8,128)(2,1)S(1)}, u32[]{:S(2)}, u32[]{:S(2)}) collective-permute-start(bf16[1024,128]{1,0:T(8,128)(2,1)S(1)} %get-tuple-element.38), channel_id=1, source_target_pairs={{0,1},{1,2},{2,3},{3,0},{4,5},{5,6},{6,7},{7,4},{8,9},{9,10},{10,1... | collective-permute-start | bytes 786440 | tf_op jit(solution)/shard_map/ppermute | solution.py:477
  80.4 6.8 %collective-permute-start.7 = (bf16[1024,128]{1,0:T(8,128)(2,1)S(1)}, bf16[1024,128]{1,0:T(8,128)(2,1)S(1)}, u32[]{:S(2)}, u32[]{:S(2)}) collective-permute-start(bf16[1024,128]{1,0:T(8,128)(2,1)S(1)} %get-tuple-element.39), channel_id=1, source_target_pairs={{0,3},{1,0},{2,1},{3,2},{4,7},{5,4},{6,5},{7,6},{8,11},{9,8},{10,9... | collective-permute-start | bytes 786440 | tf_op jit(solution)/shard_map/ppermute | solution.py:477
  82.6 3.8 %collective-permute-start.8 = (f32[8,128]{1,0:T(8,128)S(1)}, f32[8,128]{1,0:T(8,128)S(1)}, u32[]{:S(2)}, u32[]{:S(2)}) collective-permute-start(f32[8,128]{1,0:T(8,128)S(1)} %get-tuple-element.40.s0), channel_id=1, source_target_pairs={{0,1},{1,2},{2,3},{3,0},{4,5},{5,6},{6,7},{7,4},{8,9},{9,10},{10,1... | collective-permute-start | bytes 12296 | tf_op jit(solution)/shard_map/ppermute | solution.py:477
  82.6 4.1 %collective-permute-start.9 = (f32[8,128]{1,0:T(8,128)S(1)}, f32[8,128]{1,0:T(8,128)S(1)}, u32[]{:S(2)}, u32[]{:S(2)}) collective-permute-start(f32[8,128]{1,0:T(8,128)S(1)} %get-tuple-element.40.s0), channel_id=1, source_target_pairs={{0,2},{1,3},{2,0},{3,1},{4,6},{5,7},{6,4},{7,5},{8,10},{9,11},{10,... | collective-permute-start | bytes 12296 | tf_op jit(solution)/shard_map/ppermute | solution.py:477
  83.9 3.3 %collective-permute-start.10 = (f32[8,128]{1,0:T(8,128)S(1)}, f32[8,128]{1,0:T(8,128)S(1)}, u32[]{:S(2)}, u32[]{:S(2)}) collective-permute-start(f32[8,128]{1,0:T(8,128)S(1)} %get-tuple-element.40.s0), channel_id=1, source_target_pairs={{0,3},{1,0},{2,1},{3,2},{4,7},{5,4},{6,5},{7,6},{8,11},{9,8},{10,9... | collective-permute-start | bytes 12296 | tf_op jit(solution)/shard_map/ppermute | solution.py:477
  88.4 19.5 %copy-start.1 = (f32[2,256,1024]{2,1,0:T(8,128)S(1)}, f32[2,256,1024]{2,1,0:T(8,128)}, u32[]{:S(2)}) copy-start(f32[2,256,1024]{2,1,0:T(8,128)} %right_ref.3) | copy-start | bytes 6291460
  88.4 39.1 %all-to-all-start.1 = ((bf16[64,2,16,256]{3,2,1,0:T(8,128)(2,1)}), bf16[64,2,16,256]{3,2,1,0:T(8,128)(2,1)S(1)}, u32[]{:S(2)}, u32[]{:S(2)}) async-start(bf16[64,2,16,256]{3,2,1,0:T(8,128)(2,1)} %scale.1), calls=%async_computation.1 | async-start | bytes 2097152 | tf_op jit(solution)/shard_map/all_to_all | solution.py:481
  99.5 1.0 copy-start.8
  100.5 1.0 copy-start.11
  101.6 1.0 copy-start.14
  102.6 5.3 %copy-start = (f32[2,256,1024]{2,1,0:T(8,128)S(1)}, f32[2,256,1024]{2,1,0:T(8,128)}, u32[]{:S(2)}) copy-start(f32[2,256,1024]{2,1,0:T(8,128)} %left_ref.3) | copy-start | bytes 6291460
  102.6 5.3 %copy-start.9 = (bf16[64,16,256]{2,1,0:T(8,128)(2,1)S(1)}, bf16[64,16,256]{2,1,0:T(8,128)(2,1)}, u32[]{:S(2)}) copy-start(bf16[64,16,256]{2,1,0:T(8,128)(2,1)} %copy-done.7) | copy-start | bytes 1572868
  102.6 5.3 %copy-start.12 = (bf16[64,16,256]{2,1,0:T(8,128)(2,1)S(1)}, bf16[64,16,256]{2,1,0:T(8,128)(2,1)}, u32[]{:S(2)}) copy-start(bf16[64,16,256]{2,1,0:T(8,128)(2,1)} %copy-done.10) | copy-start | bytes 1572868
  102.6 5.3 %copy-start.15 = (bf16[64,16,256]{2,1,0:T(8,128)(2,1)S(1)}, bf16[64,16,256]{2,1,0:T(8,128)(2,1)}, u32[]{:S(2)}) copy-start(bf16[64,16,256]{2,1,0:T(8,128)(2,1)} %copy-done.13) | copy-start | bytes 1572868
  105.1 14.3 %collective-permute-start.11 = (bf16[256,1024]{1,0:T(8,128)(2,1)S(1)}, bf16[256,1024]{1,0:T(8,128)(2,1)S(1)}, u32[]{:S(2)}, u32[]{:S(2)}) collective-permute-start(bf16[256,1024]{1,0:T(8,128)(2,1)S(1)} %get-tuple-element.42), channel_id=1, source_target_pairs={{0,1},{1,2},{2,3},{3,0},{4,5},{5,6},{6,7},{7,4},{8,9},{9,10},{10,1... | collective-permute-start | bytes 1572872 | tf_op jit(solution)/shard_map/ppermute | solution.py:477
  105.8 13.6 %collective-permute-start.12 = (bf16[256,1024]{1,0:T(8,128)(2,1)S(1)}, bf16[256,1024]{1,0:T(8,128)(2,1)S(1)}, u32[]{:S(2)}, u32[]{:S(2)}) collective-permute-start(bf16[256,1024]{1,0:T(8,128)(2,1)S(1)} %get-tuple-element.43), channel_id=1, source_target_pairs={{0,3},{1,0},{2,1},{3,2},{4,7},{5,4},{6,5},{7,6},{8,11},{9,8},{10,9... | collective-permute-start | bytes 1572872 | tf_op jit(solution)/shard_map/ppermute | solution.py:477
  119.4 8.0 %copy-start.17 = (s32[64]{0:T(128)S(1)}, s32[64]{0:T(128)}, u32[]{:S(2)}) copy-start(s32[64]{0:T(128)} %owner_hbm.3) | copy-start | bytes 772

commit v7 on v6

--- a/solution.py
+++ b/solution.py
@@ -272,6 +272,13 @@
     )(t, token, left_root, right_root, *cuts, owned)
 
 
+def three_parts(value):
+    high = value.astype(BF16)
+    rest = value - high.astype(F32)
+    middle = rest.astype(BF16)
+    return high, middle, (rest - middle.astype(F32)).astype(BF16)
+
+
 def rest_kernel(
     t_ref, own, square, left, g1, g3, g2, c1, c3, c2, mine_ref, after_ref, before_ref, sums_ref, roots, sems
 ):
@@ -289,19 +296,27 @@
         mine = mine + dot(part, roots[i, 0])
         other = other + dot(part, roots[i, 1])
     mine_ref[...] = mine
-    after_ref[...] = other[:, : width // 2].astype(BF16)
-    before_ref[...] = other[:, width // 2 :].astype(BF16)
+    after_ref[0:full, :] = other[:, : width // 2].astype(BF16)
+    before_ref[0:full, :] = other[:, width // 2 :].astype(BF16)
     total = jnp.sum(mine * mine, keepdims=True) + jnp.sum(other * other, keepdims=True)
     row = lax.broadcasted_iota(jnp.int32, sums_ref.shape, 0)
     sums = jnp.where(row == lax.rem(t_ref[0], 2), total, jnp.zeros(sums_ref.shape, F32))
     for slot in range(2):
         sums = jnp.where(row == 2 + slot, square[slot], sums)
     sums_ref[...] = sums
+    shape = (16, width // 2)
+    row = lax.broadcasted_iota(jnp.int32, shape, 0)
+    tile = jnp.zeros(shape, F32)
+    for i, value in enumerate((total, square[0, 0:1, 0:1], square[1, 0:1, 0:1])):
+        for j, part in enumerate(three_parts(jnp.broadcast_to(value, shape))):
+            tile = jnp.where(row == 3 * i + j, part.astype(F32), tile)
+    after_ref[full : full + 16, :] = tile.astype(BF16)
+    before_ref[full : full + 16, :] = tile.astype(BF16)
 
 
 def rest_part(t, own, square, left, grads, cuts):
     _, full, width = own.shape
-    half = jax.ShapeDtypeStruct((full, width // 2), BF16)
+    half = jax.ShapeDtypeStruct((full + 16, width // 2), BF16)
     return pl.pallas_call(
         rest_kernel,
         out_shape=(
@@ -319,18 +334,23 @@
     )(t, own, square, left, *grads, *cuts)
 
 
-def scale_kernel(t_ref, mine, first, second, s0, s1, s2, s3, out_hbm, ready, halves, sems):
+def scale_kernel(t_ref, mine, first, second, s0, s2, out_hbm, ready, halves, sems):
     _, here, height, width = ready.shape
     rows = here * height
     t = t_ref[0]
-    sums = s0[...] + s1[...] + s2[...] + s3[...]
-    grafts = [
-        jnp.sqrt((sums[2 + slot : 3 + slot, 0:1] + EPSILON) / (sums[slot : slot + 1, 0:1] + EPSILON))
-        for slot in range(2)
-    ]
+    sums = s0[...] + s2[...]
+    tiles = [x[4 * rows : 4 * rows + 16, 0:1].astype(F32) for x in (first, second)]
+
+    def sent(i):
+        parts = [x[i : i + 1] + x[i + 1 : i + 2] + x[i + 2 : i + 3] for x in tiles]
+        return parts[0] + parts[1]
+
+    squares = [sums[2 + slot : 3 + slot, 0:1] + sent(3 + 3 * slot) for slot in range(2)]
     even = lax.rem(t, 2) == 0
-    own_graft = jnp.where(even, grafts[0], grafts[1])
-    other_graft = jnp.where(even, grafts[1], grafts[0])
+    own_square = jnp.where(even, squares[0], squares[1])
+    other_square = jnp.where(even, squares[1], squares[0])
+    own_graft = jnp.sqrt((own_square + EPSILON) / (sums[0:1, 0:1] + sums[1:2, 0:1] + EPSILON))
+    other_graft = jnp.sqrt((other_square + EPSILON) / (sent(0) + EPSILON))
     slot = lax.rem(t, 2)
     half = width // 2
     parts = (
@@ -357,7 +377,7 @@
     return pl.pallas_call(
         scale_kernel,
         out_shape=jax.ShapeDtypeStruct(shape, BF16),
-        in_specs=[SMEM_SPEC] + [VMEM_SPEC] * 7,
+        in_specs=[SMEM_SPEC] + [VMEM_SPEC] * 5,
         out_specs=HBM_SPEC,
         scratch_shapes=[
             pltpu.VMEM((4, here, height, width), BF16),
@@ -495,9 +515,9 @@
     far = around(for_opposite, 2)
     mine, after, before, sums = rest_part(t, raw, square, left, (below, above, far), cuts)
     first, second = around(after, 1), around(before, -1)
-    everyone = [sums] + [around(sums, k) for k in (1, 2, 3)]
+    norms = sums, around(sums, 2)
     others = (below, above, far)
-    scaled = scale(t, mine, first, second, everyone, routed.shape)
+    scaled = scale(t, mine, first, second, norms, routed.shape)
     scaled, late = lax.optimization_barrier((scaled, owned))
     returned = exchange(scaled)
     terms = neighbour_terms(t, late, others)

time: 130 us -> 130 us (level)
  starting transfers between devices: 40.6 us -> 38.1 us
  waiting for transfers between devices: 56 us -> 58.1 us
    ppermute x13 -> x11, starting transfers between devices: 16.4 us -> 13.7 us  [around(): return lax.ppermute(x, 'tensor', [(i, (i + k) % n) for i in range(n)])]
    ppermute x13 -> x11, waiting for transfers between devices: 25.7 us -> 27.8 us  [around(): return lax.ppermute(x, 'tensor', [(i, (i + k) % n) for i in range(n)])]
  transfers between devices with their start and end apart: 15 -> 13, of which waited for: 10 -> 8; matrix products, arithmetic and copies ran while one was open for 0% -> 0% of each run, Pallas kernels for 10% -> 10%
where the time goes in v7:
time: 130 us; the launch traced here: 129 us
  waiting for transfers between devices  58.1 us (45%)
  starting transfers between devices  38.1 us (29%)
  Pallas kernels  24.4 us (19%)
  local copies, waits for them, and re-layouts  7.43 us (6%)
    all_to_all x2, waiting for transfers between devices, exchange(): return lax.all_to_all(x, 'fsdp', split_axis=0, concat_axis=0, tiled=True)  30.3 us
    ppermute x11, waiting for transfers between devices, around(): return lax.ppermute(x, 'tensor', [(i, (i + k) % n) for i in range(n)])  27.8 us
    all_to_all x2, starting transfers between devices, exchange(): return lax.all_to_all(x, 'fsdp', split_axis=0, concat_axis=0, tiled=True)  24.5 us
    ppermute x11, starting transfers between devices, around(): return lax.ppermute(x, 'tensor', [(i, (i + k) % n) for i in range(n)])  13.7 us
    unnamed x36, local copies, waits for them, and re-layouts  7.43 us
    pallas_call x1, Pallas kernels, rest_part(): pl.pallas_call(rest_kernel, out_shape=(jax.ShapeDtypeStruct((full, width)...  5.11 us
    pallas_call x1, Pallas kernels, route(): pl.pallas_call(route_kernel, out_shape=(jax.ShapeDtypeStruct(shape, gradi...  3.68 us
    pallas_call x1, Pallas kernels, statistics(): pl.pallas_call(stats_kernel, out_shape=(shape, shape), grid_spec=pltpu.Pr...  3.66 us
  transfers between devices with their start and end apart: 13, of which 8 were waited for; matrix products, arithmetic and copies ran while one was open for 0% of the time, Pallas kernels for 10%

profile of v7, /device:TPU:1, one launch (start us, length us, event | category | flops | bytes accessed | tf_op | source)
XLA Modules:
  0.0 129.0 jit_solution(2733091118954815477)
XLA Ops:
  0.6 3.7 %route.1 = (bf16[64,2,16,256]{3,2,1,0:T(8,128)(2,1)}, bf16[384,1024]{1,0:T(8,128)(2,1)}, bf16[384,1024]{1,0:T(8,128)(2,1)}, bf16[384,1024]{1,0:T(8,128)(2,1)}) custom-call(s32[1]{0:T(128)} %bitcast.t_ref, s32[64]{0:T(128)} %owner_hbm.3, bf16[64,16,256]{2,1,0:T(8,128)(2,1)} %grad_hbm.1, bf16[2,256,1024]{2,1,0:T(8,128)(2,1)} %left_hbm.3, ...), custom_call_target="tpu_custom_call" | custom-call | bytes 786432 | tf_op jit(solution)/shard_map/route/pallas_call | solution.py:96
  4.3 2.1 %collective-permute-start = (bf16[384,1024]{1,0:T(8,128)(2,1)}, bf16[384,1024]{1,0:T(8,128)(2,1)S(1)}, u32[]{:S(2)}, u32[]{:S(2)}) collective-permute-start(bf16[384,1024]{1,0:T(8,128)(2,1)} %get-tuple-element.27), channel_id=1, source_target_pairs={{0,1},{1,2},{2,3},{3,0},{4,5},{5,6},{6,7},{7,4},{8,9},{9,10},{10,1... | collective-permute-start | bytes 2359304 | tf_op jit(solution)/shard_map/ppermute | solution.py:497
  6.4 1.4 %collective-permute-start.1 = (bf16[384,1024]{1,0:T(8,128)(2,1)}, bf16[384,1024]{1,0:T(8,128)(2,1)}, u32[]{:S(2)}, u32[]{:S(2)}) collective-permute-start(bf16[384,1024]{1,0:T(8,128)(2,1)} %get-tuple-element.28), channel_id=1, source_target_pairs={{0,3},{1,0},{2,1},{3,2},{4,7},{5,4},{6,5},{7,6},{8,11},{9,8},{10,9... | collective-permute-start | bytes 2359304 | tf_op jit(solution)/shard_map/ppermute | solution.py:497
  7.8 13.2 %all-to-all-start = ((bf16[64,2,16,256]{3,2,1,0:T(8,128)(2,1)}), bf16[64,2,16,256]{3,2,1,0:T(8,128)(2,1)}, u32[]{:S(2)}, u32[]{:S(2)}) async-start(bf16[64,2,16,256]{3,2,1,0:T(8,128)(2,1)} %get-tuple-element.26), calls=%async_computation | async-start | bytes 2097152 | tf_op jit(solution)/shard_map/all_to_all | solution.py:501
  21.0 1.6 %collective-permute-start.2 = (bf16[384,1024]{1,0:T(8,128)(2,1)}, bf16[384,1024]{1,0:T(8,128)(2,1)}, u32[]{:S(2)}, u32[]{:S(2)}) collective-permute-start(bf16[384,1024]{1,0:T(8,128)(2,1)} %get-tuple-element.30), channel_id=1, source_target_pairs={{0,2},{1,3},{2,0},{3,1},{4,6},{5,7},{6,4},{7,5},{8,10},{9,11},{10,... | collective-permute-start | bytes 2359304 | tf_op jit(solution)/shard_map/ppermute | solution.py:497
  22.6 0.3 collective-permute-done.a.c1
  22.9 1.6 %collective-permute-done.1.b.c3 = bf16[384,1024]{1,0:T(8,128)(2,1)} collective-permute-done((bf16[384,1024]{1,0:T(8,128)(2,1)}, bf16[384,1024]{1,0:T(8,128)(2,1)}, u32[]{:S(2)}, u32[]{:S(2)}) %collective-permute-start.1) | collective-permute-done | bytes 786464 | tf_op jit(solution)/shard_map/ppermute | solution.py:497
  24.5 0.6 hold.1.token
  25.1 23.8 %all-to-all-done.both_hbm.g0_hbm = bf16[64,2,16,256]{3,2,1,0:T(8,128)(2,1)} async-done(((bf16[64,2,16,256]{3,2,1,0:T(8,128)(2,1)}), bf16[64,2,16,256]{3,2,1,0:T(8,128)(2,1)}, u32[]{:S(2)}, u32[]{:S(2)}) %all-to-all-start) | async-done | bytes 1048608 | tf_op jit(solution)/shard_map/all_to_all | solution.py:501
  48.9 1.4 %select.1 = (bf16[64,16,256]{2,1,0:T(8,128)(2,1)S(1)}, bf16[64,16,256]{2,1,0:T(8,128)(2,1)S(1)}) custom-call(s32[1]{0:T(128)} %bitcast.t_ref, bf16[64,2,16,256]{3,2,1,0:T(8,128)(2,1)} %all-to-all-done.both_hbm.g0_hbm), custom_call_target="tpu_custom_call" | custom-call | bytes 2097152 | tf_op jit(solution)/shard_map/select/pallas_call | solution.py:179
  50.3 0.1 collective-permute-start.3
  50.4 2.7 %collective-permute-start.4 = (bf16[64,16,256]{2,1,0:T(8,128)(2,1)S(1)}, bf16[64,16,256]{2,1,0:T(8,128)(2,1)S(1)}, u32[]{:S(2)}, u32[]{:S(2)}) collective-permute-start(bf16[64,16,256]{2,1,0:T(8,128)(2,1)S(1)} %get-tuple-element.35), channel_id=1, source_target_pairs={{0,3},{1,0},{2,1},{3,2},{4,7},{5,4},{6,5},{7,6},{8,11},{9,8},{10,9... | collective-permute-start | bytes 1572872 | tf_op jit(solution)/shard_map/ppermute | solution.py:497
  53.0 0.3 collective-permute-start.5
  53.4 0.0 collective-permute-done.2.c2
  53.4 1.2 copy-done.2
  54.6 1.2 copy-done.3
  55.8 1.1 copy-done.5
  57.0 0.7 copy-done.16
  57.6 3.0 %own_part.1 = (f32[2,1024,256]{2,1,0:T(8,128)S(1)}, f32[2,8,128]{2,1,0:T(8,128)S(1)}, bf16[1024,1024]{1,0:T(8,128)(2,1)S(1)}) custom-call(s32[1]{0:T(128)} %bitcast.t_ref, f32[8,128]{1,0:T(8,128)S(1)} %copy-done.16, bf16[2,256,1024]{2,1,0:T(8,128)(2,1)S(1)} %copy-done.2, bf16[2,256,1024]{2,1,0:T(8,128)(2,1)S(1)} %copy-done.3, ...), custom_call_target="tpu_custom_call" | custom-call | flops 1073741824 | bytes 12582912 | tf_op jit(solution)/shard_map/own_part/pallas_call | solution.py:255
  60.7 3.2 %collective-permute-done.3.g1 = bf16[64,16,256]{2,1,0:T(8,128)(2,1)S(1)} collective-permute-done((bf16[64,16,256]{2,1,0:T(8,128)(2,1)S(1)}, bf16[64,16,256]{2,1,0:T(8,128)(2,1)S(1)}, u32[]{:S(2)}, u32[]{:S(2)}) %collective-permute-start.3) | collective-permute-done | bytes 524320 | tf_op jit(solution)/shard_map/ppermute | solution.py:497
  63.9 0.0 collective-permute-done.4.g3
  63.9 10.8 %collective-permute-done.5.g2 = bf16[64,16,256]{2,1,0:T(8,128)(2,1)S(1)} collective-permute-done((bf16[64,16,256]{2,1,0:T(8,128)(2,1)S(1)}, bf16[64,16,256]{2,1,0:T(8,128)(2,1)S(1)}, u32[]{:S(2)}, u32[]{:S(2)}) %collective-permute-start.5) | collective-permute-done | bytes 524320 | tf_op jit(solution)/shard_map/ppermute | solution.py:497
  74.7 0.0 copy-done.6
  74.7 5.1 %rest_part.1 = (f32[1024,256]{1,0:T(8,128)S(1)}, bf16[1040,128]{1,0:T(8,128)(2,1)S(1)}, bf16[1040,128]{1,0:T(8,128)(2,1)S(1)}, f32[8,128]{1,0:T(8,128)S(1)}) custom-call(s32[1]{0:T(128)} %bitcast.t_ref, f32[2,1024,256]{2,1,0:T(8,128)S(1)} %get-tuple-element.32.own, f32[2,8,128]{2,1,0:T(8,128)S(1)} %get-tuple-element.33.square, ...), custom_call_target="tpu_custom_call" | custom-call | flops 2415919104 | bytes 12582912 | tf_op jit(solution)/shard_map/rest_part/pallas_call | solution.py:320
  79.8 0.6 collective-permute-start.6
  80.5 2.1 %collective-permute-start.7 = (bf16[1040,128]{1,0:T(8,128)(2,1)S(1)}, bf16[1040,128]{1,0:T(8,128)(2,1)S(1)}, u32[]{:S(2)}, u32[]{:S(2)}) collective-permute-start(bf16[1040,128]{1,0:T(8,128)(2,1)S(1)} %get-tuple-element.39), channel_id=1, source_target_pairs={{0,3},{1,0},{2,1},{3,2},{4,7},{5,4},{6,5},{7,6},{8,11},{9,8},{10,9... | collective-permute-start | bytes 798728 | tf_op jit(solution)/shard_map/ppermute | solution.py:497
  82.6 0.0 collective-permute-start.8
  82.6 4.1 %collective-permute-done.8.s2 = f32[8,128]{1,0:T(8,128)S(1)} collective-permute-done((f32[8,128]{1,0:T(8,128)S(1)}, f32[8,128]{1,0:T(8,128)S(1)}, u32[]{:S(2)}, u32[]{:S(2)}) %collective-permute-start.8) | collective-permute-done | bytes 4128 | tf_op jit(solution)/shard_map/ppermute | solution.py:497
  86.7 0.0 collective-permute-done.6.first
  86.7 0.0 collective-permute-done.7.second
  86.7 1.2 scale.1
  87.9 0.0 copy-start.1
  87.9 11.3 %all-to-all-start.1 = ((bf16[64,2,16,256]{3,2,1,0:T(8,128)(2,1)}), bf16[64,2,16,256]{3,2,1,0:T(8,128)(2,1)S(1)}, u32[]{:S(2)}, u32[]{:S(2)}) async-start(bf16[64,2,16,256]{3,2,1,0:T(8,128)(2,1)} %scale.1), calls=%async_computation.1 | async-start | bytes 2097152 | tf_op jit(solution)/shard_map/all_to_all | solution.py:501
  99.2 0.0 copy-start.8
  99.2 1.0 copy-done.8
  100.2 1.0 copy-done.11
  101.3 1.0 copy-done.14
  102.3 2.5 %neighbour_terms.1 = (bf16[256,1024]{1,0:T(8,128)(2,1)S(1)}, bf16[256,1024]{1,0:T(8,128)(2,1)S(1)}) custom-call(s32[1]{0:T(128)} %bitcast.t_ref, bf16[64,2,16,256]{3,2,1,0:T(8,128)(2,1)} %all-to-all-done.both_hbm.g0_hbm, bf16[64,16,256]{2,1,0:T(8,128)(2,1)S(1)} %copy-done.8, bf16[64,16,256]{2,1,0:T(8,128)(2,1)S(1)} %copy-done.11, ...), custom_call_target="tpu_custom_call" | custom-call | flops 1073741824 | bytes 1572864 | tf_op jit(solution)/shard_map/neighbour_terms/pallas_call | solution.py:417
  104.8 0.9 collective-permute-start.9
  105.8 1.8 %collective-permute-start.10 = (bf16[256,1024]{1,0:T(8,128)(2,1)S(1)}, bf16[256,1024]{1,0:T(8,128)(2,1)S(1)}, u32[]{:S(2)}, u32[]{:S(2)}) collective-permute-start(bf16[256,1024]{1,0:T(8,128)(2,1)S(1)} %get-tuple-element.43), channel_id=1, source_target_pairs={{0,3},{1,0},{2,1},{3,2},{4,7},{5,4},{6,5},{7,6},{8,11},{9,8},{10,9... | collective-permute-start | bytes 1572872 | tf_op jit(solution)/shard_map/ppermute | solution.py:497
  107.6 0.0 copy-done.12
  107.6 0.0 copy-done.15
  107.6 3.7 %statistics.1 = (f32[2,256,1024]{2,1,0:T(8,128)}, f32[2,256,1024]{2,1,0:T(8,128)}) custom-call(s32[1]{0:T(128)} %bitcast.t_ref, bf16[64,2,16,256]{3,2,1,0:T(8,128)(2,1)} %all-to-all-done.both_hbm.g0_hbm, bf16[64,16,256]{2,1,0:T(8,128)(2,1)S(1)} %copy-done.9, bf16[64,16,256]{2,1,0:T(8,128)(2,1)S(1)} %copy-done.12, bf16[64,16,256]{2,1,0:T(8,128)(2,1)S(1)} %copy-done.15, ...), custom_call_target="tpu_custom_call" | custom-call | flops 1073741824 | bytes 3145728 | tf_op jit(solution)/shard_map/statistics/pallas_call | solution.py:454
  111.3 7.9 %collective-permute-done.9.left_term = bf16[256,1024]{1,0:T(8,128)(2,1)S(1)} collective-permute-done((bf16[256,1024]{1,0:T(8,128)(2,1)S(1)}, bf16[256,1024]{1,0:T(8,128)(2,1)S(1)}, u32[]{:S(2)}, u32[]{:S(2)}) %collective-permute-start.9) | collective-permute-done | bytes 524320 | tf_op jit(solution)/shard_map/ppermute | solution.py:497
  119.1 0.0 collective-permute-done.10.right_term
  119.2 1.5 %blend.1 = (f32[2,256,1024]{2,1,0:T(8,128)}, f32[2,256,1024]{2,1,0:T(8,128)}) custom-call(s32[1]{0:T(128)} %bitcast.t_ref, bf16[256,1024]{1,0:T(8,128)(2,1)S(1)} %collective-permute-done.9.left_term, bf16[256,1024]{1,0:T(8,128)(2,1)S(1)} %collective-permute-done.10.right_term, ...), custom_call_target="tpu_custom_call", output_to_operand_aliasing={{0}: (5, {}), {1}: (6, {})} | custom-call | flops 1048576 | bytes 4718592 | tf_op jit(solution)/shard_map/blend/pallas_call | solution.py:479
  120.7 6.5 %all-to-all-done.1.slots_hbm = bf16[64,2,16,256]{3,2,1,0:T(8,128)(2,1)S(1)} async-done(((bf16[64,2,16,256]{3,2,1,0:T(8,128)(2,1)}), bf16[64,2,16,256]{3,2,1,0:T(8,128)(2,1)S(1)}, u32[]{:S(2)}, u32[]{:S(2)}) %all-to-all-start.1) | async-done | bytes 1048608 | tf_op jit(solution)/shard_map/all_to_all | solution.py:501
  127.2 1.7 %collect.1 = bf16[64,16,256]{2,1,0:T(8,128)(2,1)} custom-call(s32[64]{0:T(128)S(1)} %copy-done.17, bf16[64,2,16,256]{3,2,1,0:T(8,128)(2,1)S(1)} %all-to-all-done.1.slots_hbm), custom_call_target="tpu_custom_call" | custom-call | bytes 1572864 | tf_op jit(solution)/shard_map/collect/pallas_call | solution.py:143
  (24 shorter events, 0.0 us)
Async XLA Ops:
  4.3 18.6 %collective-permute-start = (bf16[384,1024]{1,0:T(8,128)(2,1)}, bf16[384,1024]{1,0:T(8,128)(2,1)S(1)}, u32[]{:S(2)}, u32[]{:S(2)}) collective-permute-start(bf16[384,1024]{1,0:T(8,128)(2,1)} %get-tuple-element.27), channel_id=1, source_target_pairs={{0,1},{1,2},{2,3},{3,0},{4,5},{5,6},{6,7},{7,4},{8,9},{9,10},{10,1... | collective-permute-start | bytes 2359304 | tf_op jit(solution)/shard_map/ppermute | solution.py:497
  6.4 18.1 %collective-permute-start.1 = (bf16[384,1024]{1,0:T(8,128)(2,1)}, bf16[384,1024]{1,0:T(8,128)(2,1)}, u32[]{:S(2)}, u32[]{:S(2)}) collective-permute-start(bf16[384,1024]{1,0:T(8,128)(2,1)} %get-tuple-element.28), channel_id=1, source_target_pairs={{0,3},{1,0},{2,1},{3,2},{4,7},{5,4},{6,5},{7,6},{8,11},{9,8},{10,9... | collective-permute-start | bytes 2359304 | tf_op jit(solution)/shard_map/ppermute | solution.py:497
  7.8 41.1 %all-to-all-start = ((bf16[64,2,16,256]{3,2,1,0:T(8,128)(2,1)}), bf16[64,2,16,256]{3,2,1,0:T(8,128)(2,1)}, u32[]{:S(2)}, u32[]{:S(2)}) async-start(bf16[64,2,16,256]{3,2,1,0:T(8,128)(2,1)} %get-tuple-element.26), calls=%async_computation | async-start | bytes 2097152 | tf_op jit(solution)/shard_map/all_to_all | solution.py:501
  21.0 32.4 %collective-permute-start.2 = (bf16[384,1024]{1,0:T(8,128)(2,1)}, bf16[384,1024]{1,0:T(8,128)(2,1)}, u32[]{:S(2)}, u32[]{:S(2)}) collective-permute-start(bf16[384,1024]{1,0:T(8,128)(2,1)} %get-tuple-element.30), channel_id=1, source_target_pairs={{0,2},{1,3},{2,0},{3,1},{4,6},{5,7},{6,4},{7,5},{8,10},{9,11},{10,... | collective-permute-start | bytes 2359304 | tf_op jit(solution)/shard_map/ppermute | solution.py:497
  22.9 1.6 %copy-start.4 = (bf16[384,1024]{1,0:T(8,128)(2,1)}, bf16[384,1024]{1,0:T(8,128)(2,1)S(1)}, u32[]{:S(2)}) copy-start(bf16[384,1024]{1,0:T(8,128)(2,1)S(1)} %collective-permute-done.a.c1) | copy-start | bytes 2359300
  50.3 13.6 %collective-permute-start.3 = (bf16[64,16,256]{2,1,0:T(8,128)(2,1)S(1)}, bf16[64,16,256]{2,1,0:T(8,128)(2,1)S(1)}, u32[]{:S(2)}, u32[]{:S(2)}) collective-permute-start(bf16[64,16,256]{2,1,0:T(8,128)(2,1)S(1)} %get-tuple-element.35), channel_id=1, source_target_pairs={{0,1},{1,2},{2,3},{3,0},{4,5},{5,6},{6,7},{7,4},{8,9},{9,10},{10,1... | collective-permute-start | bytes 1572872 | tf_op jit(solution)/shard_map/ppermute | solution.py:497
  50.4 13.5 %collective-permute-start.4 = (bf16[64,16,256]{2,1,0:T(8,128)(2,1)S(1)}, bf16[64,16,256]{2,1,0:T(8,128)(2,1)S(1)}, u32[]{:S(2)}, u32[]{:S(2)}) collective-permute-start(bf16[64,16,256]{2,1,0:T(8,128)(2,1)S(1)} %get-tuple-element.35), channel_id=1, source_target_pairs={{0,3},{1,0},{2,1},{3,2},{4,7},{5,4},{6,5},{7,6},{8,11},{9,8},{10,9... | collective-permute-start | bytes 1572872 | tf_op jit(solution)/shard_map/ppermute | solution.py:497
  53.0 21.6 %collective-permute-start.5 = (bf16[64,16,256]{2,1,0:T(8,128)(2,1)S(1)}, bf16[64,16,256]{2,1,0:T(8,128)(2,1)S(1)}, u32[]{:S(2)}, u32[]{:S(2)}) collective-permute-start(bf16[64,16,256]{2,1,0:T(8,128)(2,1)S(1)} %get-tuple-element.36), channel_id=1, source_target_pairs={{0,2},{1,3},{2,0},{3,1},{4,6},{5,7},{6,4},{7,5},{8,10},{9,11},{10,... | collective-permute-start | bytes 1572872 | tf_op jit(solution)/shard_map/ppermute | solution.py:497
  53.4 1.2 copy-start.2
  54.6 1.2 copy-start.3
  55.8 1.1 copy-start.5
  57.0 0.7 copy-start.16
  57.6 17.0 %copy-start.6 = (bf16[384,1024]{1,0:T(8,128)(2,1)S(1)}, bf16[384,1024]{1,0:T(8,128)(2,1)}, u32[]{:S(2)}) copy-start(bf16[384,1024]{1,0:T(8,128)(2,1)} %copy-done.4) | copy-start | bytes 2359300
  63.9 16.0 %copy-start.7 = (bf16[64,16,256]{2,1,0:T(8,128)(2,1)}, bf16[64,16,256]{2,1,0:T(8,128)(2,1)S(1)}, u32[]{:S(2)}) copy-start(bf16[64,16,256]{2,1,0:T(8,128)(2,1)S(1)} %collective-permute-done.3.g1) | copy-start | bytes 1572868
  63.9 16.0 %copy-start.10 = (bf16[64,16,256]{2,1,0:T(8,128)(2,1)}, bf16[64,16,256]{2,1,0:T(8,128)(2,1)S(1)}, u32[]{:S(2)}) copy-start(bf16[64,16,256]{2,1,0:T(8,128)(2,1)S(1)} %collective-permute-done.4.g3) | copy-start | bytes 1572868
  74.7 5.1 %copy-start.13 = (bf16[64,16,256]{2,1,0:T(8,128)(2,1)}, bf16[64,16,256]{2,1,0:T(8,128)(2,1)S(1)}, u32[]{:S(2)}) copy-start(bf16[64,16,256]{2,1,0:T(8,128)(2,1)S(1)} %collective-permute-done.5.g2) | copy-start | bytes 1572868
  79.8 6.8 %collective-permute-start.6 = (bf16[1040,128]{1,0:T(8,128)(2,1)S(1)}, bf16[1040,128]{1,0:T(8,128)(2,1)S(1)}, u32[]{:S(2)}, u32[]{:S(2)}) collective-permute-start(bf16[1040,128]{1,0:T(8,128)(2,1)S(1)} %get-tuple-element.38), channel_id=1, source_target_pairs={{0,1},{1,2},{2,3},{3,0},{4,5},{5,6},{6,7},{7,4},{8,9},{9,10},{10,1... | collective-permute-start | bytes 798728 | tf_op jit(solution)/shard_map/ppermute | solution.py:497
  80.5 6.2 %collective-permute-start.7 = (bf16[1040,128]{1,0:T(8,128)(2,1)S(1)}, bf16[1040,128]{1,0:T(8,128)(2,1)S(1)}, u32[]{:S(2)}, u32[]{:S(2)}) collective-permute-start(bf16[1040,128]{1,0:T(8,128)(2,1)S(1)} %get-tuple-element.39), channel_id=1, source_target_pairs={{0,3},{1,0},{2,1},{3,2},{4,7},{5,4},{6,5},{7,6},{8,11},{9,8},{10,9... | collective-permute-start | bytes 798728 | tf_op jit(solution)/shard_map/ppermute | solution.py:497
  82.6 4.1 %collective-permute-start.8 = (f32[8,128]{1,0:T(8,128)S(1)}, f32[8,128]{1,0:T(8,128)S(1)}, u32[]{:S(2)}, u32[]{:S(2)}) collective-permute-start(f32[8,128]{1,0:T(8,128)S(1)} %get-tuple-element.40.s0), channel_id=1, source_target_pairs={{0,2},{1,3},{2,0},{3,1},{4,6},{5,7},{6,4},{7,5},{8,10},{9,11},{10,... | collective-permute-start | bytes 12296 | tf_op jit(solution)/shard_map/ppermute | solution.py:497
  87.9 19.7 %copy-start.1 = (f32[2,256,1024]{2,1,0:T(8,128)S(1)}, f32[2,256,1024]{2,1,0:T(8,128)}, u32[]{:S(2)}) copy-start(f32[2,256,1024]{2,1,0:T(8,128)} %right_ref.3) | copy-start | bytes 6291460
  87.9 39.3 %all-to-all-start.1 = ((bf16[64,2,16,256]{3,2,1,0:T(8,128)(2,1)}), bf16[64,2,16,256]{3,2,1,0:T(8,128)(2,1)S(1)}, u32[]{:S(2)}, u32[]{:S(2)}) async-start(bf16[64,2,16,256]{3,2,1,0:T(8,128)(2,1)} %scale.1), calls=%async_computation.1 | async-start | bytes 2097152 | tf_op jit(solution)/shard_map/all_to_all | solution.py:501
  99.2 1.0 copy-start.8
  100.2 1.0 copy-start.11
  101.3 1.0 copy-start.14
  102.3 5.3 %copy-start = (f32[2,256,1024]{2,1,0:T(8,128)S(1)}, f32[2,256,1024]{2,1,0:T(8,128)}, u32[]{:S(2)}) copy-start(f32[2,256,1024]{2,1,0:T(8,128)} %left_ref.3) | copy-start | bytes 6291460
  102.3 5.3 %copy-start.9 = (bf16[64,16,256]{2,1,0:T(8,128)(2,1)S(1)}, bf16[64,16,256]{2,1,0:T(8,128)(2,1)}, u32[]{:S(2)}) copy-start(bf16[64,16,256]{2,1,0:T(8,128)(2,1)} %copy-done.7) | copy-start | bytes 1572868
  102.3 5.3 %copy-start.12 = (bf16[64,16,256]{2,1,0:T(8,128)(2,1)S(1)}, bf16[64,16,256]{2,1,0:T(8,128)(2,1)}, u32[]{:S(2)}) copy-start(bf16[64,16,256]{2,1,0:T(8,128)(2,1)} %copy-done.10) | copy-start | bytes 1572868
  102.3 5.3 %copy-start.15 = (bf16[64,16,256]{2,1,0:T(8,128)(2,1)S(1)}, bf16[64,16,256]{2,1,0:T(8,128)(2,1)}, u32[]{:S(2)}) copy-start(bf16[64,16,256]{2,1,0:T(8,128)(2,1)} %copy-done.13) | copy-start | bytes 1572868
  104.8 14.3 %collective-permute-start.9 = (bf16[256,1024]{1,0:T(8,128)(2,1)S(1)}, bf16[256,1024]{1,0:T(8,128)(2,1)S(1)}, u32[]{:S(2)}, u32[]{:S(2)}) collective-permute-start(bf16[256,1024]{1,0:T(8,128)(2,1)S(1)} %get-tuple-element.42), channel_id=1, source_target_pairs={{0,1},{1,2},{2,3},{3,0},{4,5},{5,6},{6,7},{7,4},{8,9},{9,10},{10,1... | collective-permute-start | bytes 1572872 | tf_op jit(solution)/shard_map/ppermute | solution.py:497
  105.8 13.4 %collective-permute-start.10 = (bf16[256,1024]{1,0:T(8,128)(2,1)S(1)}, bf16[256,1024]{1,0:T(8,128)(2,1)S(1)}, u32[]{:S(2)}, u32[]{:S(2)}) collective-permute-start(bf16[256,1024]{1,0:T(8,128)(2,1)S(1)} %get-tuple-element.43), channel_id=1, source_target_pairs={{0,3},{1,0},{2,1},{3,2},{4,7},{5,4},{6,5},{7,6},{8,11},{9,8},{10,9... | collective-permute-start | bytes 1572872 | tf_op jit(solution)/shard_map/ppermute | solution.py:497
  119.2 8.0 %copy-start.17 = (s32[64]{0:T(128)S(1)}, s32[64]{0:T(128)}, u32[]{:S(2)}) copy-start(s32[64]{0:T(128)} %owner_hbm.3) | copy-start | bytes 772
